TPU v7x, 32 devices: a whole 2x2x4 slice. The times are simulated.
32 devices in a mesh: section: 2 (over core), seq: 4 (over z), fsdp: 4 (over y, x).
Axes of the slice: x: 2, y: 2, z: 4, core: 2. Of those that a mesh axis runs over, the one named last changes fastest.
Arguments:
- tokens: bfloat16 [2, 4, 1024, 1024], P(None, 'fsdp', 'seq'), may hold values from -0.1875 to 0.1875
- cotangent: bfloat16 [2, 4, 1024, 1024], P(None, 'fsdp', 'seq'), may hold values from -6 to 6
- lengths: int32 [2, 4, 4], P(None, 'fsdp'), may hold values from 1 to 896, 1024 in all within a row
- valid_mask: int32 [2, 4, 1024], P(None, 'fsdp', 'seq'), may hold values 0 or 1
- w_qkv: bfloat16 [2, 1024, 3072], P('section', 'fsdp'), may hold values from -0.1875 to 0.1875
- w_out: bfloat16 [2, 1024, 1024], P('section', 'fsdp'), may hold values from -0.1875 to 0.1875
- w_in: bfloat16 [2, 1024, 8192], P('section', 'fsdp'), may hold values from -0.1875 to 0.1875
- w_down: bfloat16 [2, 4096, 1024], P('section', 'fsdp'), may hold values from -0.09375 to 0.09375
- qk_scale: bfloat16 [2, 1024], P('section', 'fsdp'), may hold values from 0.099609375 to 1.8984375
- mlp_scale: bfloat16 [2, 8192], P('section', 'fsdp'), may hold values from 0.099609375 to 1.8984375
- alphas: bfloat16 [2, 2048], P('section', 'fsdp'), may hold values from 0.099609375 to 0.5
Outputs:
- hidden_out: bfloat16 [2, 2, 4, 1024, 1024], P('section', None, 'fsdp', 'seq')
- grad_in: float32 [2, 2, 4, 1024, 1024], P('section', None, 'fsdp', 'seq')
- grad_qkv: float32 [2, 1024, 3072], P('section', 'fsdp')
- grad_out_proj: float32 [2, 1024, 1024], P('section', 'fsdp')
- grad_in_proj: float32 [2, 1024, 8192], P('section', 'fsdp')
- grad_down: float32 [2, 4096, 1024], P('section', 'fsdp')
- grad_qk_scale: float32 [2, 1024], P('section', 'fsdp')
- grad_mlp_scale: float32 [2, 8192], P('section', 'fsdp')
- grad_alphas: float32 [2, 2048], P('section', 'fsdp')
- rms_stats: float32 [2], P('section')
Inputs may be any that keep to these rules, and one draw needn't show every extreme that they name: The 4 lengths of a row add up to 1024; the longest of each row is exactly 896.
All inputs are finite; a program needn't handle non-finite values. No bound on the sum of `valid_mask` on one device may be relied on, other than what follows from the above.
Results may differ from a plain program's by a relative error of at most 0.025.
Values may be sent and summed in bfloat16 or wider, within the bound.
A program may use at most 640 MiB of HBM per device.

v0:
```python
import math

import jax
import jax.numpy as jnp
from jax import lax
from jax.sharding import PartitionSpec as P

HEAD = 64


epsilon = 1e-06


def shifted(block, axis, distance):
    devices = range(lax.axis_size(axis))
    route = [(i - distance, i) for i in devices if i - distance in devices]
    return lax.ppermute(block, axis, route)


def for_sending(x):
    return jax.tree.map(lambda a: a.astype(jnp.bfloat16) if a.dtype == jnp.float32 else a, x)


def unit(values):
    return values * lax.rsqrt(jnp.sum(values * values, axis=-1, keepdims=True) + epsilon)


def unit_back(values, grad):
    factor = lax.rsqrt(jnp.sum(values * values, axis=-1, keepdims=True) + epsilon)
    normed = values * factor
    return factor * (grad - normed * jnp.sum(normed * grad, axis=-1, keepdims=True))


def contract_rows(left, right):
    return lax.dot_general(
        left, right, (((0,), (0,)), ((), ())), preferred_element_type=jnp.float32
    )


def contract_cols(left, right):
    return lax.dot_general(
        left, right, (((1,), (1,)), ((), ())), preferred_element_type=jnp.float32
    )


def segments_of(row_lengths, seq_len):
    ends = jnp.cumsum(row_lengths)[:-1]
    place = jnp.arange(seq_len, dtype=jnp.int32)
    return (place, jnp.sum((place[:, None] >= ends[None, :]).astype(jnp.int32), axis=1))


def allowed_pairs(row_lengths, offset, group, seq_len):
    key_place, key_segment = segments_of(row_lengths, seq_len)
    query_place = offset + jnp.arange(group, dtype=jnp.int32)
    query_segment = lax.dynamic_slice_in_dim(key_segment, offset, group)
    return (query_segment[:, None] == key_segment[None, :]) & (
        key_place[None, :] <= query_place[:, None]
    )


def masked_scores(queries, key_heads, allowed):
    scores = jnp.einsum(
        "qhd,khd->hqk", queries, key_heads, preferred_element_type=jnp.float32
    ) * math.sqrt(HEAD)
    return jnp.where(allowed[None], scores, -1e30)


def forward_layer(hidden_b, params, allowed, valid):
    w_qkv, w_out, w_in, w_down, qk_scale, mlp_scale, alphas = params
    count, width = hidden_b.shape
    heads = width // HEAD
    hidden = hidden_b.astype(jnp.float32)
    mixed = jnp.dot(hidden_b, w_qkv, preferred_element_type=jnp.float32)
    query_raw = mixed[:, :width].reshape(count, heads, HEAD)
    key_raw = mixed[:, width : 2 * width].reshape(count, heads, HEAD)
    head_scale = qk_scale.astype(jnp.float32).reshape(heads, HEAD)
    query_b = (unit(query_raw) * head_scale).astype(jnp.bfloat16)
    key_b = (unit(key_raw) * head_scale).astype(jnp.bfloat16).reshape(count, width)
    value_b = mixed[:, 2 * width :].astype(jnp.bfloat16)
    keys, values = (
        lax.all_gather(key_b, "seq", axis=0, tiled=True),
        lax.all_gather(value_b, "seq", axis=0, tiled=True),
    )
    key_heads = keys.reshape(-1, heads, HEAD)
    value_heads = values.reshape(-1, heads, HEAD)
    scores = masked_scores(query_b, key_heads, allowed)
    highest = jnp.max(scores, axis=-1, keepdims=True)
    weights = jnp.exp(scores - highest)
    denominator = jnp.sum(weights, axis=-1, keepdims=True)
    weights = weights / denominator
    log_total = highest + jnp.log(denominator)
    attended = jnp.einsum(
        "hqk,khd->qhd",
        weights.astype(jnp.bfloat16),
        value_heads,
        preferred_element_type=jnp.float32,
    )
    attended_b = attended.reshape(count, width).astype(jnp.bfloat16)
    branch = jnp.dot(attended_b, w_out, preferred_element_type=jnp.float32)
    statistic = jnp.sum(valid * jnp.sum(branch * branch, axis=-1))
    step_sizes = alphas.astype(jnp.float32)
    first_sum = hidden + step_sizes[:width] * (unit(branch) - hidden)
    middle = unit(first_sum)
    middle_b = middle.astype(jnp.bfloat16)
    lifted = jnp.dot(middle_b, w_in, preferred_element_type=jnp.float32)
    units_count = lifted.shape[1] // 2
    scales = mlp_scale.astype(jnp.float32)
    upward = lifted[:, :units_count] * scales[:units_count]
    gating = lifted[:, units_count:] * scales[units_count:] * math.sqrt(width)
    inner_b = (upward * jax.nn.silu(gating)).astype(jnp.bfloat16)
    output = jnp.dot(inner_b, w_down, preferred_element_type=jnp.float32)
    second_sum = middle + step_sizes[width:] * (unit(output) - middle)
    result = unit(second_sum).astype(jnp.bfloat16)
    kept = (
        hidden_b,
        query_raw,
        key_raw,
        query_b,
        keys,
        values,
        log_total,
        attended_b,
        branch,
        first_sum,
        middle_b,
        lifted,
        inner_b,
        output,
        second_sum,
    )
    return (result, kept, statistic)


def backward_layer(kept, params, grad_out, allowed):
    (
        hidden_b,
        query_raw,
        key_raw,
        query_b,
        keys,
        values,
        log_total,
        attended_b,
        branch,
        first_sum,
        middle_b,
        lifted,
        inner_b,
        output,
        second_sum,
    ) = kept
    w_qkv, w_out, w_in, w_down, qk_scale, mlp_scale, alphas = params
    count, width = hidden_b.shape
    heads = width // HEAD
    hidden = hidden_b.astype(jnp.float32)
    step_sizes = alphas.astype(jnp.float32)
    alpha_attn = step_sizes[:width]
    alpha_mlp = step_sizes[width:]
    middle = unit(first_sum)
    grad_second = unit_back(second_sum, grad_out)
    grad_alpha_mlp = jnp.sum(grad_second * (unit(output) - middle), axis=0)
    grad_output = unit_back(output, alpha_mlp * grad_second).astype(jnp.bfloat16)
    grad_middle = grad_second * (1.0 - alpha_mlp)
    grad_down = contract_rows(inner_b, grad_output)
    grad_inner = contract_cols(grad_output, w_down)
    units_count = lifted.shape[1] // 2
    scales = mlp_scale.astype(jnp.float32)
    root = math.sqrt(width)
    lift_up = lifted[:, :units_count]
    lift_gate = lifted[:, units_count:]
    upward = lift_up * scales[:units_count]
    gating = lift_gate * scales[units_count:] * root
    sigmoid = jax.nn.sigmoid(gating)
    grad_upward = grad_inner * jax.nn.silu(gating)
    grad_gating = grad_inner * upward * sigmoid * (1.0 + gating * (1.0 - sigmoid))
    grad_scale_mlp = jnp.concatenate(
        [jnp.sum(grad_upward * lift_up, axis=0), jnp.sum(grad_gating * root * lift_gate, axis=0)]
    )
    grad_lifted = jnp.concatenate(
        [grad_upward * scales[:units_count], grad_gating * root * scales[units_count:]], axis=1
    ).astype(jnp.bfloat16)
    grad_in_proj = contract_rows(middle_b, grad_lifted)
    grad_middle = grad_middle + contract_cols(grad_lifted, w_in)
    grad_first = unit_back(first_sum, grad_middle)
    grad_alpha_attn = jnp.sum(grad_first * (unit(branch) - hidden), axis=0)
    grad_branch = unit_back(branch, alpha_attn * grad_first).astype(jnp.bfloat16)
    grad_hidden = grad_first * (1.0 - alpha_attn)
    grad_out_proj = contract_rows(attended_b, grad_branch)
    grad_attended = (
        contract_cols(grad_branch, w_out).astype(jnp.bfloat16).reshape(count, heads, HEAD)
    )
    key_heads = keys.reshape(-1, heads, HEAD)
    value_heads = values.reshape(-1, heads, HEAD)
    scores = masked_scores(query_b, key_heads, allowed)
    weights = jnp.exp(scores - log_total)
    grad_weights = jnp.einsum(
        "qhd,khd->hqk", grad_attended, value_heads, preferred_element_type=jnp.float32
    )
    delta = jnp.sum(weights * grad_weights, axis=-1, keepdims=True)
    grad_scores = (weights * (grad_weights - delta)).astype(jnp.bfloat16)
    score_scale = math.sqrt(HEAD)
    grad_query = (
        jnp.einsum("hqk,khd->qhd", grad_scores, key_heads, preferred_element_type=jnp.float32)
        * score_scale
    )
    seq_len = keys.shape[0]
    grad_keys = (
        jnp.einsum("hqk,qhd->khd", grad_scores, query_b, preferred_element_type=jnp.float32)
        * score_scale
    )
    grad_values = jnp.einsum(
        "hqk,qhd->khd",
        weights.astype(jnp.bfloat16),
        grad_attended,
        preferred_element_type=jnp.float32,
    )
    grad_key_own, grad_value_own = (
        lax.psum_scatter(
            grad_keys.reshape(seq_len, width).astype(jnp.bfloat16),
            "seq",
            scatter_dimension=0,
            tiled=True,
        ).astype(jnp.float32),
        lax.psum_scatter(
            grad_values.reshape(seq_len, width).astype(jnp.bfloat16),
            "seq",
            scatter_dimension=0,
            tiled=True,
        ).astype(jnp.float32),
    )
    head_scale = qk_scale.astype(jnp.float32).reshape(heads, HEAD)
    grad_key_heads = grad_key_own.reshape(count, heads, HEAD)
    grad_scale_qk = (
        jnp.sum(grad_query * unit(query_raw), axis=0)
        + jnp.sum(grad_key_heads * unit(key_raw), axis=0)
    ).reshape(width)
    grad_query_raw = unit_back(query_raw, grad_query * head_scale).reshape(count, width)
    grad_key_raw = unit_back(key_raw, grad_key_heads * head_scale).reshape(count, width)
    grad_mixed = jnp.concatenate([grad_query_raw, grad_key_raw, grad_value_own], axis=1).astype(
        jnp.bfloat16
    )
    grad_qkv = contract_rows(hidden_b, grad_mixed)
    grad_hidden = grad_hidden + contract_cols(grad_mixed, w_qkv)
    grad_step_sizes = jnp.concatenate([grad_alpha_attn, grad_alpha_mlp])
    grads = (
        grad_qkv,
        grad_out_proj,
        grad_in_proj,
        grad_down,
        grad_scale_qk,
        grad_scale_mlp,
        grad_step_sizes,
    )
    return (grad_hidden, grads)


def per_device(
    tokens, cotangent, lengths, valid_mask, w_qkv, w_out, w_in, w_down, qk_scale, mlp_scale, alphas
):
    shards = (w_qkv, w_out, w_in, w_down, qk_scale, mlp_scale, alphas)
    gathered = (
        lax.all_gather(shards[0], "fsdp", axis=1, tiled=True),
        lax.all_gather(shards[1], "fsdp", axis=1, tiled=True),
        lax.all_gather(shards[2], "fsdp", axis=1, tiled=True),
        lax.all_gather(shards[3], "fsdp", axis=1, tiled=True),
        lax.all_gather(shards[4], "fsdp", axis=1, tiled=True),
        lax.all_gather(shards[5], "fsdp", axis=1, tiled=True),
        lax.all_gather(shards[6], "fsdp", axis=1, tiled=True),
    )
    params = tuple((piece[0] for piece in gathered))
    section = lax.axis_index("section")
    micro = tokens.shape[0]
    group = tokens.shape[2]
    width = tokens.shape[3]
    seq_len = group * lax.axis_size("seq")
    offset = lax.axis_index("seq") * group

    def fetch(array, index):
        return lax.dynamic_index_in_dim(array, index, 0, keepdims=False)[0]

    def forward_step(carry, step):
        incoming, stat_sum = carry
        index = step - section
        active = (index >= 0) & (index < micro)
        chosen = jnp.clip(index, 0, micro - 1)
        hidden_in = jnp.where(section == 0, fetch(tokens, chosen), incoming)
        allowed = allowed_pairs(fetch(lengths, chosen), offset, group, seq_len)
        valid = fetch(valid_mask, chosen).astype(jnp.float32)
        result, kept, statistic = forward_layer(hidden_in, params, allowed, valid)
        outgoing = shifted(result, "section", 1)
        stat_sum = stat_sum + jnp.where(active, statistic, 0.0)
        return ((outgoing, stat_sum), (result, kept))

    step_list = jnp.arange(micro + 1, dtype=jnp.int32)
    start = (jnp.zeros((group, width), jnp.bfloat16), jnp.zeros((), jnp.float32))
    (unused_fwd, stat_sum), (results, kept_all) = lax.scan(forward_step, start, step_list)
    late_shards, stat_sum = lax.optimization_barrier((shards, stat_sum))
    again = (
        lax.all_gather(late_shards[0], "fsdp", axis=1, tiled=True),
        lax.all_gather(late_shards[1], "fsdp", axis=1, tiled=True),
        lax.all_gather(late_shards[2], "fsdp", axis=1, tiled=True),
        lax.all_gather(late_shards[3], "fsdp", axis=1, tiled=True),
        lax.all_gather(late_shards[4], "fsdp", axis=1, tiled=True),
        lax.all_gather(late_shards[5], "fsdp", axis=1, tiled=True),
        lax.all_gather(late_shards[6], "fsdp", axis=1, tiled=True),
    )
    params_back = tuple((piece[0] for piece in again))

    def backward_step(carry, step):
        incoming, sums = carry
        index = step - 1 + section
        active = (index >= 0) & (index < micro)
        chosen = jnp.clip(index, 0, micro - 1)
        position = chosen + section

        def take(array):
            return lax.dynamic_index_in_dim(array, position, 0, keepdims=False)

        kept = jax.tree.map(take, kept_all)
        grad_out = jnp.where(
            section == 1, fetch(cotangent, chosen).astype(jnp.float32), incoming.astype(jnp.float32)
        )
        grad_out = jnp.where(active, grad_out, 0.0)
        row_lengths = fetch(lengths, chosen)
        allowed = allowed_pairs(row_lengths, offset, group, seq_len)
        grad_hidden, grads = backward_layer(kept, params_back, grad_out, allowed)
        outgoing = shifted(grad_hidden.astype(jnp.bfloat16), "section", -1)
        sums = tuple((total + piece for total, piece in zip(sums, grads)))
        return ((outgoing, sums), grad_hidden)

    zeros = tuple((jnp.zeros(piece.shape, jnp.float32) for piece in params_back))
    (unused_back, sums), grad_steps = lax.scan(
        backward_step, (jnp.zeros((group, width), jnp.bfloat16), zeros), step_list
    )
    hidden_out = lax.dynamic_slice_in_dim(results, section, micro, 0).reshape(
        1, micro, 1, group, width
    )
    grad_in = lax.dynamic_slice_in_dim(grad_steps, 1 - section, micro, 0).reshape(
        1, micro, 1, group, width
    )
    shard_sums = jax.tree.map(
        lambda part: part.astype(jnp.float32),
        lax.psum_scatter(for_sending(sums), "fsdp", scatter_dimension=0, tiled=True),
    )
    reduced = jax.tree.map(
        lambda part: part.astype(jnp.float32), lax.psum(for_sending(shard_sums), "seq")
    )
    total_stat = lax.psum(stat_sum, ("seq", "fsdp"))
    token_count = micro * lax.axis_size("fsdp") * seq_len
    rms_stats = jnp.sqrt(total_stat / token_count + epsilon).reshape(1)
    return (
        hidden_out,
        grad_in,
        reduced[0][None],
        reduced[1][None],
        reduced[2][None],
        reduced[3][None],
        reduced[4][None],
        reduced[5][None],
        reduced[6][None],
        rms_stats,
    )


def solution(mesh):
    placed = (
        P(None, "fsdp", "seq", None),
        P(None, "fsdp", "seq", None),
        P(None, "fsdp", None),
        P(None, "fsdp", "seq"),
        P("section", "fsdp", None),
        P("section", "fsdp", None),
        P("section", "fsdp", None),
        P("section", "fsdp", None),
        P("section", "fsdp"),
        P("section", "fsdp"),
        P("section", "fsdp"),
    )
    return jax.shard_map(
        per_device,
        mesh=mesh,
        in_specs=placed,
        out_specs=(
            P("section", None, "fsdp", "seq", None),
            P("section", None, "fsdp", "seq", None),
            P("section", "fsdp", None),
            P("section", "fsdp", None),
            P("section", "fsdp", None),
            P("section", "fsdp", None),
            P("section", "fsdp"),
            P("section", "fsdp"),
            P("section", "fsdp"),
            P("section"),
        ),
        check_vma=False,
    )
```

profile of v0, /device:TPU:0, one launch (start us, length us, event | category | flops | bytes accessed | tf_op | source)
XLA Modules:
  0.0 2527.6 jit_solution(10854135195059459904)
XLA Ops:
  35.1 12.9 all-gather.13.cloned.1.call-done
  48.0 72.0 %all-gather.11.cloned.1.call-done = bf16[1,1024,3072]{2,1,0:T(8,128)(2,1)} async-done(((bf16[1,256,3072]{2,1,0:T(8,128)(2,1)}), bf16[1,1024,3072]{2,1,0:T(8,128)(2,1)}) %all-gather.11.cloned.1.call-update) | async-done | bytes 6291472 | tf_op jit(solution)/shard_map/all_gather | solution.py:262
  120.0 89.5 %all-gather.17.cloned.1.call-done = bf16[1,4096,1024]{2,1,0:T(8,128)(2,1)} async-done(((bf16[1,1024,1024]{2,1,0:T(8,128)(2,1)}), bf16[1,4096,1024]{2,1,0:T(8,128)(2,1)}) %all-gather.17.cloned.1.call-update) | async-done | bytes 8388624 | tf_op jit(solution)/shard_map/all_gather | solution.py:265
  209.5 159.1 %all-gather.15.cloned.1.call-done = bf16[1,1024,8192]{2,1,0:T(8,128)(2,1)} async-done(((bf16[1,256,8192]{2,1,0:T(8,128)(2,1)}), bf16[1,1024,8192]{2,1,0:T(8,128)(2,1)}) %all-gather.15.cloned.1.call-update) | async-done | bytes 16777232 | tf_op jit(solution)/shard_map/all_gather | solution.py:264
  377.7 475.4 %while.75 = (s32[]{:T(128)}, bf16[256,1024]{1,0:T(8,128)(2,1)}, f32[]{:T(128)}, bf16[3,256,1024]{2,1,0:T(8,128)(2,1)}, bf16[3,256,1024]{2,1,0:T(8,128)(2,1)}, /*...) while((s32[]{:T(128)}, bf16[256,1024]{1,0:T(8,128)(2,1)}, ...), condition=%wide.region_12.13_spmd, body=%wide.region_0.12_spmd.sunk | while | flops 9734461440 | bytes 310316352 | solution.py:296
  403.7 39.8 %all-gather.29.cloned.1.call-done = bf16[1024,1024]{1,0:T(8,128)(2,1)} async-done(((bf16[256,1024]{1,0:T(8,128)(2,1)}), bf16[1024,1024]{1,0:T(8,128)(2,1)}) %all-gather.29.cloned.1.call-update) | async-done | bytes 2097168 | tf_op jit(solution)/shard_map/while/body/eval_jaxpr/all_gather | solution.py:81
  460.1 30.1 %all-gather.27.cloned.1.call-done = bf16[1024,1024]{1,0:T(8,128)(2,1)} async-done(((bf16[256,1024]{1,0:T(8,128)(2,1)}), bf16[1024,1024]{1,0:T(8,128)(2,1)}) %all-gather.27.cloned.1.call-update) | async-done | bytes 2097168 | tf_op jit(solution)/shard_map/while/body/eval_jaxpr/all_gather | solution.py:82
  562.9 38.7 %all-gather.29.cloned.1.call-done = bf16[1024,1024]{1,0:T(8,128)(2,1)} async-done(((bf16[256,1024]{1,0:T(8,128)(2,1)}), bf16[1024,1024]{1,0:T(8,128)(2,1)}) %all-gather.29.cloned.1.call-update) | async-done | bytes 2097168 | tf_op jit(solution)/shard_map/while/body/eval_jaxpr/all_gather | solution.py:81
  618.2 30.2 %all-gather.27.cloned.1.call-done = bf16[1024,1024]{1,0:T(8,128)(2,1)} async-done(((bf16[256,1024]{1,0:T(8,128)(2,1)}), bf16[1024,1024]{1,0:T(8,128)(2,1)}) %all-gather.27.cloned.1.call-update) | async-done | bytes 2097168 | tf_op jit(solution)/shard_map/while/body/eval_jaxpr/all_gather | solution.py:82
  721.1 38.7 %all-gather.29.cloned.1.call-done = bf16[1024,1024]{1,0:T(8,128)(2,1)} async-done(((bf16[256,1024]{1,0:T(8,128)(2,1)}), bf16[1024,1024]{1,0:T(8,128)(2,1)}) %all-gather.29.cloned.1.call-update) | async-done | bytes 2097168 | tf_op jit(solution)/shard_map/while/body/eval_jaxpr/all_gather | solution.py:81
  776.4 30.1 %all-gather.27.cloned.1.call-done = bf16[1024,1024]{1,0:T(8,128)(2,1)} async-done(((bf16[256,1024]{1,0:T(8,128)(2,1)}), bf16[1024,1024]{1,0:T(8,128)(2,1)}) %all-gather.27.cloned.1.call-update) | async-done | bytes 2097168 | tf_op jit(solution)/shard_map/while/body/eval_jaxpr/all_gather | solution.py:82
  890.3 71.9 %all-gather.25.cloned.1.call-done = bf16[1,1024,3072]{2,1,0:T(8,128)(2,1)} async-done(((bf16[1,256,3072]{2,1,0:T(8,128)(2,1)}), bf16[1,1024,3072]{2,1,0:T(8,128)(2,1)}) %all-gather.25.cloned.1.call-update) | async-done | bytes 6291472 | tf_op jit(solution)/shard_map/all_gather | solution.py:299
  962.2 89.5 %all-gather.19.cloned.1.call-done = bf16[1,4096,1024]{2,1,0:T(8,128)(2,1)} async-done(((bf16[1,1024,1024]{2,1,0:T(8,128)(2,1)}), bf16[1,4096,1024]{2,1,0:T(8,128)(2,1)}) %all-gather.19.cloned.1.call-update) | async-done | bytes 8388624 | tf_op jit(solution)/shard_map/all_gather | solution.py:302
  1051.7 159.1 %all-gather.21.cloned.1.call-done = bf16[1,1024,8192]{2,1,0:T(8,128)(2,1)} async-done(((bf16[1,256,8192]{2,1,0:T(8,128)(2,1)}), bf16[1,1024,8192]{2,1,0:T(8,128)(2,1)}) %all-gather.21.cloned.1.call-update) | async-done | bytes 16777232 | tf_op jit(solution)/shard_map/all_gather | solution.py:301
  1213.7 637.2 %while.76 = (s32[]{:T(128)}, bf16[256,1024]{1,0:T(8,128)(2,1)}, f32[1024,3072]{1,0:T(8,128)}, f32[1024,1024]{1,0:T(8,128)}, f32[1024,8192]{1,0:T(8,128)}, /*inde...) while((s32[]{:T(128)}, bf16[256,1024]{1,0:T(8,128)(2,1)}, ...), condition=%wide.region_37.38_spmd.clone, body=%wide.region_13.37_spmd.clone.sunk | while | flops 20014483456 | bytes 582250816 | solution.py:332
  1367.2 14.0 select_add_fusion.12
  1384.6 36.7 %reduce-scatter.15.cloned.1.call-done = bf16[256,1024]{0,1:T(8,128)(2,1)} async-done(((bf16[1024,1024]{0,1:T(8,128)(2,1)}), bf16[256,1024]{0,1:T(8,128)(2,1)}) %reduce-scatter.15.cloned.1.call-update) | async-done | bytes 524304 | tf_op jit(solution)/shard_map/while/body/eval_jaxpr/reduce_scatter | solution.py:224
  1559.9 14.7 select_add_fusion.13
  1574.6 25.5 %select_add_fusion.12 = f32[1024,8192]{1,0:T(8,128)} fusion(f32[1024,8192]{1,0:T(8,128)} %get-tuple-element.2275, pred[]{:T(512)S(6)} %compare.3, bf16[256,4096]{1,0:T(8,128)(2,1)S(1)} %copy-done.3, bf16[256,4096]{1,0:T(8,128)(2,1)} %get-tuple-element.2089, bf16[3,256,1024]{2,1,0:T(8,128)(2,1)} %get-tuple-element.2352, s32[]{:T(128)S(6)} %select_n.171), kind=kOutput, calls=%fused_computation.71.clone.1 | convolution fusion | flops 4320133120 | bytes 71827464 | tf_op jit(solution)/shard_map/while/body/eval_jaxpr/dot_general | solution.py:35
  1603.4 19.3 reduce-scatter.15.cloned.1.call-done
  1709.5 12.9 multiply_reduce_fusion.40
  1764.9 14.7 select_add_fusion.13
  1779.7 25.5 %select_add_fusion.12 = f32[1024,8192]{1,0:T(8,128)} fusion(f32[1024,8192]{1,0:T(8,128)} %get-tuple-element.2275, pred[]{:T(512)S(6)} %compare.3, bf16[256,4096]{1,0:T(8,128)(2,1)S(1)} %copy-done.3, bf16[256,4096]{1,0:T(8,128)(2,1)} %get-tuple-element.2089, bf16[3,256,1024]{2,1,0:T(8,128)(2,1)} %get-tuple-element.2352, s32[]{:T(128)S(6)} %select_n.171), kind=kOutput, calls=%fused_computation.71.clone.1 | convolution fusion | flops 4320133120 | bytes 71827464 | tf_op jit(solution)/shard_map/while/body/eval_jaxpr/dot_general | solution.py:35
  1808.4 19.3 reduce-scatter.15.cloned.1.call-done
  1872.5 17.6 convert_element_type.292
  1890.7 73.5 %reduce-scatter.7.cloned.1.call-done = bf16[256,3072]{1,0:T(8,128)(2,1)} async-done(((bf16[1024,3072]{1,0:T(8,128)(2,1)}), bf16[256,3072]{1,0:T(8,128)(2,1)}) %reduce-scatter.7.cloned.1.call-update) | async-done | bytes 1572880 | tf_op jit(solution)/shard_map/reduce_scatter | solution.py:343
  1964.2 90.4 %reduce-scatter.13.cloned.1.call-done = bf16[1024,1024]{1,0:T(8,128)(2,1)} async-done(((bf16[4096,1024]{1,0:T(8,128)(2,1)}), bf16[1024,1024]{1,0:T(8,128)(2,1)}) %reduce-scatter.13.cloned.1.call-update) | async-done | bytes 2097168 | tf_op jit(solution)/shard_map/reduce_scatter | solution.py:343
  2054.6 156.8 %reduce-scatter.11.cloned.1.call-done = bf16[256,8192]{1,0:T(8,128)(2,1)} async-done(((bf16[1024,8192]{1,0:T(8,128)(2,1)}), bf16[256,8192]{1,0:T(8,128)(2,1)}) %reduce-scatter.11.cloned.1.call-update) | async-done | bytes 4194320 | tf_op jit(solution)/shard_map/reduce_scatter | solution.py:343
  2214.5 43.5 %psum.63 = f32[]{:T(128)} all-reduce(f32[]{:T(128)} %get-tuple-element.906), channel_id=1, replica_groups=mesh['section'=2,'seq'=4,'fsdp'=4] {'seq','fsdp'}, use_global_device_ids=true, to_apply=%region_52.53 | all-reduce | flops 1 | bytes 8 | tf_op jit(solution)/shard_map/psum | solution.py:348
  2261.0 14.0 all-reduce.3
  2275.2 16.8 all-reduce.4
  2295.2 212.9 %all-reduce.8.cloned.1.call-done = (bf16[1,256,3072]{2,1,0:T(8,128)(2,1)}, bf16[1,256,1024]{2,1,0:T(8,128)(2,1)}, bf16[1,256,8192]{2,1,0:T(8,128)(2,1)}, bf16[1,1024,1024]{2,1,0:T(8,128)(2,1)}) async-done(((bf16[1,256,3072]{2,1,0:T(8,128)(2,1)}, bf16[1,256,1024]{2,1,0:T(8,128)(2,1)}, bf16[1,256,8192]{2,1,0:T(8,128)(2,1)}, bf16[1,1024,1024]{2,1,0:T(8,128)(2,1)}), (bf16[1,256,3072]{2,1,0:T(8,128)(2,1)}, ...) | async-done | bytes 8388624 | tf_op jit(solution)/shard_map/psum | solution.py:346
  (637 shorter events, 806.0 us)
Async XLA Ops:
  7.2 40.8 %all-gather.13.cloned.1.call-start = ((), (), s32[]{:S(2)}) async-start(), calls=%async_computation.7 | async-start | bytes 2621440 | tf_op jit(solution)/shard_map/all_gather | solution.py:263
  7.9 112.1 %all-gather.11.cloned.1.call-start = ((), (), s32[]{:S(2)}) async-start(), calls=%async_computation.6 | async-start | bytes 7864320 | tf_op jit(solution)/shard_map/all_gather | solution.py:262
  8.7 200.8 %all-gather.17.cloned.1.call-start = ((), (), s32[]{:S(2)}) async-start(), calls=%async_computation.9 | async-start | bytes 10485760 | tf_op jit(solution)/shard_map/all_gather | solution.py:265
  9.4 359.2 %all-gather.15.cloned.1.call-start = ((), (), s32[]{:S(2)}) async-start(), calls=%async_computation.8 | async-start | bytes 20971520 | tf_op jit(solution)/shard_map/all_gather | solution.py:264
  377.7 65.8 %all-gather.29.cloned.1.call-start = ((), (), s32[]{:S(2)}) async-start(), calls=%async_computation.20 | async-start | bytes 2621440 | tf_op jit(solution)/shard_map/while/body/eval_jaxpr/all_gather | solution.py:81
  397.4 92.8 %all-gather.27.cloned.1.call-start = ((), (), s32[]{:S(2)}) async-start(), calls=%async_computation.19 | async-start | bytes 2621440 | tf_op jit(solution)/shard_map/while/body/eval_jaxpr/all_gather | solution.py:82
  528.2 8.6 collective-permute-start
  536.9 64.7 %all-gather.29.cloned.1.call-start = ((), (), s32[]{:S(2)}) async-start(), calls=%async_computation.20 | async-start | bytes 2621440 | tf_op jit(solution)/shard_map/while/body/eval_jaxpr/all_gather | solution.py:81
  556.5 91.9 %all-gather.27.cloned.1.call-start = ((), (), s32[]{:S(2)}) async-start(), calls=%async_computation.19 | async-start | bytes 2621440 | tf_op jit(solution)/shard_map/while/body/eval_jaxpr/all_gather | solution.py:82
  686.5 8.6 collective-permute-start
  695.1 64.7 %all-gather.29.cloned.1.call-start = ((), (), s32[]{:S(2)}) async-start(), calls=%async_computation.20 | async-start | bytes 2621440 | tf_op jit(solution)/shard_map/while/body/eval_jaxpr/all_gather | solution.py:81
  714.7 91.7 %all-gather.27.cloned.1.call-start = ((), (), s32[]{:S(2)}) async-start(), calls=%async_computation.19 | async-start | bytes 2621440 | tf_op jit(solution)/shard_map/while/body/eval_jaxpr/all_gather | solution.py:82
  844.6 8.6 collective-permute-start
  853.2 37.1 %all-gather.23.cloned.1.call-start = ((), (), s32[]{:S(2)}) async-start(), calls=%async_computation.12 | async-start | bytes 2621440 | tf_op jit(solution)/shard_map/all_gather | solution.py:300
  853.9 108.3 %all-gather.25.cloned.1.call-start = ((), (), s32[]{:S(2)}) async-start(), calls=%async_computation.13 | async-start | bytes 7864320 | tf_op jit(solution)/shard_map/all_gather | solution.py:299
  854.5 197.2 %all-gather.19.cloned.1.call-start = ((), (), s32[]{:S(2)}) async-start(), calls=%async_computation.10 | async-start | bytes 10485760 | tf_op jit(solution)/shard_map/all_gather | solution.py:302
  855.2 358.5 %copy-start.7 = (f32[3,256,1024]{2,1,0:T(8,128)S(1)}, f32[3,256,1024]{2,1,0:T(8,128)}, u32[]{:S(2)}) copy-start(f32[3,256,1024]{2,1,0:T(8,128)} %get-tuple-element.2244) | copy-start | bytes 9437188
  855.2 355.6 %all-gather.21.cloned.1.call-start = ((), (), s32[]{:S(2)}) async-start(), calls=%async_computation.11 | async-start | bytes 20971520 | tf_op jit(solution)/shard_map/all_gather | solution.py:301
  1235.9 145.3 %reduce-scatter.17.cloned.1.call-start = ((), (), s32[]{:S(2)}) async-start(), calls=%async_computation.22 | async-start | bytes 2621440 | tf_op jit(solution)/shard_map/while/body/eval_jaxpr/reduce_scatter | solution.py:218
  1331.9 89.4 %reduce-scatter.15.cloned.1.call-start = ((), (), s32[]{:S(2)}) async-start(), calls=%async_computation.21 | async-start | bytes 2621440 | tf_op jit(solution)/shard_map/while/body/eval_jaxpr/reduce_scatter | solution.py:224
  1426.2 10.2 collective-permute-start.1
  1437.1 163.0 %reduce-scatter.17.cloned.1.call-start = ((), (), s32[]{:S(2)}) async-start(), calls=%async_computation.22 | async-start | bytes 2621440 | tf_op jit(solution)/shard_map/while/body/eval_jaxpr/reduce_scatter | solution.py:218
  1533.1 89.6 %reduce-scatter.15.cloned.1.call-start = ((), (), s32[]{:S(2)}) async-start(), calls=%async_computation.21 | async-start | bytes 2621440 | tf_op jit(solution)/shard_map/while/body/eval_jaxpr/reduce_scatter | solution.py:224
  1627.6 13.8 collective-permute-start.1
  1642.2 163.0 %reduce-scatter.17.cloned.1.call-start = ((), (), s32[]{:S(2)}) async-start(), calls=%async_computation.22 | async-start | bytes 2621440 | tf_op jit(solution)/shard_map/while/body/eval_jaxpr/reduce_scatter | solution.py:218
  1738.1 89.6 %reduce-scatter.15.cloned.1.call-start = ((), (), s32[]{:S(2)}) async-start(), calls=%async_computation.21 | async-start | bytes 2621440 | tf_op jit(solution)/shard_map/while/body/eval_jaxpr/reduce_scatter | solution.py:224
  1832.7 13.8 collective-permute-start.1
  1850.9 39.8 %reduce-scatter.9.cloned.1.call-start = ((), (), s32[]{:S(2)}) async-start(), calls=%async_computation.15 | async-start | bytes 2621440 | tf_op jit(solution)/shard_map/reduce_scatter | solution.py:343
  1854.8 109.4 %reduce-scatter.7.cloned.1.call-start = ((), (), s32[]{:S(2)}) async-start(), calls=%async_computation.14 | async-start | bytes 7864320 | tf_op jit(solution)/shard_map/reduce_scatter | solution.py:343
  1863.0 191.5 %reduce-scatter.13.cloned.1.call-start = ((), (), s32[]{:S(2)}) async-start(), calls=%async_computation.17 | async-start | bytes 10485760 | tf_op jit(solution)/shard_map/reduce_scatter | solution.py:343
  1872.5 338.9 %reduce-scatter.11.cloned.1.call-start = ((), (), s32[]{:S(2)}) async-start(), calls=%async_computation.16 | async-start | bytes 20971520 | tf_op jit(solution)/shard_map/reduce_scatter | solution.py:343
  1890.1 618.1 %all-reduce.8.cloned.1.call-start = ((), (), s32[]{:S(2)}) async-start(), calls=%async_computation.18 | async-start | bytes 16777216 | tf_op jit(solution)/shard_map/psum | solution.py:346
  (88 other events, 816.4 us)
Sparse Core Ops, SparseCore 0:
  9.9 38.0 all-gather.12
  49.8 70.1 all-gather.10
  121.9 87.5 all-gather.16
  211.2 157.4 all-gather.14
  397.5 45.9 all-gather.28
  445.5 44.6 all-gather.26
  556.7 44.8 all-gather.28
  603.7 44.6 all-gather.26
  714.9 44.8 all-gather.28
  761.8 44.6 all-gather.26
  855.8 34.4 all-gather.22
  892.0 70.1 all-gather.24
  964.0 87.5 all-gather.18
  1053.4 157.4 all-gather.20
  1332.0 43.8 reduce-scatter.16
  1378.1 43.1 reduce-scatter.14
  1533.2 44.0 reduce-scatter.16
  1579.5 43.1 reduce-scatter.14
  1738.2 43.9 reduce-scatter.16
  1784.4 43.2 reduce-scatter.14
  1855.3 35.3 reduce-scatter.8
  1893.9 70.2 reduce-scatter.6
  1968.1 86.3 reduce-scatter.12
  2057.5 153.8 reduce-scatter.10
  2214.2 293.8 all-reduce.7
where the time goes:
time: 2550 us; the launch traced here: 2530 us
  waiting for transfers between devices  1490 us (58%)
  matrix products  465 us (18%)
  other arithmetic  222 us (9%)
  local copies, waits for them, and re-layouts  167 us (7%)
  blocking collectives  123 us (5%)
  loops' own time  33.6 us (1%)
    reduce_scatter x4, waiting for transfers between devices, per_device(): lax.psum_scatter(for_sending(sums), 'fsdp', scatter_dimension=0, tiled=True)  321 us
    psum x1, waiting for transfers between devices, per_device(): lax.psum(for_sending(shard_sums), 'seq')  213 us
    all_gather x1, waiting for transfers between devices, per_device(): lax.all_gather(shards[2], 'fsdp', axis=1, tiled=True)  159 us
    all_gather x1, waiting for transfers between devices, per_device(): lax.all_gather(late_shards[2], 'fsdp', axis=1, tiled=True)  159 us
    dot_general x12, matrix products, contract_rows(): lax.dot_general(left, right, (((0,), (0,)), ((), ())), preferred_element_...  149 us
    all_gather x3, waiting for transfers between devices, forward_layer(): lax.all_gather(key_b, 'seq', axis=0, tiled=True)  117 us
    all_gather x3, waiting for transfers between devices, forward_layer(): lax.all_gather(value_b, 'seq', axis=0, tiled=True)  90.4 us
    all_gather x1, waiting for transfers between devices, per_device(): lax.all_gather(shards[3], 'fsdp', axis=1, tiled=True)  89.5 us
  transfers between devices with their start and end apart: 31, of which 22 were waited for; matrix products, arithmetic and copies ran while one was open for 13% of the time, Pallas kernels for 0%

commit v1 on v0

--- a/solution.py
+++ b/solution.py
@@ -3,6 +3,8 @@
 import jax
 import jax.numpy as jnp
 from jax import lax
+from jax.experimental import pallas as pl
+from jax.experimental.pallas import tpu as pltpu
 from jax.sharding import PartitionSpec as P
 
 HEAD = 64
@@ -254,7 +256,7 @@
     return (grad_hidden, grads)
 
 
-def per_device(
+def per_device_general(
     tokens, cotangent, lengths, valid_mask, w_qkv, w_out, w_in, w_down, qk_scale, mlp_scale, alphas
 ):
     shards = (w_qkv, w_out, w_in, w_down, qk_scale, mlp_scale, alphas)
@@ -362,6 +364,523 @@
     )
 
 
+FIRST = (1, 2)
+SECOND = (0, 3)
+EVERY = (0, 1, 2, 3)
+BLOCK = 128
+SCORE_SCALE = math.sqrt(HEAD)
+MASKED = -1e30
+
+
+def dot(left, right):
+    return jnp.dot(left, right, preferred_element_type=jnp.float32)
+
+
+def low(x):
+    return x.astype(jnp.bfloat16)
+
+
+def swap(x):
+    return lax.ppermute(x, "section", [(0, 1), (1, 0)])
+
+
+def hop(x, bit, planes):
+    route = [(s * 4 + f, s * 4 + (f ^ bit)) for s in planes for f in range(4)]
+    return lax.ppermute(x, ("seq", "fsdp"), route)
+
+
+def along(x, route):
+    return lax.ppermute(x, "seq", route)
+
+
+def pick(x, index, axis):
+    return lax.dynamic_index_in_dim(x, index, axis, keepdims=False)
+
+
+def gather_rows(piece, f):
+    half = piece.shape[0] // 2
+    from_x = hop(piece, 1, EVERY)
+    from_y = hop(piece, 2, EVERY)
+    across = jnp.concatenate([hop(from_x[:half], 2, EVERY), hop(from_y[half:], 1, EVERY)])
+    rows = jnp.zeros((4,) + piece.shape, piece.dtype)
+    for bit, block in enumerate((piece, from_x, from_y, across)):
+        rows = lax.dynamic_update_index_in_dim(rows, block, f ^ bit, 0)
+    return rows.reshape((-1,) + piece.shape[1:])
+
+
+def scatter_rows(total, f, planes):
+    blocks = total.reshape((4, 2, total.shape[0] // 8) + total.shape[1:])
+
+    def block(bit, part):
+        return lax.dynamic_slice(
+            blocks, (f ^ bit, part, 0, 0), (1, 1) + blocks.shape[2:]
+        ).reshape(blocks.shape[2:])
+
+    done = []
+    for part, (near, far) in enumerate(((1, 2), (2, 1))):
+        got_own = hop(block(near, part), near, planes)
+        got_far = hop(block(3, part), near, planes)
+        passed = low(block(far, part).astype(jnp.float32) + got_far.astype(jnp.float32))
+        got_last = hop(passed, far, planes)
+        done.append(
+            block(0, part).astype(jnp.float32)
+            + got_own.astype(jnp.float32)
+            + got_last.astype(jnp.float32)
+        )
+    return low(jnp.concatenate(done))
+
+
+def sums_of_halves(x):
+    row = lax.broadcasted_iota(jnp.int32, (2 * HEAD, 2 * HEAD), 0) // HEAD
+    col = lax.broadcasted_iota(jnp.int32, (2 * HEAD, 2 * HEAD), 1) // HEAD
+    same = (row == col).astype(jnp.bfloat16)
+    high = x.astype(jnp.bfloat16)
+    rest = (x - high.astype(jnp.float32)).astype(jnp.bfloat16)
+    return dot(high, same) + dot(rest, same)
+
+
+def normal_heads(raw):
+    factor = lax.rsqrt(sums_of_halves(raw * raw) + epsilon)
+    return raw * factor, factor
+
+
+def merge(to, own, oth):
+    for s in range(4):
+        to[s * 256 : s * 256 + BLOCK, : own.shape[1]] = own[s * BLOCK : (s + 1) * BLOCK]
+        to[s * 256 + BLOCK : (s + 1) * 256, : own.shape[1]] = oth[s * BLOCK : (s + 1) * BLOCK]
+
+
+def last_dims(left, right):
+    return lax.dot_general(left, right, (((1,), (1,)), ((), ())), preferred_element_type=jnp.float32)
+
+
+def head_lanes(h, dtype):
+    lane = lax.broadcasted_iota(jnp.int32, (1, 2 * HEAD), 1) // HEAD
+    return (lane == h).astype(dtype)
+
+
+def attention_kernel(
+    q_own, k_own, v_own, q_oth, k_oth, v_oth, scale, place_col, start_col, place_row,
+    out_own, out_oth, bias, raw, queries, keys, values,
+):
+    @pl.when(pl.program_id(0) == 0)
+    def _():
+        fits = (place_row[...] >= start_col[...]) & (place_row[...] <= place_col[...])
+        bias[...] = jnp.where(fits, 0.0, MASKED)
+        values[:, 2 * HEAD :] = jnp.ones_like(values[:, 2 * HEAD :])
+
+    merge(raw, q_own[...], q_oth[...])
+    normed, _ = normal_heads(raw[...].astype(jnp.float32))
+    queries[...] = low(normed * scale[...]) * SCORE_SCALE
+    merge(raw, k_own[...], k_oth[...])
+    normed, _ = normal_heads(raw[...].astype(jnp.float32))
+    keys[...] = low(normed * scale[...])
+    merge(values, v_own[...], v_oth[...])
+    for s in range(4):
+        upto = (s + 1) * 256
+        block = queries[s * 256 : upto]
+        parts = []
+        for h in range(2):
+            scores = last_dims(block * head_lanes(h, jnp.bfloat16), keys[:upto])
+            weights = jnp.exp(scores + bias[s * 256 : upto, :upto])
+            summed = dot(low(weights), values[:upto])
+            parts.append(summed[:, : 2 * HEAD] / summed[:, 2 * HEAD :])
+        joined = low(jnp.where(head_lanes(0, jnp.float32) > 0, parts[0], parts[1]))
+        out_own[s * BLOCK : (s + 1) * BLOCK] = joined[:BLOCK]
+        out_oth[s * BLOCK : (s + 1) * BLOCK] = joined[BLOCK:]
+
+
+def attention_back_kernel(
+    q_own, k_own, v_own, q_oth, k_oth, v_oth, g_own, g_oth, scale,
+    place_col, place_row, start_row,
+    out_own, out_oth, grad_scale, bias, raw, queries, keys, values, grads, dq, dk, dv,
+):
+    pair = pl.program_id(0)
+
+    @pl.when(pair == 0)
+    def _():
+        fits = (place_col[...] >= start_row[...]) & (place_col[...] <= place_row[...])
+        bias[...] = jnp.where(fits, 0.0, MASKED)
+
+    merge(raw, q_own[...], q_oth[...])
+    normed, _ = normal_heads(raw[...].astype(jnp.float32))
+    queries[...] = low(normed * scale[...]) * SCORE_SCALE
+    merge(raw, k_own[...], k_oth[...])
+    normed, _ = normal_heads(raw[...].astype(jnp.float32))
+    keys[...] = low(normed * scale[...])
+    merge(values, v_own[...], v_oth[...])
+    merge(grads, g_own[...], g_oth[...])
+    dk[...] = jnp.zeros_like(dk)
+    dv[...] = jnp.zeros_like(dv)
+    for s in range(4):
+        upto = (s + 1) * 256
+        total = 0.0
+        for h in range(2):
+            lanes = head_lanes(h, jnp.bfloat16)
+            query = queries[s * 256 : upto] * lanes
+            grad = grads[s * 256 : upto] * lanes
+            scores = last_dims(keys[:upto], query)
+            weights = jnp.exp(scores + bias[:upto, s * 256 : upto])
+            weights = weights * (1.0 / jnp.sum(weights, axis=0, keepdims=True))
+            grad_weights = last_dims(values[:upto], grad)
+            delta = jnp.sum(weights * grad_weights, axis=0, keepdims=True)
+            grad_scores = low(weights * (grad_weights - delta))
+            dv[:upto] += dot(low(weights), grad)
+            dk[:upto] += dot(grad_scores, query)
+            total = total + head_lanes(h, jnp.float32) * contract_rows(grad_scores, keys[:upto])
+        dq[s * 256 : upto] = total * SCORE_SCALE
+
+    width = out_own.shape[1] // 3
+    scale_sum = 0.0
+    for part, (own, oth, grad) in enumerate(((q_own, q_oth, dq), (k_own, k_oth, dk))):
+        merge(raw, own[...], oth[...])
+        normed, factor = normal_heads(raw[...].astype(jnp.float32))
+        scale_sum = scale_sum + jnp.sum(grad[...] * normed, axis=0, keepdims=True)
+        step = grad[...] * scale[...]
+        grad[...] = factor * (step - normed * sums_of_halves(normed * step))
+    grad_scale[...] = scale_sum
+    for part, grad in enumerate((dq, dk, dv)):
+        lanes = pl.ds(pl.multiple_of(part * width + pair * 2 * HEAD, 2 * HEAD), 2 * HEAD)
+        for s in range(4):
+            rows = slice(s * BLOCK, (s + 1) * BLOCK)
+            out_own[rows, lanes] = low(grad[s * 256 : s * 256 + BLOCK])
+            out_oth[rows, lanes] = low(grad[s * 256 + BLOCK : (s + 1) * 256])
+
+
+def mixed_specs(rows, pairs):
+    return [
+        pl.BlockSpec((rows, 2 * HEAD), lambda p, part=part: (0, part * pairs + p))
+        for part in range(3)
+    ]
+
+
+def whole(shape):
+    return pl.BlockSpec(shape, lambda p: (0,) * len(shape))
+
+
+def attention(mixed_own, mixed_oth, scale, places):
+    rows, width = mixed_own.shape
+    width //= 3
+    pairs = width // (2 * HEAD)
+    place, start = places
+    total = 2 * rows
+    spec = pl.BlockSpec((rows, 2 * HEAD), lambda p: (0, p))
+    return pl.pallas_call(
+        attention_kernel,
+        grid=(pairs,),
+        out_shape=[jax.ShapeDtypeStruct((rows, width), jnp.bfloat16)] * 2,
+        in_specs=mixed_specs(rows, pairs) * 2
+        + [pl.BlockSpec((1, 2 * HEAD), lambda p: (0, p))]
+        + [whole((total, 1)), whole((total, 1)), whole((1, total))],
+        out_specs=[spec, spec],
+        scratch_shapes=[
+            pltpu.VMEM((total, total), jnp.float32),
+            pltpu.VMEM((total, 2 * HEAD), jnp.bfloat16),
+            pltpu.VMEM((total, 2 * HEAD), jnp.bfloat16),
+            pltpu.VMEM((total, 2 * HEAD), jnp.bfloat16),
+            pltpu.VMEM((total, 4 * HEAD), jnp.bfloat16),
+        ],
+        compiler_params=pltpu.CompilerParams(vmem_limit_bytes=40 * 2**20),
+        cost_estimate=pl.CostEstimate(
+            flops=8 * total * total * width, bytes_accessed=8 * total * width,
+            transcendentals=total * total * pairs,
+        ),
+    )(
+        *[mixed_own] * 3, *[mixed_oth] * 3, scale,
+        place[:, None], start[:, None], place[None, :],
+    )
+
+
+def attention_back(mixed_own, mixed_oth, grad_own, grad_oth, scale, places):
+    rows, width = mixed_own.shape
+    width //= 3
+    pairs = width // (2 * HEAD)
+    place, start = places
+    total = 2 * rows
+    spec = pl.BlockSpec((rows, 2 * HEAD), lambda p: (0, p))
+    pair_spec = pl.BlockSpec((1, 2 * HEAD), lambda p: (0, p))
+    low_scratch = pltpu.VMEM((total, 2 * HEAD), jnp.bfloat16)
+    full_scratch = pltpu.VMEM((total, 2 * HEAD), jnp.float32)
+    return pl.pallas_call(
+        attention_back_kernel,
+        grid=(pairs,),
+        out_shape=[jax.ShapeDtypeStruct((rows, 3 * width), jnp.bfloat16)] * 2
+        + [jax.ShapeDtypeStruct((1, width), jnp.float32)],
+        in_specs=mixed_specs(rows, pairs) * 2
+        + [spec, spec, pair_spec]
+        + [whole((total, 1)), whole((1, total)), whole((1, total))],
+        out_specs=[whole((rows, 3 * width)), whole((rows, 3 * width)), pair_spec],
+        scratch_shapes=[pltpu.VMEM((total, total), jnp.float32)]
+        + [low_scratch] * 5
+        + [full_scratch] * 3,
+        compiler_params=pltpu.CompilerParams(vmem_limit_bytes=48 * 2**20),
+        cost_estimate=pl.CostEstimate(
+            flops=20 * total * total * width, bytes_accessed=16 * total * width,
+            transcendentals=total * total * pairs,
+        ),
+    )(
+        *[mixed_own] * 3, *[mixed_oth] * 3, grad_own, grad_oth, scale,
+        place[:, None], place[None, :], start[None, :],
+    )
+
+
+def forward_row(hidden_own, weights, scales, places):
+    w_qkv, w_out, w_up, w_gate, w_down = weights
+    scale_qk, scale_up, scale_gate, alpha_attn, alpha_mlp = scales
+    hidden_oth = swap(hidden_own)
+    mixed_own = low(dot(hidden_own, w_qkv))
+    mixed_oth = low(dot(hidden_oth, w_qkv))
+    attended_own, attended_oth = attention(mixed_own, mixed_oth, scale_qk, places)
+    branch_got = swap(low(dot(attended_oth, w_out)))
+    branch = dot(attended_own, w_out) + branch_got.astype(jnp.float32)
+    hidden = hidden_own.astype(jnp.float32)
+    first_sum = hidden + alpha_attn * (unit(branch) - hidden)
+    middle = unit(first_sum)
+    middle_own = low(middle)
+    middle_oth = swap(middle_own)
+
+    def lift(rows):
+        lift_up = low(dot(rows, w_up))
+        lift_gate = dot(rows, w_gate)
+        upward = lift_up.astype(jnp.float32) * scale_up
+        gating = lift_gate * scale_gate
+        return lift_up, low(lift_gate), low(upward * jax.nn.silu(gating))
+
+    lifted_own = lift(middle_own)
+    lifted_oth = lift(middle_oth)
+    output_got = swap(low(dot(lifted_oth[2], w_down)))
+    output = dot(lifted_own[2], w_down) + output_got.astype(jnp.float32)
+    second_sum = middle + alpha_mlp * (unit(output) - middle)
+    result = low(unit(second_sum))
+    kept = (
+        (hidden_own, hidden_oth), (mixed_own, mixed_oth), (attended_own, attended_oth),
+        (middle_own, middle_oth), (lifted_own, lifted_oth), branch, output,
+    )
+    return result, kept
+
+
+def backward_row(grad_out, kept, weights, scales, places):
+    w_qkv, w_out, w_up, w_gate, w_down = weights
+    scale_qk, scale_up, scale_gate, alpha_attn, alpha_mlp = scales
+    hiddens, mixed, attended, middles, lifted, branch, output = kept
+    hidden = hiddens[0].astype(jnp.float32)
+    unit_branch = unit(branch)
+    first_sum = hidden + alpha_attn * (unit_branch - hidden)
+    middle = unit(first_sum)
+    unit_output = unit(output)
+    second_sum = middle + alpha_mlp * (unit_output - middle)
+    grad_second = unit_back(second_sum, grad_out)
+    grad_alpha_mlp = jnp.sum(grad_second * (unit_output - middle), axis=0)
+    grad_output_own = low(unit_back(output, alpha_mlp * grad_second))
+    grad_output_oth = swap(grad_output_own)
+
+    def unlift(grad_rows, lifts):
+        lift_up, lift_gate, _ = lifts
+        lift_up = lift_up.astype(jnp.float32)
+        lift_gate = lift_gate.astype(jnp.float32)
+        grad_inner = contract_cols(grad_rows, w_down)
+        gating = lift_gate * scale_gate
+        sigmoid = jax.nn.sigmoid(gating)
+        grad_up = grad_inner * (gating * sigmoid)
+        grad_gate = grad_inner * (lift_up * scale_up) * sigmoid * (1.0 + gating * (1.0 - sigmoid))
+        sums = (jnp.sum(grad_up * lift_up, axis=0), jnp.sum(grad_gate * lift_gate, axis=0))
+        return low(grad_up * scale_up), low(grad_gate * scale_gate), sums
+
+    grad_lift_own = unlift(grad_output_own, lifted[0])
+    grad_lift_oth = unlift(grad_output_oth, lifted[1])
+    middle_got = swap(
+        low(contract_cols(grad_lift_oth[0], w_up) + contract_cols(grad_lift_oth[1], w_gate))
+    )
+    grad_middle = (
+        contract_cols(grad_lift_own[0], w_up)
+        + contract_cols(grad_lift_own[1], w_gate)
+        + middle_got.astype(jnp.float32)
+        + grad_second * (1.0 - alpha_mlp)
+    )
+    grad_first = unit_back(first_sum, grad_middle)
+    grad_alpha_attn = jnp.sum(grad_first * (unit_branch - hidden), axis=0)
+    grad_branch_own = low(unit_back(branch, alpha_attn * grad_first))
+    grad_branch_oth = swap(grad_branch_own)
+    grad_attended_own = low(contract_cols(grad_branch_own, w_out))
+    grad_attended_oth = low(contract_cols(grad_branch_oth, w_out))
+    grad_mixed_own, grad_mixed_oth, grad_scale_qk = attention_back(
+        *mixed, grad_attended_own, grad_attended_oth, scale_qk, places
+    )
+    hidden_got = swap(low(contract_cols(grad_mixed_oth, w_qkv)))
+    grad_hidden = (
+        contract_cols(grad_mixed_own, w_qkv)
+        + hidden_got.astype(jnp.float32)
+        + grad_first * (1.0 - alpha_attn)
+    )
+    operands = (
+        (hiddens, (grad_mixed_own, grad_mixed_oth)),
+        (attended, (grad_branch_own, grad_branch_oth)),
+        (middles, (grad_lift_own[0], grad_lift_oth[0])),
+        (middles, (grad_lift_own[1], grad_lift_oth[1])),
+        ((lifted[0][2], lifted[1][2]), (grad_output_own, grad_output_oth)),
+    )
+    small = (
+        jnp.concatenate([grad_alpha_attn, grad_alpha_mlp]),
+        grad_lift_own[2][0] + grad_lift_oth[2][0],
+        (grad_lift_own[2][1] + grad_lift_oth[2][1]) * math.sqrt(hidden.shape[1]),
+        grad_scale_qk[0],
+    )
+    return low(grad_hidden), operands, small
+
+
+def weight_grads(operands):
+    return tuple(
+        low(contract_rows(jnp.concatenate(left), jnp.concatenate(right)))
+        for left, right in operands
+    )
+
+
+def to_rows_of_planes(sent, s):
+    return lax.all_to_all(sent, "seq", 0, 0)
+
+
+def per_device(
+    tokens, cotangent, lengths, valid_mask, w_qkv, w_out, w_in, w_down, qk_scale, mlp_scale, alphas
+):
+    c = lax.axis_index("section")
+    s = lax.axis_index("seq")
+    f = lax.axis_index("fsdp")
+    second = (s == 0) | (s == 3)
+    layer = second.astype(jnp.int32)
+    micro = s // 2
+    width = tokens.shape[3]
+    group = tokens.shape[2]
+    units = w_down.shape[1] * 4
+
+    sources = jnp.stack([cotangent[0, 0], tokens[0, 0], tokens[1, 0], cotangent[1, 0]])
+    sent = pick(sources.reshape(4, 2, BLOCK, width), c, 1)
+    row = to_rows_of_planes(sent, s).reshape(4 * BLOCK, width)
+
+    def mine(shard, axis):
+        own = pick(shard, c, axis)
+        got = swap(pick(shard, 1 - c, axis))
+        return jnp.where(layer == c, own, got)
+
+    half_qkv = mine(w_qkv[0].reshape(-1, 3, 4, 2, 2 * HEAD), 3).reshape(-1, 3 * width // 2)
+    half_out = mine(w_out[0].reshape(2, -1, width), 0)
+    half_in = mine(w_in[0].reshape(-1, 2, 4, 2, units // 8), 3).reshape(-1, 2, units // 2)
+    half_down = mine(w_down[0].reshape(2, -1, width), 0)
+    weights = (
+        gather_rows(half_qkv, f),
+        gather_rows(half_out, f),
+        gather_rows(half_in[:, 0], f),
+        gather_rows(half_in[:, 1], f),
+        gather_rows(half_down, f),
+    )
+
+    vectors = jnp.concatenate([qk_scale, mlp_scale, alphas], axis=1)
+    vectors = lax.all_gather(vectors, ("section", "fsdp"), axis=0, tiled=True)
+    vectors = pick(vectors.reshape(2, 4, -1), layer, 0).astype(jnp.float32)
+    cut_qk, cut_mlp = qk_scale.shape[1], qk_scale.shape[1] + mlp_scale.shape[1]
+    all_qk = vectors[:, :cut_qk].reshape(4, 2, -1)
+    all_mlp = vectors[:, cut_qk:cut_mlp].reshape(2, 4, 2, -1)
+    all_alphas = vectors[:, cut_mlp:].reshape(2, 1, -1)
+    mlp_half = pick(all_mlp, c, 2).reshape(2, 1, -1)
+    scales = (
+        pick(all_qk, c, 1).reshape(1, -1),
+        mlp_half[0],
+        mlp_half[1] * math.sqrt(width),
+        all_alphas[0],
+        all_alphas[1],
+    )
+
+    index = jnp.arange(4 * group, dtype=jnp.int32)
+    place = (index // 256) * 256 + (((index // BLOCK) + c) % 2) * BLOCK + index % BLOCK
+    ends = jnp.cumsum(pick(lengths, micro, 0)[0])[:-1]
+    passed = place[:, None] >= ends[None, :]
+    start = jnp.max(jnp.where(passed, ends[None, :], 0), axis=1)
+    places = (place, start)
+
+    valid = lax.all_gather(low(valid_mask[:, 0]), "seq", axis=0)
+    valid = pick(pick(valid, micro, 1).reshape(4, 2, BLOCK), c, 1).reshape(-1).astype(jnp.float32)
+
+    result, _ = forward_row(row, weights, scales, places)
+    arrived = along(result, [(1, 0), (2, 3)])
+    hidden_own = jnp.where(second, arrived, row)
+    result, kept = forward_row(hidden_own, weights, scales, places)
+    branch = kept[5]
+    statistic = jnp.sum(valid * jnp.sum(branch * branch, axis=-1))
+
+    grad_row = row.astype(jnp.float32)
+    grad_hidden, operands, small_second = backward_row(grad_row, kept, weights, scales, places)
+    arrived = along(grad_hidden, [(0, 1), (3, 2)])
+    grads_second = weight_grads(operands)
+    grad_row = jnp.where(second, grad_row, arrived.astype(jnp.float32))
+    grad_hidden, operands, small_first = backward_row(grad_row, kept, weights, scales, places)
+    grads_first = weight_grads(operands)
+
+    reduced = []
+    for from_second, from_first in zip(grads_second, grads_first):
+        part = scatter_rows(from_second, f, SECOND)
+        near = along(part, [(0, 1), (3, 2)])
+        both = jnp.where(second, part, near)
+        across = along(both, [(1, 2), (2, 1)])
+        far = along(jnp.where(second, part, across), [(1, 0), (2, 3)])
+        layer_1 = jnp.where(second, part, near).astype(jnp.float32) + jnp.where(
+            second, far, across
+        ).astype(jnp.float32)
+        part = scatter_rows(from_first, f, FIRST)
+        across = along(part, [(1, 2), (2, 1)])
+        total = low(part.astype(jnp.float32) + across.astype(jnp.float32))
+        outward = along(total, [(1, 0), (2, 3)])
+        layer_0 = jnp.where(second, outward, total)
+        layer_1 = low(layer_1)
+        own = jnp.where(c == 0, layer_0, layer_1)
+        got = swap(jnp.where(c == 0, layer_1, layer_0))
+        reduced.append((jnp.where(c == 0, own, got), jnp.where(c == 0, got, own)))
+
+    def columns(halves, groups):
+        parts = [half.reshape(half.shape[0], groups, -1) for half in halves]
+        return jnp.stack(parts, axis=2).reshape(parts[0].shape[0], -1)
+
+    grad_qkv = columns(reduced[0], 12)
+    grad_out = jnp.concatenate(reduced[1])
+    grad_in_proj = jnp.concatenate([columns(reduced[2], 4), columns(reduced[3], 4)], axis=1)
+    grad_down = jnp.concatenate(reduced[4])
+
+    def to_owners(block):
+        got = to_rows_of_planes(block.reshape(4, BLOCK, width), s)
+        layers = (jnp.stack([got[1], got[2]]), jnp.stack([got[0], got[3]]))
+        own = jnp.where(c == 0, layers[0], layers[1])
+        other = swap(jnp.where(c == 0, layers[1], layers[0]))
+        halves = (jnp.where(c == 0, own, other), jnp.where(c == 0, other, own))
+        return jnp.concatenate(halves, axis=1)[None, :, None]
+
+    hidden_out = to_owners(result)
+    grad_in = to_owners(grad_hidden).astype(jnp.float32)
+
+    small = [jnp.where(second, late, early) for late, early in zip(small_second, small_first)]
+    up_gate = jnp.stack([small[1], small[2]]).reshape(2, 4, 1, -1)
+    at_half = jnp.arange(2).reshape(1, 1, 2, 1) == c
+    full = jnp.concatenate(
+        [
+            small[0],
+            jnp.where(at_half, up_gate, 0.0).reshape(-1),
+            jnp.where(at_half, small[3].reshape(1, 4, 1, -1), 0.0).reshape(-1),
+            statistic[None],
+        ]
+    )
+    full = jnp.where(jnp.arange(2)[:, None] == layer, full[None], 0.0)
+    full = pick(lax.psum(full, ("section", "seq", "fsdp")), c, 0)
+    ends = (2 * width, 2 * width + 2 * units, 3 * width + 2 * units)
+    grad_alphas = pick(full[: ends[0]].reshape(4, -1), f, 0)[None]
+    grad_mlp_scale = pick(full[ends[0] : ends[1]].reshape(4, -1), f, 0)[None]
+    grad_qk_scale = pick(full[ends[1] : ends[2]].reshape(4, -1), f, 0)[None]
+    token_count = tokens.shape[0] * lax.axis_size("fsdp") * 4 * group
+    rms_stats = jnp.sqrt(full[ends[2] :] / token_count + epsilon)
+    as_float = [
+        part.astype(jnp.float32)[None] for part in (grad_qkv, grad_out, grad_in_proj, grad_down)
+    ]
+    return (
+        hidden_out, grad_in, *as_float, grad_qk_scale, grad_mlp_scale, grad_alphas, rms_stats,
+    )
+
+
 def solution(mesh):
     placed = (
         P(None, "fsdp", "seq", None),
@@ -376,8 +895,9 @@
         P("section", "fsdp"),
         P("section", "fsdp"),
     )
+    planes = mesh.shape["section"] == 2 and mesh.shape["seq"] == 4 and mesh.shape["fsdp"] == 4
     return jax.shard_map(
-        per_device,
+        per_device if planes else per_device_general,
         mesh=mesh,
         in_specs=placed,
         out_specs=(

time: 2550 us -> 1420 us (0.56)
  waiting for transfers between devices: 1490 us -> 416 us
  starting transfers between devices: 12.2 us -> 326 us
  matrix products: 465 us -> 204 us
  blocking collectives: 123 us -> 35.9 us
  Pallas kernels: 0 us -> 80.8 us
  other arithmetic: 222 us -> 151 us
  loops' own time: 33.6 us -> 0 us
    all_gather x14 -> x0, waiting for transfers between devices: 872 us -> none  [the longest x1 159 us: per_device(): lax.all_gather(shards[2], 'fsdp', axis=1, tiled=True)]
    reduce_scatter x10 -> x0, waiting for transfers between devices: 397 us -> none  [the longest x4 321 us: per_device(): lax.psum_scatter(for_sending(sums), 'fsdp', scatter_dimension=0, tiled=True)]
    ppermute x6 -> x134, waiting for transfers between devices: 0.02 us -> 323 us  [the longest x27 187 us: along(): return lax.ppermute(x, 'seq', route)]
    ppermute x6 -> x134, starting transfers between devices: 11.4 us -> 278 us  [the longest x80 150 us: hop(): return lax.ppermute(x, ('seq', 'fsdp'), route)]
    dot_general x33 -> x18, matrix products: 236 us -> 69.6 us  [dot(): return jnp.dot(left, right, preferred_element_type=jnp.float32)]
    psum x1, waiting for transfers between devices: 213 us -> 92.8 us  [per_device(): full = pick(lax.psum(full, ('section', 'seq', 'fsdp')), c, 0)]
    dot_general x12 -> x10, matrix products: 149 us -> 48.9 us  [contract_rows(): lax.dot_general(left, right, (((0,), (0,)), ((), ())), preferred_element_...]
    pallas_call x0 -> x4, Pallas kernels: none -> 80.8 us  [the longest x2 58.7 us: attention_back(): pl.pallas_call(attention_back_kernel, grid=(pairs,), out_shape=[jax.Shape...]
  transfers between devices with their start and end apart: 31 -> 138, of which waited for: 22 -> 34; matrix products, arithmetic and copies ran while one was open for 13% -> 29% of each run, Pallas kernels for 0% -> 5%
where the time goes in v1:
time: 1420 us; the launch traced here: 1410 us
  waiting for transfers between devices  416 us (29%)
  starting transfers between devices  326 us (23%)
  matrix products  204 us (14%)
  local copies, waits for them, and re-layouts  180 us (13%)
  other arithmetic  151 us (11%)
  Pallas kernels  80.8 us (6%)
  blocking collectives  35.9 us (3%)
  between operations  20.2 us (1%)
    ppermute x27, waiting for transfers between devices, along(): return lax.ppermute(x, 'seq', route)  187 us
    ppermute x80, starting transfers between devices, hop(): return lax.ppermute(x, ('seq', 'fsdp'), route)  150 us
    ppermute x80, waiting for transfers between devices, hop(): return lax.ppermute(x, ('seq', 'fsdp'), route)  131 us
    ppermute x27, starting transfers between devices, along(): return lax.ppermute(x, 'seq', route)  123 us
    psum x1, waiting for transfers between devices, per_device(): full = pick(lax.psum(full, ('section', 'seq', 'fsdp')), c, 0)  92.8 us
    dot_general x20, matrix products, contract_cols(): lax.dot_general(left, right, (((1,), (1,)), ((), ())), preferred_element_...  85.2 us
    dot_general x18, matrix products, dot(): return jnp.dot(left, right, preferred_element_type=jnp.float32)  69.6 us
    pallas_call x2, Pallas kernels, attention_back(): pl.pallas_call(attention_back_kernel, grid=(pairs,), out_shape=[jax.Shape...  58.7 us
  transfers between devices with their start and end apart: 138, of which 34 were waited for; matrix products, arithmetic and copies ran while one was open for 29% of the time, Pallas kernels for 5%

profile of v1, /device:TPU:0, one launch (start us, length us, event | category | flops | bytes accessed | tf_op | source)
XLA Modules:
  0.0 1413.1 jit_solution(10211667410463775354)
XLA Ops:
  32.9 24.0 %all-gather.1 = bf16[8,1,2816]{2,1,0:T(2,128)(2,1)S(1)} all-gather(bf16[1,1,2816]{2,1,0:T(2,128)(2,1)S(1)} %maximum_bitcast_fusion.7), channel_id=1, replica_groups=mesh['section'=2,'seq'=4,'fsdp'=4] {'section','fsdp'}, dimensions={0}, use_global_device_ids=true | all-gather | bytes 50688 | tf_op jit(solution)/shard_map/all_gather | solution.py:777
  112.4 18.0 %collective-permute-done.3 = bf16[128,1536]{0,1:T(8,128)(2,1)} collective-permute-done((bf16[128,1536]{0,1:T(8,128)(2,1)}, bf16[128,1536]{0,1:T(8,128)(2,1)}, u32[]{:S(2)}, u32[]{:S(2)}) %collective-permute-start.3) | collective-permute-done | bytes 393248 | tf_op jit(solution)/shard_map/ppermute | solution.py:389
  178.5 14.9 %collective-permute-done.24 = bf16[256,1024]{1,0:T(8,128)(2,1)S(1)} collective-permute-done((bf16[256,1024]{1,0:T(8,128)(2,1)S(1)}, bf16[256,1024]{1,0:T(8,128)(2,1)S(1)}, u32[]{:S(2)}, u32[]{:S(2)}) %collective-permute-start.24) | collective-permute-done | bytes 524320 | tf_op jit(solution)/shard_map/ppermute | solution.py:389
  198.5 10.8 shard_map.186
  232.3 8.1 collective-permute-done.19
  246.6 10.1 fusion.95
  262.6 10.7 multiply_reduce_fusion.16
  279.4 26.5 %collective-permute-done.28 = bf16[512,1024]{1,0:T(8,128)(2,1)S(1)} collective-permute-done((bf16[512,1024]{1,0:T(8,128)(2,1)S(1)}, bf16[512,1024]{1,0:T(8,128)(2,1)S(1)}, u32[]{:S(2)}, u32[]{:S(2)}) %collective-permute-start.28) | collective-permute-done | bytes 1048608 | tf_op jit(solution)/shard_map/ppermute | solution.py:393
  311.7 11.2 shard_map.187
  350.6 11.9 all-gather
  380.0 11.0 multiply_convert_fusion.7
  408.4 7.1 convolution_convert_fusion.2
  444.8 11.2 collective-permute-done.89
  459.8 7.4 collective-permute-done.107
  488.2 6.9 collective-permute-done.126
  520.1 8.7 collective-permute-done.108
  543.9 7.4 collective-permute-done.91
  573.2 29.4 %shard_map.188 = (bf16[512,1536]{1,0:T(8,128)(2,1)S(1)}, bf16[512,1536]{1,0:T(8,128)(2,1)S(1)}, f32[1,512]{1,0:T(1,128)S(1)}) custom-call(bf16[512,1536]{1,0:T(8,128)(2,1)} %copy-done.4, bf16[512,1536]{1,0:T(8,128)(2,1)} %copy-done.4, bf16[512,1536]{1,0:T(8,128)(2,1)} %copy-done.4, bf16[512,1536]{1,0:T(8,128)(2,1)} %copy-done.5, ...), custom_call_target="tpu_custom_call" | custom-call | flops 10737418240 | bytes 8388608 | tf_op jit(solution)/shard_map/pallas_call | solution.py:604
  655.4 12.9 collective-permute-done.38
  674.7 37.6 %all-to-all-start.1 = ((bf16[4,128,1024]{2,1,0:T(8,128)(2,1)}), bf16[4,128,1024]{2,1,0:T(8,128)(2,1)S(1)}, u32[]{:S(2)}, u32[]{:S(2)}) async-start(bf16[4,128,1024]{2,1,0:T(8,128)(2,1)} %bitcast.504), calls=%async_computation.1 | async-start | bytes 2097152 | tf_op jit(solution)/shard_map/all_to_all | solution.py:739
  719.2 20.1 %fusion.32 = (f32[2048]{0:T(1024)S(1)}, f32[2048]{0:T(1024)S(1)}, f32[2048]{0:T(1024)S(1)}, f32[2048]{0:T(1024)S(1)}, f32[2048]{0:T(1024)S(1)}, /*index=5*/f32[2...) fusion(bf16[512,2048]{1,0:T(8,128)(2,1)} %copy-done.104, ...), kind=kOutput, calls=%fused_computation.44 | convolution fusion | flops 2201993216 | bytes 47267840 | tf_op jit(solution)/shard_map/dot_general | solution.py:43
  754.3 7.5 convolution_convert_fusion.3
  766.5 7.3 collective-permute-start.116
  826.0 81.8 %collective-permute-start.132 = (bf16[512,1024]{1,0:T(8,128)(2,1)}, bf16[512,1024]{1,0:T(8,128)(2,1)}, u32[]{:S(2)}, u32[]{:S(2)}) collective-permute-start(bf16[512,1024]{1,0:T(8,128)(2,1)} %broadcast_select_fusion.16), channel_id=1, source_target_pairs={{4,0},{8,12},{5,1},{9,13},{6,2},{10,14},{7,3},{11,15},{20,16},{24,... | collective-permute-start | bytes 3145736 | tf_op jit(solution)/shard_map/ppermute | solution.py:393
  918.6 29.4 %shard_map.189 = (bf16[512,1536]{1,0:T(8,128)(2,1)S(1)}, bf16[512,1536]{1,0:T(8,128)(2,1)S(1)}, f32[1,512]{1,0:T(1,128)S(1)}) custom-call(bf16[512,1536]{1,0:T(8,128)(2,1)} %copy-done.4, bf16[512,1536]{1,0:T(8,128)(2,1)} %copy-done.4, bf16[512,1536]{1,0:T(8,128)(2,1)} %copy-done.4, bf16[512,1536]{1,0:T(8,128)(2,1)} %copy-done.5, ...), custom_call_target="tpu_custom_call" | custom-call | flops 10737418240 | bytes 8388608 | tf_op jit(solution)/shard_map/pallas_call | solution.py:604
  994.9 92.8 %all-reduce.2.cloned.1.call-done = f32[2,11265]{1,0:T(2,128)} async-done(((f32[2,11265]{1,0:T(2,128)}), f32[2,11265]{1,0:T(2,128)}) %all-reduce.2.cloned.1.call-update) | async-done | bytes 90136 | tf_op jit(solution)/shard_map/psum | solution.py:869
  1111.1 8.6 collective-permute-done.56
  1161.3 66.4 %collective-permute-done.69 = bf16[128,1024]{1,0:T(8,128)(2,1)S(1)} collective-permute-done((bf16[128,1024]{1,0:T(8,128)(2,1)S(1)}, bf16[128,1024]{1,0:T(8,128)(2,1)S(1)}, u32[]{:S(2)}, u32[]{:S(2)}) %collective-permute-start.69) | collective-permute-done | bytes 262176 | tf_op jit(solution)/shard_map/ppermute | solution.py:393
  1244.3 12.6 collective-permute-done.123
  1263.2 20.8 %collective-permute-done.87 = bf16[256,2048]{1,0:T(8,128)(2,1)} collective-permute-done((bf16[256,2048]{1,0:T(8,128)(2,1)}, bf16[256,2048]{1,0:T(8,128)(2,1)}, u32[]{:S(2)}, u32[]{:S(2)}) %collective-permute-start.87) | collective-permute-done | bytes 1048608 | tf_op jit(solution)/shard_map/ppermute | solution.py:393
  1287.8 24.2 %collective-permute-done.114 = bf16[256,2048]{1,0:T(8,128)(2,1)S(1)} collective-permute-done((bf16[256,2048]{1,0:T(8,128)(2,1)}, bf16[256,2048]{1,0:T(8,128)(2,1)S(1)}, u32[]{:S(2)}, u32[]{:S(2)}) %collective-permute-start.114) | collective-permute-done | bytes 1048608 | tf_op jit(solution)/shard_map/ppermute | solution.py:393
  1312.6 17.2 %collective-permute-done.105 = bf16[256,2048]{1,0:T(8,128)(2,1)S(1)} collective-permute-done((bf16[256,2048]{1,0:T(8,128)(2,1)S(1)}, bf16[256,2048]{1,0:T(8,128)(2,1)S(1)}, u32[]{:S(2)}, u32[]{:S(2)}) %collective-permute-start.105) | collective-permute-done | bytes 1048608 | tf_op jit(solution)/shard_map/ppermute | solution.py:393
  (923 shorter events, 718.5 us)
Async XLA Ops:
  11.1 66.4 %collective-permute-start = (bf16[256,3,4,128]{3,0,2,1:T(8,128)(2,1)}, bf16[256,3,4,128]{3,0,2,1:T(8,128)(2,1)}, u32[]{:S(2)}, u32[]{:S(2)}) collective-permute-start(bf16[256,3,4,128]{3,0,2,1:T(8,128)(2,1)} %bitcast.536), channel_id=1, source_target_pairs={{0,16},{16,0},{1,17},{17,1},{2,18},{18,2},{3,19},{19,3},{4,20},{20... | collective-permute-start | bytes 2359304 | tf_op jit(solution)/shard_map/ppermute | solution.py:384
  12.9 99.6 %all-to-all-start = ((bf16[4,128,1024]{2,1,0:T(8,128)(2,1)}), bf16[4,128,1024]{2,1,0:T(8,128)(2,1)S(1)}, u32[]{:S(2)}, u32[]{:S(2)}) async-start(bf16[4,128,1024]{2,1,0:T(8,128)(2,1)} %fusion.105), calls=%async_computation | async-start | bytes 2097152 | tf_op jit(solution)/shard_map/all_to_all | solution.py:739
  21.3 69.2 %collective-permute-start.21 = (bf16[512,1024]{1,0:T(8,128)(2,1)}, bf16[512,1024]{1,0:T(8,128)(2,1)}, u32[]{:S(2)}, u32[]{:S(2)}) collective-permute-start(bf16[512,1024]{1,0:T(8,128)(2,1)} %dynamic-slice_bitcast_fusion), channel_id=1, source_target_pairs={{0,16},{16,0},{1,17},{17,1},{2,18},{18,2},{3,19},{19,3},{4,20},{20... | collective-permute-start | bytes 3145736 | tf_op jit(solution)/shard_map/ppermute | solution.py:384
  96.2 62.6 %collective-permute-start.22 = (bf16[512,1024]{1,0:T(8,128)(2,1)}, bf16[512,1024]{1,0:T(8,128)(2,1)}, u32[]{:S(2)}, u32[]{:S(2)}) collective-permute-start(bf16[512,1024]{1,0:T(8,128)(2,1)} %get-tuple-element.136), channel_id=1, source_target_pairs={{0,1},{1,0},{2,3},{3,2},{4,5},{5,4},{6,7},{7,6},{8,9},{9,8},{10,11... | collective-permute-start | bytes 3145736 | tf_op jit(solution)/shard_map/ppermute | solution.py:389
  97.6 68.7 %collective-permute-start.23 = (bf16[512,1024]{1,0:T(8,128)(2,1)}, bf16[512,1024]{1,0:T(8,128)(2,1)}, u32[]{:S(2)}, u32[]{:S(2)}) collective-permute-start(bf16[512,1024]{1,0:T(8,128)(2,1)} %get-tuple-element.136), channel_id=1, source_target_pairs={{0,2},{1,3},{2,0},{3,1},{4,6},{5,7},{6,4},{7,5},{8,10},{9,11},{10,... | collective-permute-start | bytes 3145736 | tf_op jit(solution)/shard_map/ppermute | solution.py:389
  154.4 59.3 %collective-permute-start.13 = (bf16[256,2048]{1,0:T(8,128)(2,1)}, bf16[256,2048]{1,0:T(8,128)(2,1)}, u32[]{:S(2)}, u32[]{:S(2)}) collective-permute-start(bf16[256,2048]{1,0:T(8,128)(2,1)} %bitcast.462), channel_id=1, source_target_pairs={{0,1},{1,0},{2,3},{3,2},{4,5},{5,4},{6,7},{7,6},{8,9},{9,8},{10,11... | collective-permute-start | bytes 3145736 | tf_op jit(solution)/shard_map/ppermute | solution.py:389
  155.9 60.4 %collective-permute-start.14 = (bf16[256,2048]{1,0:T(8,128)(2,1)}, bf16[256,2048]{1,0:T(8,128)(2,1)}, u32[]{:S(2)}, u32[]{:S(2)}) collective-permute-start(bf16[256,2048]{1,0:T(8,128)(2,1)} %bitcast.463), channel_id=1, source_target_pairs={{0,2},{1,3},{2,0},{3,1},{4,6},{5,7},{6,4},{7,5},{8,10},{9,11},{10,... | collective-permute-start | bytes 3145736 | tf_op jit(solution)/shard_map/ppermute | solution.py:389
  158.8 59.2 %collective-permute-start.17 = (bf16[256,2048]{1,0:T(8,128)(2,1)}, bf16[256,2048]{1,0:T(8,128)(2,1)S(1)}, u32[]{:S(2)}, u32[]{:S(2)}) collective-permute-start(bf16[256,2048]{1,0:T(8,128)(2,1)} %bitcast.460), channel_id=1, source_target_pairs={{0,1},{1,0},{2,3},{3,2},{4,5},{5,4},{6,7},{7,6},{8,9},{9,8},{10,11... | collective-permute-start | bytes 3145736 | tf_op jit(solution)/shard_map/ppermute | solution.py:389
  408.2 61.6 %collective-permute-start.35 = (bf16[512,1024]{1,0:T(8,128)(2,1)}, bf16[512,1024]{1,0:T(8,128)(2,1)}, u32[]{:S(2)}, u32[]{:S(2)}) collective-permute-start(bf16[512,1024]{1,0:T(8,128)(2,1)} %add_convert_fusion.9), channel_id=1, source_target_pairs={{0,16},{16,0},{1,17},{17,1},{2,18},{18,2},{3,19},{19,3},{4,20},{20... | collective-permute-start | bytes 3145736 | tf_op jit(solution)/shard_map/ppermute | solution.py:384
  422.7 59.5 %collective-permute-start.128 = (bf16[256,1024]{1,0:T(8,128)(2,1)}, bf16[256,1024]{1,0:T(8,128)(2,1)}, u32[]{:S(2)}, u32[]{:S(2)}) collective-permute-start(bf16[256,1024]{1,0:T(8,128)(2,1)} %get-tuple-element.142), channel_id=1, source_target_pairs={{0,2},{1,3},{2,0},{3,1},{12,14},{13,15},{14,12},{15,13},{16,18},{1... | collective-permute-start | bytes 1572872 | tf_op jit(solution)/shard_map/ppermute | solution.py:389
  551.3 76.3 %collective-permute-start.130 = (bf16[512,1024]{1,0:T(8,128)(2,1)}, bf16[512,1024]{1,0:T(8,128)(2,1)}, u32[]{:S(2)}, u32[]{:S(2)}) collective-permute-start(bf16[512,1024]{1,0:T(8,128)(2,1)} %pad_maximum_fusion.14), channel_id=1, source_target_pairs={{0,4},{12,8},{1,5},{13,9},{2,6},{14,10},{3,7},{15,11},{16,20},{28,... | collective-permute-start | bytes 3145736 | tf_op jit(solution)/shard_map/ppermute | solution.py:393
  556.0 76.2 %collective-permute-start.94 = (bf16[256,2048]{1,0:T(8,128)(2,1)}, bf16[256,2048]{1,0:T(8,128)(2,1)}, u32[]{:S(2)}, u32[]{:S(2)}) collective-permute-start(bf16[256,2048]{1,0:T(8,128)(2,1)} %pad_maximum_fusion.10), channel_id=1, source_target_pairs={{0,4},{12,8},{1,5},{13,9},{2,6},{14,10},{3,7},{15,11},{16,20},{28,... | collective-permute-start | bytes 3145736 | tf_op jit(solution)/shard_map/ppermute | solution.py:393
  674.7 118.4 %all-to-all-start.1 = ((bf16[4,128,1024]{2,1,0:T(8,128)(2,1)}), bf16[4,128,1024]{2,1,0:T(8,128)(2,1)S(1)}, u32[]{:S(2)}, u32[]{:S(2)}) async-start(bf16[4,128,1024]{2,1,0:T(8,128)(2,1)} %bitcast.504), calls=%async_computation.1 | async-start | bytes 2097152 | tf_op jit(solution)/shard_map/all_to_all | solution.py:739
  712.3 375.4 %all-reduce.2.cloned.1.call-start = ((), (), s32[]{:S(2)}) async-start(), calls=%async_computation.3 | async-start | bytes 182272 | tf_op jit(solution)/shard_map/psum | solution.py:869
  818.5 341.4 %collective-permute-start.78 = (bf16[128,1024]{1,0:T(8,128)(2,1)}, bf16[128,1024]{1,0:T(8,128)(2,1)}, u32[]{:S(2)}, u32[]{:S(2)}) collective-permute-start(bf16[128,1024]{1,0:T(8,128)(2,1)} %broadcast_select_fusion.33), channel_id=1, source_target_pairs={{4,0},{8,12},{5,1},{9,13},{6,2},{10,14},{7,3},{11,15},{20,16},{24,... | collective-permute-start | bytes 786440 | tf_op jit(solution)/shard_map/ppermute | solution.py:393
  819.9 89.9 %collective-permute-start.119 = (bf16[256,1024]{1,0:T(8,128)(2,1)S(1)}, bf16[256,1024]{1,0:T(8,128)(2,1)S(1)}, u32[]{:S(2)}, u32[]{:S(2)}) collective-permute-start(bf16[256,1024]{1,0:T(8,128)(2,1)S(1)} %get-tuple-element.149), channel_id=1, source_target_pairs={{4,6},{5,7},{6,4},{7,5},{8,10},{9,11},{10,8},{11,9},{20,22},{21,23... | collective-permute-start | bytes 1572872 | tf_op jit(solution)/shard_map/ppermute | solution.py:389
  823.0 87.2 %collective-permute-start.121 = (bf16[256,1024]{1,0:T(8,128)(2,1)S(1)}, bf16[256,1024]{1,0:T(8,128)(2,1)S(1)}, u32[]{:S(2)}, u32[]{:S(2)}) collective-permute-start(bf16[256,1024]{1,0:T(8,128)(2,1)S(1)} %get-tuple-element.146), channel_id=1, source_target_pairs={{4,5},{5,4},{6,7},{7,6},{8,9},{9,8},{10,11},{11,10},{20,21},{21,20... | collective-permute-start | bytes 1572872 | tf_op jit(solution)/shard_map/ppermute | solution.py:389
  823.8 84.1 %collective-permute-start.85 = (bf16[128,2048]{1,0:T(8,128)(2,1)S(1)}, bf16[128,2048]{1,0:T(8,128)(2,1)S(1)}, u32[]{:S(2)}, u32[]{:S(2)}) collective-permute-start(bf16[128,2048]{1,0:T(8,128)(2,1)S(1)} %get-tuple-element.158), channel_id=1, source_target_pairs={{4,5},{5,4},{6,7},{7,6},{8,9},{9,8},{10,11},{11,10},{20,21},{21,20... | collective-permute-start | bytes 1572872 | tf_op jit(solution)/shard_map/ppermute | solution.py:389
  826.0 416.7 %collective-permute-start.132 = (bf16[512,1024]{1,0:T(8,128)(2,1)}, bf16[512,1024]{1,0:T(8,128)(2,1)}, u32[]{:S(2)}, u32[]{:S(2)}) collective-permute-start(bf16[512,1024]{1,0:T(8,128)(2,1)} %broadcast_select_fusion.16), channel_id=1, source_target_pairs={{4,0},{8,12},{5,1},{9,13},{6,2},{10,14},{7,3},{11,15},{20,16},{24,... | collective-permute-start | bytes 3145736 | tf_op jit(solution)/shard_map/ppermute | solution.py:393
  955.9 133.7 %collective-permute-start.63 = (bf16[64,1024]{1,0:T(8,128)(2,1)}, bf16[64,1024]{1,0:T(8,128)(2,1)}, u32[]{:S(2)}, u32[]{:S(2)}) collective-permute-start(bf16[64,1024]{1,0:T(8,128)(2,1)} %get-tuple-element.221), channel_id=1, source_target_pairs={{4,5},{5,4},{6,7},{7,6},{8,9},{9,8},{10,11},{11,10},{20,21},{21,20... | collective-permute-start | bytes 393224 | tf_op jit(solution)/shard_map/ppermute | solution.py:389
  957.2 134.7 %collective-permute-start.62 = (bf16[64,1024]{1,0:T(8,128)(2,1)}, bf16[64,1024]{1,0:T(8,128)(2,1)}, u32[]{:S(2)}, u32[]{:S(2)}) collective-permute-start(bf16[64,1024]{1,0:T(8,128)(2,1)} %get-tuple-element.218), channel_id=1, source_target_pairs={{4,5},{5,4},{6,7},{7,6},{8,9},{9,8},{10,11},{11,10},{20,21},{21,20... | collective-permute-start | bytes 393224 | tf_op jit(solution)/shard_map/ppermute | solution.py:389
  958.6 134.0 %collective-permute-start.66 = (bf16[64,1024]{1,0:T(8,128)(2,1)}, bf16[64,1024]{1,0:T(8,128)(2,1)}, u32[]{:S(2)}, u32[]{:S(2)}) collective-permute-start(bf16[64,1024]{1,0:T(8,128)(2,1)} %get-tuple-element.219), channel_id=1, source_target_pairs={{4,6},{5,7},{6,4},{7,5},{8,10},{9,11},{10,8},{11,9},{20,22},{21,23... | collective-permute-start | bytes 393224 | tf_op jit(solution)/shard_map/ppermute | solution.py:389
  1135.5 127.0 %collective-permute-start.96 = (bf16[256,2048]{1,0:T(8,128)(2,1)}, bf16[256,2048]{1,0:T(8,128)(2,1)}, u32[]{:S(2)}, u32[]{:S(2)}) collective-permute-start(bf16[256,2048]{1,0:T(8,128)(2,1)} %broadcast_select_fusion.5), channel_id=1, source_target_pairs={{4,0},{8,12},{5,1},{9,13},{6,2},{10,14},{7,3},{11,15},{20,16},{24,... | collective-permute-start | bytes 3145736 | tf_op jit(solution)/shard_map/ppermute | solution.py:393
  1156.2 75.0 %collective-permute-start.42 = (bf16[512,1024]{1,0:T(8,128)(2,1)S(1)}, bf16[512,1024]{1,0:T(8,128)(2,1)S(1)}, u32[]{:S(2)}, u32[]{:S(2)}) collective-permute-start(bf16[512,1024]{1,0:T(8,128)(2,1)S(1)} %copy-done.168), channel_id=1, source_target_pairs={{0,16},{16,0},{1,17},{17,1},{2,18},{18,2},{3,19},{19,3},{4,20},{20... | collective-permute-start | bytes 3145736 | tf_op jit(solution)/shard_map/ppermute | solution.py:384
  1156.3 71.4 %collective-permute-start.69 = (bf16[128,1024]{1,0:T(8,128)(2,1)S(1)}, bf16[128,1024]{1,0:T(8,128)(2,1)S(1)}, u32[]{:S(2)}, u32[]{:S(2)}) collective-permute-start(bf16[128,1024]{1,0:T(8,128)(2,1)S(1)} %add_convert_fusion.13), channel_id=1, source_target_pairs={{4,0},{8,12},{5,1},{9,13},{6,2},{10,14},{7,3},{11,15},{20,16},{24,... | collective-permute-start | bytes 786440 | tf_op jit(solution)/shard_map/ppermute | solution.py:393
  1159.9 97.0 %collective-permute-start.123 = (bf16[512,1024]{1,0:T(8,128)(2,1)}, bf16[512,1024]{1,0:T(8,128)(2,1)}, u32[]{:S(2)}, u32[]{:S(2)}) collective-permute-start(bf16[512,1024]{1,0:T(8,128)(2,1)} %add_convert_fusion.1), channel_id=1, source_target_pairs={{4,0},{8,12},{5,1},{9,13},{6,2},{10,14},{7,3},{11,15},{20,16},{24,... | collective-permute-start | bytes 3145736 | tf_op jit(solution)/shard_map/ppermute | solution.py:393
  1234.2 151.8 %all-to-all-start.2 = ((bf16[4,128,1024]{2,1,0:T(8,128)(2,1)}), bf16[4,128,1024]{2,1,0:T(8,128)(2,1)S(1)}, u32[]{:S(2)}, u32[]{:S(2)}) async-start(bf16[4,128,1024]{2,1,0:T(8,128)(2,1)} %bitcast.527), calls=%async_computation.2 | async-start | bytes 2097152 | tf_op jit(solution)/shard_map/all_to_all | solution.py:739
  1239.0 73.0 %collective-permute-start.114 = (bf16[256,2048]{1,0:T(8,128)(2,1)}, bf16[256,2048]{1,0:T(8,128)(2,1)S(1)}, u32[]{:S(2)}, u32[]{:S(2)}) collective-permute-start(bf16[256,2048]{1,0:T(8,128)(2,1)} %broadcast_select_fusion.2), channel_id=1, source_target_pairs={{4,0},{8,12},{5,1},{9,13},{6,2},{10,14},{7,3},{11,15},{20,16},{24,... | collective-permute-start | bytes 3145736 | tf_op jit(solution)/shard_map/ppermute | solution.py:393
  1242.7 87.1 %collective-permute-start.105 = (bf16[256,2048]{1,0:T(8,128)(2,1)S(1)}, bf16[256,2048]{1,0:T(8,128)(2,1)S(1)}, u32[]{:S(2)}, u32[]{:S(2)}) collective-permute-start(bf16[256,2048]{1,0:T(8,128)(2,1)S(1)} %copy-done.53), channel_id=1, source_target_pairs={{4,0},{8,12},{5,1},{9,13},{6,2},{10,14},{7,3},{11,15},{20,16},{24,... | collective-permute-start | bytes 3145736 | tf_op jit(solution)/shard_map/ppermute | solution.py:393
  1262.5 69.9 %collective-permute-start.50 = (bf16[256,1536]{0,1:T(8,128)(2,1)S(1)}, bf16[256,1536]{0,1:T(8,128)(2,1)S(1)}, u32[]{:S(2)}, u32[]{:S(2)}) collective-permute-start(bf16[256,1536]{0,1:T(8,128)(2,1)S(1)} %copy-done.134), channel_id=1, source_target_pairs={{4,8},{8,4},{5,9},{9,5},{6,10},{10,6},{7,11},{11,7},{20,24},{24,20... | collective-permute-start | bytes 2359304 | tf_op jit(solution)/shard_map/ppermute | solution.py:393
  1284.0 112.2 %collective-permute-start.133 = (bf16[512,1024]{1,0:T(8,128)(2,1)}, bf16[512,1024]{1,0:T(8,128)(2,1)}, u32[]{:S(2)}, u32[]{:S(2)}) collective-permute-start(bf16[512,1024]{1,0:T(8,128)(2,1)} %get-tuple-element.101), channel_id=1, source_target_pairs={{0,16},{16,0},{1,17},{17,1},{2,18},{18,2},{3,19},{19,3},{4,20},{20... | collective-permute-start | bytes 3145736 | tf_op jit(solution)/shard_map/ppermute | solution.py:384
  1333.5 60.0 %collective-permute-start.51 = (bf16[256,1536]{0,1:T(8,128)(2,1)}, bf16[256,1536]{0,1:T(8,128)(2,1)}, u32[]{:S(2)}, u32[]{:S(2)}) collective-permute-start(bf16[256,1536]{0,1:T(8,128)(2,1)} %add_convert_fusion.11), channel_id=1, source_target_pairs={{4,0},{8,12},{5,1},{9,13},{6,2},{10,14},{7,3},{11,15},{20,16},{24,... | collective-permute-start | bytes 2359304 | tf_op jit(solution)/shard_map/ppermute | solution.py:393
  (291 other events, 5260.2 us)
Sparse Core Ops, SparseCore 0:
  951.8 135.8 all-reduce.1

commit v2 on v1

--- a/solution.py
+++ b/solution.py
@@ -384,50 +384,12 @@
     return lax.ppermute(x, "section", [(0, 1), (1, 0)])
 
 
-def hop(x, bit, planes):
-    route = [(s * 4 + f, s * 4 + (f ^ bit)) for s in planes for f in range(4)]
-    return lax.ppermute(x, ("seq", "fsdp"), route)
-
-
 def along(x, route):
     return lax.ppermute(x, "seq", route)
 
 
 def pick(x, index, axis):
     return lax.dynamic_index_in_dim(x, index, axis, keepdims=False)
-
-
-def gather_rows(piece, f):
-    half = piece.shape[0] // 2
-    from_x = hop(piece, 1, EVERY)
-    from_y = hop(piece, 2, EVERY)
-    across = jnp.concatenate([hop(from_x[:half], 2, EVERY), hop(from_y[half:], 1, EVERY)])
-    rows = jnp.zeros((4,) + piece.shape, piece.dtype)
-    for bit, block in enumerate((piece, from_x, from_y, across)):
-        rows = lax.dynamic_update_index_in_dim(rows, block, f ^ bit, 0)
-    return rows.reshape((-1,) + piece.shape[1:])
-
-
-def scatter_rows(total, f, planes):
-    blocks = total.reshape((4, 2, total.shape[0] // 8) + total.shape[1:])
-
-    def block(bit, part):
-        return lax.dynamic_slice(
-            blocks, (f ^ bit, part, 0, 0), (1, 1) + blocks.shape[2:]
-        ).reshape(blocks.shape[2:])
-
-    done = []
-    for part, (near, far) in enumerate(((1, 2), (2, 1))):
-        got_own = hop(block(near, part), near, planes)
-        got_far = hop(block(3, part), near, planes)
-        passed = low(block(far, part).astype(jnp.float32) + got_far.astype(jnp.float32))
-        got_last = hop(passed, far, planes)
-        done.append(
-            block(0, part).astype(jnp.float32)
-            + got_own.astype(jnp.float32)
-            + got_last.astype(jnp.float32)
-        )
-    return low(jnp.concatenate(done))
 
 
 def sums_of_halves(x):
@@ -624,10 +586,10 @@
     )
 
 
-def forward_row(hidden_own, weights, scales, places):
+def forward_row(hiddens, weights, scales, places):
     w_qkv, w_out, w_up, w_gate, w_down = weights
     scale_qk, scale_up, scale_gate, alpha_attn, alpha_mlp = scales
-    hidden_oth = swap(hidden_own)
+    hidden_own, hidden_oth = hiddens
     mixed_own = low(dot(hidden_own, w_qkv))
     mixed_oth = low(dot(hidden_oth, w_qkv))
     attended_own, attended_oth = attention(mixed_own, mixed_oth, scale_qk, places)
@@ -653,7 +615,7 @@
     second_sum = middle + alpha_mlp * (unit(output) - middle)
     result = low(unit(second_sum))
     kept = (
-        (hidden_own, hidden_oth), (mixed_own, mixed_oth), (attended_own, attended_oth),
+        hiddens, (mixed_own, mixed_oth), (attended_own, attended_oth),
         (middle_own, middle_oth), (lifted_own, lifted_oth), branch, output,
     )
     return result, kept
@@ -735,51 +697,540 @@
     )
 
 
-def to_rows_of_planes(sent, s):
-    return lax.all_to_all(sent, "seq", 0, 0)
+MESH = pl.DeviceIdType.MESH
+
+
+def position():
+    c, s, f = (lax.axis_index(name) for name in ("section", "seq", "fsdp"))
+    x, y = f % 2, f // 2
+    layer = 1 - ((s + 1) // 2) % 2
+    return c, s, f, y * 2 + 1 - x, (1 - y) * 2 + x, layer
+
+
+def greet(devices):
+    barrier = pltpu.get_barrier_semaphore()
+    for device in devices:
+        pl.semaphore_signal(barrier, inc=1, device_id=device, device_id_type=MESH)
+    pl.semaphore_wait(barrier, len(devices))
+
+
+def remote(src, dst, send, recv, device):
+    return pltpu.make_async_remote_copy(
+        src_ref=src, dst_ref=dst, send_sem=send, recv_sem=recv, device_id=device, device_id_type=MESH
+    )
+
+
+def arrived(ref, sem):
+    pltpu.make_async_copy(ref, ref, sem).wait()
+
+
+def lane(offset):
+    return pl.multiple_of(offset, 128)
+
+
+def gather_kernel(
+    w_qkv, w_out, w_in, w_down, vectors, valid, tokens, cotangent,
+    o_qkv, o_out, o_up, o_gate, o_down, o_vectors, o_valid, row_own, row_oth,
+    first_send, first_recv, next_send, next_recv, row_send, row_recv, valid_send, valid_recv,
+    swap_send, swap_recv,
+):
+    c, s, f, fx, fy, layer = position()
+    greet(
+        [(1 - c, s, f), (c, s, fx), (1 - c, s, fx), (c, s, fy), (1 - c, s, fy)]
+        + [(c, (s + step) % 4, f) for step in (1, 2, 3)]
+    )
+
+    for to, held in enumerate((cotangent.at[0], tokens.at[0], tokens.at[1], cotangent.at[1])):
+        src = held.at[pl.ds(c * BLOCK, BLOCK)]
+        dst = row_own.at[pl.ds(s * BLOCK, BLOCK)]
+        flags, flags_to = valid.at[to // 2], o_valid.at[s]
+
+        @pl.when(s == to)
+        def _():
+            pltpu.make_async_copy(src, dst, row_recv.at[s]).start()
+            pltpu.make_async_copy(flags, flags_to, valid_recv.at[s]).start()
+
+        @pl.when(s != to)
+        def _():
+            remote(src, dst, row_send.at[to], row_recv.at[s], (c, to, f)).start()
+            remote(flags, flags_to, valid_send.at[to], valid_recv.at[s], (c, to, f)).start()
+
+    def pieces(item, h):
+        if item == 0:
+            return [(vectors, o_vectors.at[f])]
+        if item == 1:
+            return [
+                (
+                    w_qkv.at[:, pl.ds(lane(part * 256 + h * 128), 128)],
+                    o_qkv.at[pl.ds(f * 256, 256), pl.ds(part * 128, 128)],
+                )
+                for part in range(12)
+            ]
+        if item == 2:
+            return [(w_out.at[pl.ds(h * 128, 128)], o_out.at[pl.ds(f * 128, 128)])]
+        if item in (3, 4):
+            to = (o_up, o_gate)[item - 3]
+            return [
+                (
+                    w_in.at[:, pl.ds(lane((item - 3) * 4096 + part * 1024 + h * 512), 512)],
+                    to.at[pl.ds(f * 256, 256), pl.ds(part * 512, 512)],
+                )
+                for part in range(4)
+            ]
+        return [(w_down.at[pl.ds(h * 512, 512)], o_down.at[pl.ds(f * 512, 512)])]
+
+    outputs = (o_vectors, o_qkv, o_out, o_up, o_gate, o_down)
+
+    def block(item, of):
+        if item == 0:
+            return o_vectors.at[of]
+        rows = outputs[item].shape[0] // 4
+        return outputs[item].at[pl.ds(of * rows, rows)]
+
+    def part_of(item, of, part):
+        if item == 0:
+            return o_vectors.at[of, pl.ds(part * 16, 16)]
+        rows = outputs[item].shape[0] // 8
+        return outputs[item].at[pl.ds(of * 2 * rows + part * rows, rows)]
+
+    targets = (
+        ((c, s, fx), c, 1), ((c, s, fy), c, 2), ((1 - c, s, fx), 1 - c, 1),
+        ((1 - c, s, fy), 1 - c, 2), ((1 - c, s, f), 1 - c, 0),
+    )
+
+    @pl.when(c == layer)
+    def _():
+        for item in range(6):
+            for index, (device, h, came) in enumerate(targets):
+                for src, dst in pieces(item, h):
+                    remote(
+                        src, dst, first_send.at[item, index], first_recv.at[item, came], device
+                    ).start()
+            for src, dst in pieces(item, c):
+                pltpu.make_async_copy(src, dst, first_recv.at[item, 0]).start()
+
+    for came in range(4):
+        arrived(row_own.at[pl.ds(came * BLOCK, BLOCK)], row_recv.at[came])
+    swapped = remote(row_own, row_oth, swap_send, swap_recv, (1 - c, s, f))
+    swapped.start()
+
+    forwards = []
+    for item in range(6):
+        for part, (came, of, to) in enumerate(((1, fx, fy), (2, fy, fx))):
+            arrived(block(item, of), first_recv.at[item, came])
+            forward = remote(
+                part_of(item, of, part), part_of(item, of, part),
+                next_send.at[item, part], next_recv.at[item, part], (c, s, to),
+            )
+            forward.start()
+            forwards.append(forward)
+
+    across = 3 - f
+    for item in range(6):
+        arrived(block(item, f), first_recv.at[item, 0])
+        for part in range(2):
+            arrived(part_of(item, across, part), next_recv.at[item, part])
+    for forward in forwards:
+        forward.wait_send()
+    swapped.wait()
+    for came in range(4):
+        arrived(o_valid.at[came], valid_recv.at[came])
+
+        @pl.when(s != came)
+        def _():
+            arrived(row_own.at[pl.ds(came * BLOCK, BLOCK)], row_send.at[came])
+            arrived(o_valid.at[came], valid_send.at[came])
+
+    @pl.when(c == layer)
+    def _():
+        for item in range(6):
+            for index in range(len(targets)):
+                arrived(block(item, f), first_send.at[item, index])
+
+
+def gather(w_qkv, w_out, w_in, w_down, vectors, valid, tokens, cotangent):
+    width = w_out.shape[1]
+    units = w_down.shape[0] * 4
+    low_shape = lambda *shape: jax.ShapeDtypeStruct(shape, jnp.bfloat16)
+    sems = pltpu.SemaphoreType.DMA
+    return pl.pallas_call(
+        gather_kernel,
+        out_shape=[
+            low_shape(width, 3 * width // 2),
+            low_shape(width // 2, width),
+            low_shape(width, units // 2),
+            low_shape(width, units // 2),
+            low_shape(units // 2, width),
+            low_shape(4, *vectors.shape),
+            low_shape(4, *valid.shape[1:]),
+            low_shape(4 * BLOCK, width),
+            low_shape(4 * BLOCK, width),
+        ],
+        in_specs=[pl.BlockSpec(memory_space=pl.ANY)] * 8,
+        out_specs=[pl.BlockSpec(memory_space=pl.ANY)] * 9,
+        scratch_shapes=[
+            sems((6, 5)), sems((6, 3)), sems((6, 2)), sems((6, 2)), sems((4,)), sems((4,)),
+            sems((4,)), sems((4,)), sems, sems,
+        ],
+        compiler_params=pltpu.CompilerParams(collective_id=0, has_side_effects=True),
+    )(w_qkv, w_out, w_in, w_down, vectors, valid, tokens, cotangent)
+
+
+CHUNKS = 16
+
+
+BUFFERS, SEMAPHORES = 8, 18
+
+
+class Flow:
+    def __init__(self, buffers, semaphores):
+        (
+            self.near_own, self.near_far, self.far_in, self.own, self.passing,
+            self.from_left, self.from_right, self.pair_sum,
+        ) = buffers
+        (
+            self.load_own, self.load_pass, self.send_own, self.recv_own, self.send_far,
+            self.recv_far, self.send_next, self.recv_next, self.send_z, self.recv_left,
+            self.recv_right, self.recv_pair, self.send_on, self.send_back, self.send_out,
+            self.keep, self.give, self.given,
+        ) = semaphores
+        self.place_of = position()
+
+    def neighbours(self, k):
+        c, s, f, fx, fy, _ = self.place_of
+        return fx + (fy - fx) * (k % 2), fy + (fx - fy) * (k % 2)
+
+    def begin(self, k, source):
+        c, s, f, _, _, _ = self.place_of
+        near, far = self.neighbours(k)
+        to = (c, s, near)
+        remote(source(near), self.near_own.at[k], self.send_own.at[k], self.recv_own.at[k], to).start()
+        remote(
+            source(3 - f), self.near_far.at[k], self.send_far.at[k], self.recv_far.at[k], to
+        ).start()
+        pltpu.make_async_copy(source(far), self.passing.at[k], self.load_pass.at[k]).start()
+        pltpu.make_async_copy(source(f), self.own.at[k], self.load_own.at[k]).start()
+
+    def add(self, to, *refs):
+        total = refs[0][...].astype(jnp.float32)
+        for ref in refs[1:]:
+            total = total + ref[...].astype(jnp.float32)
+        to[...] = total.astype(to.dtype)
+
+    def pass_on(self, k):
+        c, s, f, _, _, _ = self.place_of
+        _, far = self.neighbours(k)
+        arrived(self.passing.at[k], self.load_pass.at[k])
+        arrived(self.near_far.at[k], self.recv_far.at[k])
+        self.add(self.passing.at[k], self.passing.at[k], self.near_far.at[k])
+        remote(
+            self.passing.at[k], self.far_in.at[k], self.send_next.at[k], self.recv_next.at[k],
+            (c, s, far),
+        ).start()
+
+    def finish_plane(self, k):
+        c, s, f, _, _, _ = self.place_of
+        own = self.own.at[k]
+        arrived(own, self.load_own.at[k])
+        arrived(self.near_own.at[k], self.recv_own.at[k])
+        arrived(self.far_in.at[k], self.recv_next.at[k])
+        self.add(own, own, self.near_own.at[k], self.far_in.at[k])
+        send = self.send_z.at[k]
+
+        @pl.when(s == 0)
+        def _():
+            remote(own, self.from_left.at[k], send, self.recv_left.at[k], (c, 1, f)).start()
+
+        @pl.when(s == 3)
+        def _():
+            remote(own, self.from_right.at[k], send, self.recv_right.at[k], (c, 2, f)).start()
+
+        @pl.when((s == 1) | (s == 2))
+        def _():
+            remote(own, self.pair_sum.at[k], send, self.recv_pair.at[k], (c, 3 - s, f)).start()
+
+    def middle_planes(self, k):
+        c, s, f, _, _, _ = self.place_of
+        left, right, pair = self.from_left.at[k], self.from_right.at[k], self.pair_sum.at[k]
+
+        @pl.when(s == 1)
+        def _():
+            arrived(left, self.recv_left.at[k])
+            remote(left, left, self.send_on.at[k], self.recv_left.at[k], (c, 2, f)).start()
+
+        @pl.when(s == 2)
+        def _():
+            arrived(right, self.recv_right.at[k])
+            remote(right, right, self.send_on.at[k], self.recv_right.at[k], (c, 1, f)).start()
+
+        @pl.when((s == 1) | (s == 2))
+        def _():
+            arrived(pair, self.recv_pair.at[k])
+            arrived(pair, self.send_z.at[k])
+            self.add(pair, pair, self.own.at[k])
+            to = (c, (s - 1) * 3, f)
+            remote(pair, pair, self.send_out.at[k], self.recv_pair.at[k], to).start()
+
+    def all_planes(self, k):
+        c, s, f, _, _, _ = self.place_of
+        left, right, pair = self.from_left.at[k], self.from_right.at[k], self.pair_sum.at[k]
+        own, total = self.own.at[k], self.near_own.at[k]
+
+        @pl.when(s == 1)
+        def _():
+            arrived(right, self.recv_right.at[k])
+            remote(right, right, self.send_back.at[k], self.recv_right.at[k], (c, 0, f)).start()
+
+        @pl.when(s == 2)
+        def _():
+            arrived(left, self.recv_left.at[k])
+            remote(left, left, self.send_back.at[k], self.recv_left.at[k], (c, 3, f)).start()
+
+        @pl.when((s == 1) | (s == 2))
+        def _():
+            self.add(total, left, right)
+
+        @pl.when(s == 0)
+        def _():
+            arrived(pair, self.recv_pair.at[k])
+            arrived(right, self.recv_right.at[k])
+            self.add(total, own, right)
+
+        @pl.when(s == 3)
+        def _():
+            arrived(pair, self.recv_pair.at[k])
+            arrived(left, self.recv_left.at[k])
+            self.add(total, own, left)
+
+    def place(self, k, pieces):
+        c, s, f, _, _, _ = self.place_of
+        for owner, chunk in ((0, self.pair_sum.at[k]), (1, self.near_own.at[k])):
+            for src, dst in pieces:
+
+                @pl.when(c == owner)
+                def _():
+                    pltpu.make_async_copy(src(chunk), dst, self.keep.at[k]).start()
+
+                @pl.when(c != owner)
+                def _():
+                    remote(
+                        src(chunk), dst, self.give.at[k], self.given.at[k], (1 - c, s, f)
+                    ).start()
+
+    def settle(self, k):
+        c, s, f, _, _, _ = self.place_of
+        chunk = self.own.at[k]
+        for sem in (
+            self.send_own, self.send_far, self.send_next, self.keep, self.give, self.given
+        ):
+            arrived(chunk, sem.at[k])
+
+        @pl.when((s == 1) | (s == 2))
+        def _():
+            for sem in (self.send_on, self.send_back, self.send_out):
+                arrived(chunk, sem.at[k])
+
+        @pl.when((s == 0) | (s == 3))
+        def _():
+            arrived(chunk, self.send_z.at[k])
+
+
+def reduce_kernel(
+    g_down, g_up, g_gate, g_out, g_qkv, g_vectors, hidden, grad,
+    o_down, o_in, o_out, o_qkv, o_vectors, o_hidden, o_grad,
+    *scratch,
+):
+    c, s, f, fx, fy, layer = position()
+    greet(
+        [(c, s, fx), (c, s, fy), (1 - c, s, f)]
+        + [(core, (s + step) % 4, f) for core in (0, 1) for step in (1, 2, 3)]
+    )
+    rows_send, rows_recv = scratch[-2:]
+
+    for array, (held, to_ref) in enumerate(((hidden, o_hidden), (grad, o_grad))):
+        for to in range(4):
+            src = held.at[pl.ds(to * BLOCK, BLOCK)]
+            dst = to_ref.at[s // 2, pl.ds(c * BLOCK, BLOCK)]
+            recv = rows_recv.at[array, s // 2, c]
+            here = (s == to) & (c == layer)
+
+            @pl.when(here)
+            def _():
+                pltpu.make_async_copy(src, dst, recv).start()
+
+            @pl.when(jnp.logical_not(here))
+            def _():
+                remote(src, dst, rows_send.at[array, to], recv, (layer, to, f)).start()
+
+    matrices = Flow(scratch[:BUFFERS], scratch[BUFFERS : BUFFERS + SEMAPHORES])
+    rest = scratch[BUFFERS + SEMAPHORES : -2]
+    vectors = Flow(rest[:BUFFERS], rest[BUFFERS:])
+
+    def start_first(k):
+        @pl.when(k < 4)
+        def _():
+            matrices.begin(
+                k,
+                lambda to: g_down.at[
+                    pl.ds(to * 512 + (k // 2) * 256, 256), pl.ds(lane((k % 2) * 512), 512)
+                ],
+            )
+
+        for first, ref in ((4, g_up), (8, g_gate), (12, g_out), (13, g_qkv)):
+            count = ref.shape[1] // 512
+
+            @pl.when((k >= first) & (k < first + count))
+            def _():
+                matrices.begin(
+                    k,
+                    lambda to: ref.at[pl.ds(to * 256, 256), pl.ds(lane((k - first) * 512), 512)],
+                )
+
+    def everything(chunk):
+        return chunk
+
+    def place(k):
+        @pl.when(k < 4)
+        def _():
+            rows = pl.ds(c * 512 + (k // 2) * 256, 256)
+            matrices.place(k, [(everything, o_down.at[rows, pl.ds(lane((k % 2) * 512), 512)])])
+
+        @pl.when((k >= 4) & (k < 12))
+        def _():
+            lanes = pl.ds(lane((k - 4) * 1024 + c * 512), 512)
+            matrices.place(k, [(everything, o_in.at[:, lanes])])
+
+        @pl.when(k == 12)
+        def _():
+            matrices.place(
+                k,
+                [
+                    (
+                        lambda chunk, part=part: chunk.at[pl.ds(part * 128, 128)],
+                        o_out.at[pl.ds(c * 128, 128), pl.ds(part * 512, 512)],
+                    )
+                    for part in range(2)
+                ],
+            )
+
+        @pl.when(k > 12)
+        def _():
+            matrices.place(
+                k,
+                [
+                    (
+                        lambda chunk, part=part: chunk.at[:, pl.ds(part * 128, 128)],
+                        o_qkv.at[:, pl.ds(lane((k - 13) * 1024 + part * 256 + c * 128), 128)],
+                    )
+                    for part in range(4)
+                ],
+            )
+
+    vectors.begin(0, lambda to: g_vectors.at[to])
+    ahead, lag_plane, lag_middle, lag_all = 3, 2, 4, 7
+    for k in range(ahead):
+        start_first(k)
+
+    def last(k):
+        matrices.all_planes(k)
+        place(k)
+
+    def last_vectors(k):
+        vectors.all_planes(k)
+        vectors.place(k, [(everything, o_vectors.at[c])])
+
+    def step(t, carry):
+        @pl.when(t + ahead < CHUNKS)
+        def _():
+            start_first(t + ahead)
+
+        for lag, work, work_vectors in (
+            (0, matrices.pass_on, vectors.pass_on),
+            (lag_plane, matrices.finish_plane, vectors.finish_plane),
+            (lag_middle, matrices.middle_planes, vectors.middle_planes),
+            (lag_all, last, last_vectors),
+        ):
+            @pl.when(t == lag)
+            def _():
+                work_vectors(0)
+
+            @pl.when((t >= lag) & (t < CHUNKS + lag))
+            def _():
+                work(t - lag)
+
+        return carry
+
+    lax.fori_loop(0, CHUNKS + lag_all, step, 0)
+
+    def settle(k, carry):
+        matrices.settle(k)
+        return carry
+
+    lax.fori_loop(0, CHUNKS, settle, 0)
+    vectors.settle(0)
+    for array, (held, to_ref) in enumerate(((hidden, o_hidden), (grad, o_grad))):
+        for to in range(4):
+            @pl.when(jnp.logical_not((s == to) & (c == layer)))
+            def _():
+                arrived(held.at[pl.ds(to * BLOCK, BLOCK)], rows_send.at[array, to])
+
+        for micro in range(2):
+            for core in range(2):
+                arrived(
+                    to_ref.at[micro, pl.ds(core * BLOCK, BLOCK)], rows_recv.at[array, micro, core]
+                )
+
+
+def reduce_all(g_down, g_up, g_gate, g_out, g_qkv, g_vectors, hidden, grad):
+    width = g_down.shape[1]
+    low_shape = lambda *shape: jax.ShapeDtypeStruct(shape, jnp.bfloat16)
+    sems = pltpu.SemaphoreType.DMA
+    small = g_vectors.shape[1:]
+    return pl.pallas_call(
+        reduce_kernel,
+        out_shape=[
+            low_shape(g_down.shape[0] // 2, width),
+            low_shape(g_up.shape[0] // 4, 4 * g_up.shape[1]),
+            low_shape(width // 4, width),
+            low_shape(width // 4, 2 * g_qkv.shape[1]),
+            jax.ShapeDtypeStruct((2, *small), jnp.float32),
+            low_shape(2, 2 * BLOCK, width),
+            low_shape(2, 2 * BLOCK, width),
+        ],
+        in_specs=[pl.BlockSpec(memory_space=pl.ANY)] * 8,
+        out_specs=[pl.BlockSpec(memory_space=pl.ANY)] * 7,
+        scratch_shapes=[pltpu.VMEM((CHUNKS, 256, 512), jnp.bfloat16)] * BUFFERS
+        + [sems((CHUNKS,))] * SEMAPHORES
+        + [pltpu.VMEM((1, *small), jnp.float32)] * BUFFERS
+        + [sems((1,))] * SEMAPHORES
+        + [sems((2, 4)), sems((2, 2, 2))],
+        compiler_params=pltpu.CompilerParams(
+            collective_id=1, has_side_effects=True, vmem_limit_bytes=48 * 2**20
+        ),
+    )(g_down, g_up, g_gate, g_out, g_qkv, g_vectors, hidden, grad)
 
 
 def per_device(
     tokens, cotangent, lengths, valid_mask, w_qkv, w_out, w_in, w_down, qk_scale, mlp_scale, alphas
 ):
-    c = lax.axis_index("section")
-    s = lax.axis_index("seq")
-    f = lax.axis_index("fsdp")
-    second = (s == 0) | (s == 3)
-    layer = second.astype(jnp.int32)
+    c, s, f, _, _, layer = position()
+    second = layer == 1
     micro = s // 2
     width = tokens.shape[3]
     group = tokens.shape[2]
     units = w_down.shape[1] * 4
 
-    sources = jnp.stack([cotangent[0, 0], tokens[0, 0], tokens[1, 0], cotangent[1, 0]])
-    sent = pick(sources.reshape(4, 2, BLOCK, width), c, 1)
-    row = to_rows_of_planes(sent, s).reshape(4 * BLOCK, width)
-
-    def mine(shard, axis):
-        own = pick(shard, c, axis)
-        got = swap(pick(shard, 1 - c, axis))
-        return jnp.where(layer == c, own, got)
-
-    half_qkv = mine(w_qkv[0].reshape(-1, 3, 4, 2, 2 * HEAD), 3).reshape(-1, 3 * width // 2)
-    half_out = mine(w_out[0].reshape(2, -1, width), 0)
-    half_in = mine(w_in[0].reshape(-1, 2, 4, 2, units // 8), 3).reshape(-1, 2, units // 2)
-    half_down = mine(w_down[0].reshape(2, -1, width), 0)
-    weights = (
-        gather_rows(half_qkv, f),
-        gather_rows(half_out, f),
-        gather_rows(half_in[:, 0], f),
-        gather_rows(half_in[:, 1], f),
-        gather_rows(half_down, f),
-    )
-
-    vectors = jnp.concatenate([qk_scale, mlp_scale, alphas], axis=1)
-    vectors = lax.all_gather(vectors, ("section", "fsdp"), axis=0, tiled=True)
-    vectors = pick(vectors.reshape(2, 4, -1), layer, 0).astype(jnp.float32)
+    vectors = jnp.concatenate([qk_scale[0], mlp_scale[0], alphas[0]])
+    vectors = jnp.pad(vectors, (0, 32 * 128 - vectors.shape[0])).reshape(32, 128)
+    valid = low(jnp.pad(valid_mask[:, 0], ((0, 0), (0, 16 * 128 - group)))).reshape(2, 16, 128)
+    *weights, vectors, valid, row, row_oth = gather(
+        w_qkv[0], w_out[0], w_in[0], w_down[0], vectors, valid, tokens[:, 0], cotangent[:, 0]
+    )
+    vectors = vectors.reshape(4, -1).astype(jnp.float32)
     cut_qk, cut_mlp = qk_scale.shape[1], qk_scale.shape[1] + mlp_scale.shape[1]
     all_qk = vectors[:, :cut_qk].reshape(4, 2, -1)
     all_mlp = vectors[:, cut_qk:cut_mlp].reshape(2, 4, 2, -1)
-    all_alphas = vectors[:, cut_mlp:].reshape(2, 1, -1)
+    all_alphas = vectors[:, cut_mlp : cut_mlp + alphas.shape[1]].reshape(2, 1, -1)
     mlp_half = pick(all_mlp, c, 2).reshape(2, 1, -1)
     scales = (
         pick(all_qk, c, 1).reshape(1, -1),
@@ -795,89 +1246,51 @@
     passed = place[:, None] >= ends[None, :]
     start = jnp.max(jnp.where(passed, ends[None, :], 0), axis=1)
     places = (place, start)
-
-    valid = lax.all_gather(low(valid_mask[:, 0]), "seq", axis=0)
-    valid = pick(pick(valid, micro, 1).reshape(4, 2, BLOCK), c, 1).reshape(-1).astype(jnp.float32)
-
-    result, _ = forward_row(row, weights, scales, places)
-    arrived = along(result, [(1, 0), (2, 3)])
-    hidden_own = jnp.where(second, arrived, row)
-    result, kept = forward_row(hidden_own, weights, scales, places)
+    valid = pick(valid[:, :2], c, 1).reshape(-1).astype(jnp.float32)
+
+    result, _ = forward_row((row, row_oth), weights, scales, places)
+    arrived_row = along(result, [(1, 0), (2, 3)])
+    hidden_own = jnp.where(second, arrived_row, row)
+    result, kept = forward_row((hidden_own, swap(hidden_own)), weights, scales, places)
     branch = kept[5]
     statistic = jnp.sum(valid * jnp.sum(branch * branch, axis=-1))
 
     grad_row = row.astype(jnp.float32)
-    grad_hidden, operands, small_second = backward_row(grad_row, kept, weights, scales, places)
-    arrived = along(grad_hidden, [(0, 1), (3, 2)])
-    grads_second = weight_grads(operands)
-    grad_row = jnp.where(second, grad_row, arrived.astype(jnp.float32))
-    grad_hidden, operands, small_first = backward_row(grad_row, kept, weights, scales, places)
-    grads_first = weight_grads(operands)
-
-    reduced = []
-    for from_second, from_first in zip(grads_second, grads_first):
-        part = scatter_rows(from_second, f, SECOND)
-        near = along(part, [(0, 1), (3, 2)])
-        both = jnp.where(second, part, near)
-        across = along(both, [(1, 2), (2, 1)])
-        far = along(jnp.where(second, part, across), [(1, 0), (2, 3)])
-        layer_1 = jnp.where(second, part, near).astype(jnp.float32) + jnp.where(
-            second, far, across
-        ).astype(jnp.float32)
-        part = scatter_rows(from_first, f, FIRST)
-        across = along(part, [(1, 2), (2, 1)])
-        total = low(part.astype(jnp.float32) + across.astype(jnp.float32))
-        outward = along(total, [(1, 0), (2, 3)])
-        layer_0 = jnp.where(second, outward, total)
-        layer_1 = low(layer_1)
-        own = jnp.where(c == 0, layer_0, layer_1)
-        got = swap(jnp.where(c == 0, layer_1, layer_0))
-        reduced.append((jnp.where(c == 0, own, got), jnp.where(c == 0, got, own)))
-
-    def columns(halves, groups):
-        parts = [half.reshape(half.shape[0], groups, -1) for half in halves]
-        return jnp.stack(parts, axis=2).reshape(parts[0].shape[0], -1)
-
-    grad_qkv = columns(reduced[0], 12)
-    grad_out = jnp.concatenate(reduced[1])
-    grad_in_proj = jnp.concatenate([columns(reduced[2], 4), columns(reduced[3], 4)], axis=1)
-    grad_down = jnp.concatenate(reduced[4])
-
-    def to_owners(block):
-        got = to_rows_of_planes(block.reshape(4, BLOCK, width), s)
-        layers = (jnp.stack([got[1], got[2]]), jnp.stack([got[0], got[3]]))
-        own = jnp.where(c == 0, layers[0], layers[1])
-        other = swap(jnp.where(c == 0, layers[1], layers[0]))
-        halves = (jnp.where(c == 0, own, other), jnp.where(c == 0, other, own))
-        return jnp.concatenate(halves, axis=1)[None, :, None]
-
-    hidden_out = to_owners(result)
-    grad_in = to_owners(grad_hidden).astype(jnp.float32)
-
-    small = [jnp.where(second, late, early) for late, early in zip(small_second, small_first)]
+    grad_hidden, _, _ = backward_row(grad_row, kept, weights, scales, places)
+    arrived_row = along(grad_hidden, [(0, 1), (3, 2)])
+    grad_row = jnp.where(second, grad_row, arrived_row.astype(jnp.float32))
+    grad_hidden, operands, small = backward_row(grad_row, kept, weights, scales, places)
+    g_qkv, g_out, g_up, g_gate, g_down = weight_grads(operands)
+    g_out = g_out.reshape(4, BLOCK, 2, -1).transpose(0, 2, 1, 3).reshape(4 * 2 * BLOCK, -1)
+
+    at_half = jnp.arange(2).reshape(1, 1, 2, 1) == c
     up_gate = jnp.stack([small[1], small[2]]).reshape(2, 4, 1, -1)
-    at_half = jnp.arange(2).reshape(1, 1, 2, 1) == c
-    full = jnp.concatenate(
+    g_vectors = jnp.concatenate(
         [
-            small[0],
-            jnp.where(at_half, up_gate, 0.0).reshape(-1),
-            jnp.where(at_half, small[3].reshape(1, 4, 1, -1), 0.0).reshape(-1),
-            statistic[None],
-        ]
-    )
-    full = jnp.where(jnp.arange(2)[:, None] == layer, full[None], 0.0)
-    full = pick(lax.psum(full, ("section", "seq", "fsdp")), c, 0)
-    ends = (2 * width, 2 * width + 2 * units, 3 * width + 2 * units)
-    grad_alphas = pick(full[: ends[0]].reshape(4, -1), f, 0)[None]
-    grad_mlp_scale = pick(full[ends[0] : ends[1]].reshape(4, -1), f, 0)[None]
-    grad_qk_scale = pick(full[ends[1] : ends[2]].reshape(4, -1), f, 0)[None]
+            jnp.where(at_half[0], small[3].reshape(4, 1, -1), 0.0).reshape(4, -1),
+            jnp.where(at_half, up_gate, 0.0).reshape(4, -1),
+            small[0].reshape(4, -1),
+            jnp.full((4, 1), statistic),
+        ],
+        axis=1,
+    )
+    g_vectors = jnp.pad(g_vectors, ((0, 0), (0, 24 * 128 - g_vectors.shape[1]))).reshape(4, 24, 128)
+    grad_down, grad_in_proj, grad_out, grad_qkv, vectors, hidden_out, grad_in = reduce_all(
+        g_down, g_up, g_gate, g_out, g_qkv, g_vectors, result, grad_hidden
+    )
+    full = jnp.sum(vectors, axis=0).reshape(-1)
+    cuts = (cut_qk, cut_mlp, cut_mlp + alphas.shape[1])
+    grad_qk_scale = full[: cuts[0]][None]
+    grad_mlp_scale = full[cuts[0] : cuts[1]][None]
+    grad_alphas = full[cuts[1] : cuts[2]][None]
     token_count = tokens.shape[0] * lax.axis_size("fsdp") * 4 * group
-    rms_stats = jnp.sqrt(full[ends[2] :] / token_count + epsilon)
+    rms_stats = jnp.sqrt(full[cuts[2] : cuts[2] + 1] / token_count + epsilon)
     as_float = [
         part.astype(jnp.float32)[None] for part in (grad_qkv, grad_out, grad_in_proj, grad_down)
     ]
     return (
-        hidden_out, grad_in, *as_float, grad_qk_scale, grad_mlp_scale, grad_alphas, rms_stats,
+        hidden_out[None, :, None], grad_in.astype(jnp.float32)[None, :, None], *as_float,
+        grad_qk_scale, grad_mlp_scale, grad_alphas, rms_stats,
     )
 
 

time: 1420 us -> 791 us (0.56)
  Pallas kernels: 80.8 us -> 459 us
  waiting for transfers between devices: 416 us -> 60.7 us
  starting transfers between devices: 326 us -> 20.3 us
  local copies, waits for them, and re-layouts: 180 us -> 24 us
  other arithmetic: 151 us -> 41.2 us
  blocking collectives: 35.9 us -> 0 us
  matrix products: 204 us -> 175 us
  between operations: 20.2 us -> 3.91 us
    pallas_call x0 -> x2, Pallas kernels: none -> 377 us  [the longest x1 248 us: reduce_all(): pl.pallas_call(reduce_kernel, out_shape=[low_shape(g_down.shape[0] // 2,...]
    ppermute x80 -> x0, starting transfers between devices: 150 us -> none  [hop(): return lax.ppermute(x, ('seq', 'fsdp'), route)]
    ppermute x27 -> x2, waiting for transfers between devices: 187 us -> 49 us  [along(): return lax.ppermute(x, 'seq', route)]
    ppermute x80 -> x0, waiting for transfers between devices: 131 us -> none  [hop(): return lax.ppermute(x, ('seq', 'fsdp'), route)]
    ppermute x27 -> x2, starting transfers between devices: 123 us -> 2.65 us  [along(): return lax.ppermute(x, 'seq', route)]
    psum x1 -> x0, waiting for transfers between devices: 92.8 us -> none  [per_device(): full = pick(lax.psum(full, ('section', 'seq', 'fsdp')), c, 0)]
    all_to_all x3 -> x0, starting transfers between devices: 48.4 us -> none  [to_rows_of_planes(): return lax.all_to_all(sent, 'seq', 0, 0)]
    all_gather x2 -> x0, blocking collectives: 35.9 us -> none  [the longest x1 24 us: per_device(): vectors = lax.all_gather(vectors, ('section', 'fsdp'), axis=0, tiled=True)]
  transfers between devices with their start and end apart: 138 -> 17, of which waited for: 34 -> 8; matrix products, arithmetic and copies ran while one was open for 29% -> 8% of each run, Pallas kernels for 5% -> 0%
where the time goes in v2:
time: 791 us; the launch traced here: 784 us
  Pallas kernels  459 us (58%)
  matrix products  175 us (22%)
  waiting for transfers between devices  60.7 us (8%)
  other arithmetic  41.2 us (5%)
  local copies, waits for them, and re-layouts  24 us (3%)
  starting transfers between devices  20.3 us (3%)
    pallas_call x1, Pallas kernels, reduce_all(): pl.pallas_call(reduce_kernel, out_shape=[low_shape(g_down.shape[0] // 2,...  248 us
    pallas_call x1, Pallas kernels, gather(): pl.pallas_call(gather_kernel, out_shape=[low_shape(width, 3 * width // 2)...  130 us
    dot_general x20, matrix products, contract_cols(): lax.dot_general(left, right, (((1,), (1,)), ((), ())), preferred_element_...  79.6 us
    dot_general x18, matrix products, dot(): return jnp.dot(left, right, preferred_element_type=jnp.float32)  65.2 us
    pallas_call x2, Pallas kernels, attention_back(): pl.pallas_call(attention_back_kernel, grid=(pairs,), out_shape=[jax.Shape...  59.5 us
    ppermute x2, waiting for transfers between devices, along(): return lax.ppermute(x, 'seq', route)  49 us
    dot_general x5, matrix products, contract_rows(): lax.dot_general(left, right, (((0,), (0,)), ((), ())), preferred_element_...  30.6 us
    pallas_call x2, Pallas kernels, attention(): pl.pallas_call(attention_kernel, grid=(pairs,), out_shape=[jax.ShapeDtype...  22.2 us
  transfers between devices with their start and end apart: 17, of which 8 were waited for; matrix products, arithmetic and copies ran while one was open for 8% of the time, Pallas kernels for 0%

profile of v2, /device:TPU:0, one launch (start us, length us, event | category | flops | bytes accessed | tf_op | source)
XLA Modules:
  0.0 784.4 jit_solution(6162617720898130323)
XLA Ops:
  5.9 129.8 %shard_map.186 = (bf16[1024,1536]{1,0:T(8,128)(2,1)}, bf16[512,1024]{1,0:T(8,128)(2,1)}, bf16[1024,2048]{1,0:T(8,128)(2,1)}, bf16[1024,2048]{1,0:T(8,128)(2,1)},...) custom-call(bf16[256,3072]{1,0:T(8,128)(2,1)} %bitcast.169, ...), custom_call_target="tpu_custom_call" | custom-call | tf_op jit(solution)/shard_map/pallas_call | solution.py:856
  136.5 5.3 convolution_convert_fusion.7.q_oth.k_oth.v_oth
  147.6 11.0 %shard_map.187 = (bf16[512,512]{1,0:T(8,128)(2,1)S(1)}, bf16[512,512]{1,0:T(8,128)(2,1)S(1)}) custom-call(bf16[512,1536]{1,0:T(8,128)(2,1)S(1)} %copy-done.12, bf16[512,1536]{1,0:T(8,128)(2,1)S(1)} %copy-done.12, bf16[512,1536]{1,0:T(8,128)(2,1)S(1)} %copy-done.12, bf16[512,1536]{1,0:T(8,128)(2,1)S(1)} %copy-done.11, bf16[512,1536]{1,0:T(8,128)(2,1)S(1)} %copy-done.11, ...), custom_call_target="tpu_custom_call" | custom-call | flops 4294967296 | bytes 4194304 | tf_op jit(solution)/shard_map/pallas_call | solution.py:530
  159.3 13.4 %collective-permute-start = (bf16[512,1024]{1,0:T(8,128)(2,1)S(1)}, bf16[512,1024]{1,0:T(8,128)(2,1)S(1)}, u32[]{:S(2)}, u32[]{:S(2)}) collective-permute-start(bf16[512,1024]{1,0:T(8,128)(2,1)S(1)} %convolution_convert_fusion.12), channel_id=1, source_target_pairs={{0,16},{16,0},{1,17},{17,1},{2,18},{18,2},{3,19},{19,3},{4,20},{20... | collective-permute-start | bytes 3145736 | tf_op jit(solution)/shard_map/ppermute | solution.py:384
  182.7 6.2 convolution_convert_fusion.3
  188.9 10.1 %fusion.95 = bf16[512,1024]{1,0:T(8,128)(2,1)} fusion(bf16[2048,1024]{1,0:T(8,128)(2,1)} %get-tuple-element.44, bf16[512,2048]{1,0:T(8,128)(2,1)} %convolution_convert_fusion.3, bf16[512,1024]{1,0:T(8,128)(2,1)} %collective-permute-done.1, bf16[1024,2048]{1,0:T(8,128)(2,1)} %get-tuple-element.43, f32[2048]{0:T(1024)S(1)} %bitcast.193, f32[2048]{0:T(1024)S(1)} %bitcast.205), kind=kOutput, calls=%fused_computation.163 | convolution fusion | flops 4304928768 | bytes 12599296 | tf_op jit(solution)/shard_map/dot_general | solution.py:376
  199.4 5.8 convolution_convert_fusion.4
  205.2 10.7 %multiply_reduce_fusion.14 = (f32[512]{0:T(512)S(1)}, f32[512,1024]{1,0:T(8,128)}) fusion(bf16[512,1024]{1,0:T(8,128)(2,1)} %collective-permute-done.2, bf16[2048,1024]{1,0:T(8,128)(2,1)} %get-tuple-element.44, bf16[512,2048]{1,0:T(8,128)(2,1)} %convolution_convert_fusion.4, bf16[512,1024]{1,0:T(8,128)(2,1)S(1)} %multiply_convert_fusion.15, ...), kind=kOutput, calls=%fused_computation.142 | convolution fusion | flops 4306501120 | bytes 14698496 | tf_op jit(solution)/shard_map/dot_general | solution.py:376
  222.5 25.8 %collective-permute-done.3 = bf16[512,1024]{1,0:T(8,128)(2,1)} collective-permute-done((bf16[512,1024]{1,0:T(8,128)(2,1)S(1)}, bf16[512,1024]{1,0:T(8,128)(2,1)}, u32[]{:S(2)}, u32[]{:S(2)}) %collective-permute-start.3) | collective-permute-done | bytes 1048608 | tf_op jit(solution)/shard_map/ppermute | solution.py:388
  255.2 11.2 %shard_map.188 = (bf16[512,512]{1,0:T(8,128)(2,1)S(1)}, bf16[512,512]{1,0:T(8,128)(2,1)S(1)}) custom-call(bf16[512,1536]{1,0:T(8,128)(2,1)S(1)} %convolution_convert_fusion.6.q_own.k_own.v_own, bf16[512,1536]{1,0:T(8,128)(2,1)S(1)} %convolution_convert_fusion.6.q_own.k_own.v_own, bf16[512,1536]{1,0:T(8,128)(2,1)S(1)} %convolution_convert_fusion.6.q_own.k_own.v_own, ...), custom_call_target="tpu_custom_call" | custom-call | flops 4294967296 | bytes 4194304 | tf_op jit(solution)/shard_map/pallas_call | solution.py:530
  280.6 4.5 fusion.159
  287.7 3.4 fusion.158
  297.1 4.4 fusion.160
  301.4 4.4 fusion.161
  305.8 8.2 %fusion.69 = f32[512,1024]{1,0:T(8,128)} fusion(bf16[1024,2048]{1,0:T(8,128)(2,1)S(1)} %copy-done.36, f32[512,2048]{1,0:T(8,128)} %fusion.161, bf16[512,2048]{1,0:T(8,128)(2,1)S(1)} %convolution_convert_fusion.1, bf16[512,2048]{1,0:T(8,128)(2,1)} %get-tuple-element.120, f32[2048]{0:T(1024)S(1)} %bitcast.197, f32[2048]{0:T(1024)S(1)} %bitcast.209), kind=kOutput, calls=%fused_computation.96 | convolution fusion | flops 2163212288 | bytes 14696448 | tf_op jit(solution)/shard_map/dot_general | solution.py:43
  314.0 6.2 add_convert_fusion.3
  320.5 5.8 fusion.71
  326.3 5.8 multiply_reduce_fusion.7
  336.9 29.7 %shard_map.189 = (bf16[512,1536]{1,0:T(8,128)(2,1)S(1)}, bf16[512,1536]{1,0:T(8,128)(2,1)S(1)}, f32[1,512]{1,0:T(1,128)}) custom-call(bf16[512,1536]{1,0:T(8,128)(2,1)} %copy-done.9, bf16[512,1536]{1,0:T(8,128)(2,1)} %copy-done.9, bf16[512,1536]{1,0:T(8,128)(2,1)} %copy-done.9, bf16[512,1536]{1,0:T(8,128)(2,1)} %copy-done.10, bf16[512,1536]{1,0:T(8,128)(2,1)} %copy-done.10, ...), custom_call_target="tpu_custom_call" | custom-call | flops 10737418240 | bytes 8388608 | tf_op jit(solution)/shard_map/pallas_call | solution.py:566
  366.7 3.9 convolution_convert_fusion.10
  376.5 23.1 %collective-permute-done.12 = bf16[512,1024]{1,0:T(8,128)(2,1)S(1)} collective-permute-done((bf16[512,1024]{1,0:T(8,128)(2,1)S(1)}, bf16[512,1024]{1,0:T(8,128)(2,1)S(1)}, u32[]{:S(2)}, u32[]{:S(2)}) %collective-permute-start.12) | collective-permute-done | bytes 1048608 | tf_op jit(solution)/shard_map/ppermute | solution.py:388
  405.3 4.7 fusion.162
  411.2 12.0 %fusion.27 = (f32[2048]{0:T(1024)S(1)}, f32[2048]{0:T(1024)S(1)}, f32[2048]{0:T(1024)S(1)}, f32[2048]{0:T(1024)S(1)}, f32[512,2048]{1,0:T(8,128)}, /*index=5*/f3...) fusion(bf16[512,2048]{1,0:T(8,128)(2,1)S(1)} %copy-done.56, f32[2048]{0:T(1024)S(1)} %bitcast.201, ...), kind=kOutput, calls=%fused_computation.35 | convolution fusion | flops 2191515648 | bytes 30457856 | tf_op jit(solution)/shard_map/dot_general | solution.py:43
  423.3 5.3 fusion.163
  437.3 6.3 fusion.53.g_up
  443.6 6.4 fusion.50.g_gate
  456.4 9.1 %fusion.56.g_down = bf16[2048,1024]{1,0:T(8,128)(2,1)} fusion(bf16[512,2048]{1,0:T(8,128)(2,1)} %copy-done.58, bf16[512,2048]{1,0:T(8,128)(2,1)} %copy-done.57, bf16[512,1024]{1,0:T(8,128)(2,1)} %collective-permute-done.13, bf16[512,1024]{1,0:T(8,128)(2,1)S(1)} %multiply_convert_fusion.11), kind=kOutput, calls=%fused_computation.74 | convolution fusion | flops 4309647360 | bytes 10485760 | tf_op jit(solution)/shard_map/dot_general | solution.py:37
  467.9 3.8 fusion.96
  477.9 29.7 %shard_map.190 = (bf16[512,1536]{1,0:T(8,128)(2,1)S(1)}, bf16[512,1536]{1,0:T(8,128)(2,1)S(1)}, f32[1,512]{1,0:T(1,128)S(1)}) custom-call(bf16[512,1536]{1,0:T(8,128)(2,1)} %copy-done.9, bf16[512,1536]{1,0:T(8,128)(2,1)} %copy-done.9, bf16[512,1536]{1,0:T(8,128)(2,1)} %copy-done.9, bf16[512,1536]{1,0:T(8,128)(2,1)} %copy-done.10, ...), custom_call_target="tpu_custom_call" | custom-call | flops 10737418240 | bytes 8388608 | tf_op jit(solution)/shard_map/pallas_call | solution.py:566
  509.8 4.9 convolution_convert_fusion.g_qkv
  516.6 247.5 %shard_map.191 = (bf16[1024,1024]{1,0:T(8,128)(2,1)}, bf16[256,8192]{1,0:T(8,128)(2,1)}, bf16[256,1024]{1,0:T(8,128)(2,1)S(1)}, bf16[256,3072]{1,0:T(8,128)(2,1)...) custom-call(bf16[2048,1024]{1,0:T(8,128)(2,1)} %fusion.56.g_down, ...), custom_call_target="tpu_custom_call" | custom-call | tf_op jit(solution)/shard_map/pallas_call | solution.py:1189
  777.7 4.4 bitcast_convert_fusion
  (262 shorter events, 117.5 us)
Async XLA Ops:
  5.0 130.7 %copy-start.5 = (s32[1024]{0:T(1024)}, s32[1024]{0:T(1024)S(1)}, u32[]{:S(2)}) copy-start(s32[1024]{0:T(1024)S(1)} %select_reduce_fusion) | copy-start | bytes 12292
  147.6 11.0 %copy-start.29 = (bf16[512,1024]{1,0:T(8,128)(2,1)S(1)}, bf16[512,1024]{1,0:T(8,128)(2,1)}, u32[]{:S(2)}) copy-start(bf16[512,1024]{1,0:T(8,128)(2,1)} %get-tuple-element.40) | copy-start | bytes 3145732
  159.3 15.7 %collective-permute-start = (bf16[512,1024]{1,0:T(8,128)(2,1)S(1)}, bf16[512,1024]{1,0:T(8,128)(2,1)S(1)}, u32[]{:S(2)}, u32[]{:S(2)}) collective-permute-start(bf16[512,1024]{1,0:T(8,128)(2,1)S(1)} %convolution_convert_fusion.12), channel_id=1, source_target_pairs={{0,16},{16,0},{1,17},{17,1},{2,18},{18,2},{3,19},{19,3},{4,20},{20... | collective-permute-start | bytes 3145736 | tf_op jit(solution)/shard_map/ppermute | solution.py:384
  179.9 2.9 collective-permute-start.1
  199.0 6.2 collective-permute-start.2
  221.2 27.2 %collective-permute-start.3 = (bf16[512,1024]{1,0:T(8,128)(2,1)S(1)}, bf16[512,1024]{1,0:T(8,128)(2,1)}, u32[]{:S(2)}, u32[]{:S(2)}) collective-permute-start(bf16[512,1024]{1,0:T(8,128)(2,1)S(1)} %multiply_convert_fusion.14), channel_id=1, source_target_pairs={{4,0},{8,12},{5,1},{9,13},{6,2},{10,14},{7,3},{11,15},{20,16},{24,... | collective-permute-start | bytes 3145736 | tf_op jit(solution)/shard_map/ppermute | solution.py:388
  222.5 27.3 %copy-start.43 = (bf16[1024,1536]{1,0:T(8,128)(2,1)S(1)}, bf16[1024,1536]{1,0:T(8,128)(2,1)}, u32[]{:S(2)}) copy-start(bf16[1024,1536]{1,0:T(8,128)(2,1)} %get-tuple-element.37) | copy-start | bytes 9437188
  249.7 21.1 %copy-start.18 = (bf16[512,1024]{1,0:T(8,128)(2,1)}, bf16[512,1024]{1,0:T(8,128)(2,1)S(1)}, u32[]{:S(2)}) copy-start(bf16[512,1024]{1,0:T(8,128)(2,1)S(1)} %broadcast_select_fusion) | copy-start | bytes 3145732
  249.7 2.7 collective-permute-start.4
  255.2 11.3 %copy-start.10 = (bf16[512,1536]{1,0:T(8,128)(2,1)}, bf16[512,1536]{1,0:T(8,128)(2,1)S(1)}, u32[]{:S(2)}) copy-start(bf16[512,1536]{1,0:T(8,128)(2,1)S(1)} %convolution_convert_fusion.5.q_oth.k_oth.v_oth) | copy-start | bytes 4718596
  255.2 11.3 %copy-start.30 = (bf16[512,1024]{1,0:T(8,128)(2,1)S(1)}, bf16[512,1024]{1,0:T(8,128)(2,1)}, u32[]{:S(2)}) copy-start(bf16[512,1024]{1,0:T(8,128)(2,1)} %get-tuple-element.40) | copy-start | bytes 3145732
  267.2 2.7 collective-permute-start.5
  270.8 62.2 %copy-start.13 = (f32[512,1024]{1,0:T(8,128)}, f32[512,1024]{1,0:T(8,128)S(1)}, u32[]{:S(2)}) copy-start(f32[512,1024]{1,0:T(8,128)S(1)} %get-tuple-element.113) | copy-start | bytes 6291460
  271.6 128.6 %copy-start.15 = (f32[512,1024]{1,0:T(8,128)}, f32[512,1024]{1,0:T(8,128)S(1)}, u32[]{:S(2)}) copy-start(f32[512,1024]{1,0:T(8,128)S(1)} %get-tuple-element.111) | copy-start | bytes 6291460
  271.8 15.9 %copy-start.34 = (bf16[512,1024]{1,0:T(8,128)(2,1)}, bf16[512,1024]{1,0:T(8,128)(2,1)S(1)}, u32[]{:S(2)}) copy-start(bf16[512,1024]{1,0:T(8,128)(2,1)S(1)} %multiply_convert_fusion.19) | copy-start | bytes 3145732
  271.8 5.4 collective-permute-start.6
  277.2 43.2 %copy-start.53 = (bf16[512,2048]{1,0:T(8,128)(2,1)}, bf16[512,2048]{1,0:T(8,128)(2,1)S(1)}, u32[]{:S(2)}) copy-start(bf16[512,2048]{1,0:T(8,128)(2,1)S(1)} %convolution_convert_fusion.2) | copy-start | bytes 6291460
  280.6 25.3 %copy-start.55 = (bf16[512,2048]{1,0:T(8,128)(2,1)}, bf16[512,2048]{1,0:T(8,128)(2,1)S(1)}, u32[]{:S(2)}) copy-start(bf16[512,2048]{1,0:T(8,128)(2,1)S(1)} %convolution_convert_fusion.1) | copy-start | bytes 6291460
  287.5 3.7 collective-permute-start.7
  291.2 29.3 %copy-start.59 = (bf16[512,2048]{1,0:T(8,128)(2,1)}, bf16[512,2048]{1,0:T(8,128)(2,1)S(1)}, u32[]{:S(2)}) copy-start(bf16[512,2048]{1,0:T(8,128)(2,1)S(1)} %get-tuple-element.118) | copy-start | bytes 6291460
  296.7 4.8 collective-permute-start.8
  320.2 6.0 collective-permute-start.9
  333.4 2.7 collective-permute-start.10
  366.7 6.6 copy-start.44
  370.5 2.7 collective-permute-start.11
  375.2 24.5 %collective-permute-start.12 = (bf16[512,1024]{1,0:T(8,128)(2,1)S(1)}, bf16[512,1024]{1,0:T(8,128)(2,1)S(1)}, u32[]{:S(2)}, u32[]{:S(2)}) collective-permute-start(bf16[512,1024]{1,0:T(8,128)(2,1)S(1)} %add_convert_fusion.2), channel_id=1, source_target_pairs={{0,4},{12,8},{1,5},{13,9},{2,6},{14,10},{3,7},{15,11},{16,20},{28,... | collective-permute-start | bytes 3145736 | tf_op jit(solution)/shard_map/ppermute | solution.py:388
  403.2 6.8 collective-permute-start.13
  436.7 13.4 %collective-permute-start.14 = (bf16[512,1024]{1,0:T(8,128)(2,1)S(1)}, bf16[512,1024]{1,0:T(8,128)(2,1)S(1)}, u32[]{:S(2)}, u32[]{:S(2)}) collective-permute-start(bf16[512,1024]{1,0:T(8,128)(2,1)S(1)} %add_convert_fusion.1), channel_id=1, source_target_pairs={{0,16},{16,0},{1,17},{17,1},{2,18},{18,2},{3,19},{19,3},{4,20},{20... | collective-permute-start | bytes 3145736 | tf_op jit(solution)/shard_map/ppermute | solution.py:384
  443.6 6.5 copy-start.22
  455.9 12.0 %collective-permute-start.15 = (bf16[512,1024]{1,0:T(8,128)(2,1)}, bf16[512,1024]{1,0:T(8,128)(2,1)}, u32[]{:S(2)}, u32[]{:S(2)}) collective-permute-start(bf16[512,1024]{1,0:T(8,128)(2,1)} %multiply_convert_fusion.10), channel_id=1, source_target_pairs={{0,16},{16,0},{1,17},{17,1},{2,18},{18,2},{3,19},{19,3},{4,20},{20... | collective-permute-start | bytes 3145736 | tf_op jit(solution)/shard_map/ppermute | solution.py:384
  477.9 29.8 %copy-start.45 = (bf16[1024,1536]{1,0:T(8,128)(2,1)S(1)}, bf16[1024,1536]{1,0:T(8,128)(2,1)}, u32[]{:S(2)}) copy-start(bf16[1024,1536]{1,0:T(8,128)(2,1)} %get-tuple-element.37) | copy-start | bytes 9437188
  509.5 5.3 collective-permute-start.16
  (47 other events, 154.6 us)

commit v3 on v2

--- a/solution.py
+++ b/solution.py
@@ -380,14 +380,6 @@
     return x.astype(jnp.bfloat16)
 
 
-def swap(x):
-    return lax.ppermute(x, "section", [(0, 1), (1, 0)])
-
-
-def along(x, route):
-    return lax.ppermute(x, "seq", route)
-
-
 def pick(x, index, axis):
     return lax.dynamic_index_in_dim(x, index, axis, keepdims=False)
 
@@ -421,282 +413,6 @@
     return (lane == h).astype(dtype)
 
 
-def attention_kernel(
-    q_own, k_own, v_own, q_oth, k_oth, v_oth, scale, place_col, start_col, place_row,
-    out_own, out_oth, bias, raw, queries, keys, values,
-):
-    @pl.when(pl.program_id(0) == 0)
-    def _():
-        fits = (place_row[...] >= start_col[...]) & (place_row[...] <= place_col[...])
-        bias[...] = jnp.where(fits, 0.0, MASKED)
-        values[:, 2 * HEAD :] = jnp.ones_like(values[:, 2 * HEAD :])
-
-    merge(raw, q_own[...], q_oth[...])
-    normed, _ = normal_heads(raw[...].astype(jnp.float32))
-    queries[...] = low(normed * scale[...]) * SCORE_SCALE
-    merge(raw, k_own[...], k_oth[...])
-    normed, _ = normal_heads(raw[...].astype(jnp.float32))
-    keys[...] = low(normed * scale[...])
-    merge(values, v_own[...], v_oth[...])
-    for s in range(4):
-        upto = (s + 1) * 256
-        block = queries[s * 256 : upto]
-        parts = []
-        for h in range(2):
-            scores = last_dims(block * head_lanes(h, jnp.bfloat16), keys[:upto])
-            weights = jnp.exp(scores + bias[s * 256 : upto, :upto])
-            summed = dot(low(weights), values[:upto])
-            parts.append(summed[:, : 2 * HEAD] / summed[:, 2 * HEAD :])
-        joined = low(jnp.where(head_lanes(0, jnp.float32) > 0, parts[0], parts[1]))
-        out_own[s * BLOCK : (s + 1) * BLOCK] = joined[:BLOCK]
-        out_oth[s * BLOCK : (s + 1) * BLOCK] = joined[BLOCK:]
-
-
-def attention_back_kernel(
-    q_own, k_own, v_own, q_oth, k_oth, v_oth, g_own, g_oth, scale,
-    place_col, place_row, start_row,
-    out_own, out_oth, grad_scale, bias, raw, queries, keys, values, grads, dq, dk, dv,
-):
-    pair = pl.program_id(0)
-
-    @pl.when(pair == 0)
-    def _():
-        fits = (place_col[...] >= start_row[...]) & (place_col[...] <= place_row[...])
-        bias[...] = jnp.where(fits, 0.0, MASKED)
-
-    merge(raw, q_own[...], q_oth[...])
-    normed, _ = normal_heads(raw[...].astype(jnp.float32))
-    queries[...] = low(normed * scale[...]) * SCORE_SCALE
-    merge(raw, k_own[...], k_oth[...])
-    normed, _ = normal_heads(raw[...].astype(jnp.float32))
-    keys[...] = low(normed * scale[...])
-    merge(values, v_own[...], v_oth[...])
-    merge(grads, g_own[...], g_oth[...])
-    dk[...] = jnp.zeros_like(dk)
-    dv[...] = jnp.zeros_like(dv)
-    for s in range(4):
-        upto = (s + 1) * 256
-        total = 0.0
-        for h in range(2):
-            lanes = head_lanes(h, jnp.bfloat16)
-            query = queries[s * 256 : upto] * lanes
-            grad = grads[s * 256 : upto] * lanes
-            scores = last_dims(keys[:upto], query)
-            weights = jnp.exp(scores + bias[:upto, s * 256 : upto])
-            weights = weights * (1.0 / jnp.sum(weights, axis=0, keepdims=True))
-            grad_weights = last_dims(values[:upto], grad)
-            delta = jnp.sum(weights * grad_weights, axis=0, keepdims=True)
-            grad_scores = low(weights * (grad_weights - delta))
-            dv[:upto] += dot(low(weights), grad)
-            dk[:upto] += dot(grad_scores, query)
-            total = total + head_lanes(h, jnp.float32) * contract_rows(grad_scores, keys[:upto])
-        dq[s * 256 : upto] = total * SCORE_SCALE
-
-    width = out_own.shape[1] // 3
-    scale_sum = 0.0
-    for part, (own, oth, grad) in enumerate(((q_own, q_oth, dq), (k_own, k_oth, dk))):
-        merge(raw, own[...], oth[...])
-        normed, factor = normal_heads(raw[...].astype(jnp.float32))
-        scale_sum = scale_sum + jnp.sum(grad[...] * normed, axis=0, keepdims=True)
-        step = grad[...] * scale[...]
-        grad[...] = factor * (step - normed * sums_of_halves(normed * step))
-    grad_scale[...] = scale_sum
-    for part, grad in enumerate((dq, dk, dv)):
-        lanes = pl.ds(pl.multiple_of(part * width + pair * 2 * HEAD, 2 * HEAD), 2 * HEAD)
-        for s in range(4):
-            rows = slice(s * BLOCK, (s + 1) * BLOCK)
-            out_own[rows, lanes] = low(grad[s * 256 : s * 256 + BLOCK])
-            out_oth[rows, lanes] = low(grad[s * 256 + BLOCK : (s + 1) * 256])
-
-
-def mixed_specs(rows, pairs):
-    return [
-        pl.BlockSpec((rows, 2 * HEAD), lambda p, part=part: (0, part * pairs + p))
-        for part in range(3)
-    ]
-
-
-def whole(shape):
-    return pl.BlockSpec(shape, lambda p: (0,) * len(shape))
-
-
-def attention(mixed_own, mixed_oth, scale, places):
-    rows, width = mixed_own.shape
-    width //= 3
-    pairs = width // (2 * HEAD)
-    place, start = places
-    total = 2 * rows
-    spec = pl.BlockSpec((rows, 2 * HEAD), lambda p: (0, p))
-    return pl.pallas_call(
-        attention_kernel,
-        grid=(pairs,),
-        out_shape=[jax.ShapeDtypeStruct((rows, width), jnp.bfloat16)] * 2,
-        in_specs=mixed_specs(rows, pairs) * 2
-        + [pl.BlockSpec((1, 2 * HEAD), lambda p: (0, p))]
-        + [whole((total, 1)), whole((total, 1)), whole((1, total))],
-        out_specs=[spec, spec],
-        scratch_shapes=[
-            pltpu.VMEM((total, total), jnp.float32),
-            pltpu.VMEM((total, 2 * HEAD), jnp.bfloat16),
-            pltpu.VMEM((total, 2 * HEAD), jnp.bfloat16),
-            pltpu.VMEM((total, 2 * HEAD), jnp.bfloat16),
-            pltpu.VMEM((total, 4 * HEAD), jnp.bfloat16),
-        ],
-        compiler_params=pltpu.CompilerParams(vmem_limit_bytes=40 * 2**20),
-        cost_estimate=pl.CostEstimate(
-            flops=8 * total * total * width, bytes_accessed=8 * total * width,
-            transcendentals=total * total * pairs,
-        ),
-    )(
-        *[mixed_own] * 3, *[mixed_oth] * 3, scale,
-        place[:, None], start[:, None], place[None, :],
-    )
-
-
-def attention_back(mixed_own, mixed_oth, grad_own, grad_oth, scale, places):
-    rows, width = mixed_own.shape
-    width //= 3
-    pairs = width // (2 * HEAD)
-    place, start = places
-    total = 2 * rows
-    spec = pl.BlockSpec((rows, 2 * HEAD), lambda p: (0, p))
-    pair_spec = pl.BlockSpec((1, 2 * HEAD), lambda p: (0, p))
-    low_scratch = pltpu.VMEM((total, 2 * HEAD), jnp.bfloat16)
-    full_scratch = pltpu.VMEM((total, 2 * HEAD), jnp.float32)
-    return pl.pallas_call(
-        attention_back_kernel,
-        grid=(pairs,),
-        out_shape=[jax.ShapeDtypeStruct((rows, 3 * width), jnp.bfloat16)] * 2
-        + [jax.ShapeDtypeStruct((1, width), jnp.float32)],
-        in_specs=mixed_specs(rows, pairs) * 2
-        + [spec, spec, pair_spec]
-        + [whole((total, 1)), whole((1, total)), whole((1, total))],
-        out_specs=[whole((rows, 3 * width)), whole((rows, 3 * width)), pair_spec],
-        scratch_shapes=[pltpu.VMEM((total, total), jnp.float32)]
-        + [low_scratch] * 5
-        + [full_scratch] * 3,
-        compiler_params=pltpu.CompilerParams(vmem_limit_bytes=48 * 2**20),
-        cost_estimate=pl.CostEstimate(
-            flops=20 * total * total * width, bytes_accessed=16 * total * width,
-            transcendentals=total * total * pairs,
-        ),
-    )(
-        *[mixed_own] * 3, *[mixed_oth] * 3, grad_own, grad_oth, scale,
-        place[:, None], place[None, :], start[None, :],
-    )
-
-
-def forward_row(hiddens, weights, scales, places):
-    w_qkv, w_out, w_up, w_gate, w_down = weights
-    scale_qk, scale_up, scale_gate, alpha_attn, alpha_mlp = scales
-    hidden_own, hidden_oth = hiddens
-    mixed_own = low(dot(hidden_own, w_qkv))
-    mixed_oth = low(dot(hidden_oth, w_qkv))
-    attended_own, attended_oth = attention(mixed_own, mixed_oth, scale_qk, places)
-    branch_got = swap(low(dot(attended_oth, w_out)))
-    branch = dot(attended_own, w_out) + branch_got.astype(jnp.float32)
-    hidden = hidden_own.astype(jnp.float32)
-    first_sum = hidden + alpha_attn * (unit(branch) - hidden)
-    middle = unit(first_sum)
-    middle_own = low(middle)
-    middle_oth = swap(middle_own)
-
-    def lift(rows):
-        lift_up = low(dot(rows, w_up))
-        lift_gate = dot(rows, w_gate)
-        upward = lift_up.astype(jnp.float32) * scale_up
-        gating = lift_gate * scale_gate
-        return lift_up, low(lift_gate), low(upward * jax.nn.silu(gating))
-
-    lifted_own = lift(middle_own)
-    lifted_oth = lift(middle_oth)
-    output_got = swap(low(dot(lifted_oth[2], w_down)))
-    output = dot(lifted_own[2], w_down) + output_got.astype(jnp.float32)
-    second_sum = middle + alpha_mlp * (unit(output) - middle)
-    result = low(unit(second_sum))
-    kept = (
-        hiddens, (mixed_own, mixed_oth), (attended_own, attended_oth),
-        (middle_own, middle_oth), (lifted_own, lifted_oth), branch, output,
-    )
-    return result, kept
-
-
-def backward_row(grad_out, kept, weights, scales, places):
-    w_qkv, w_out, w_up, w_gate, w_down = weights
-    scale_qk, scale_up, scale_gate, alpha_attn, alpha_mlp = scales
-    hiddens, mixed, attended, middles, lifted, branch, output = kept
-    hidden = hiddens[0].astype(jnp.float32)
-    unit_branch = unit(branch)
-    first_sum = hidden + alpha_attn * (unit_branch - hidden)
-    middle = unit(first_sum)
-    unit_output = unit(output)
-    second_sum = middle + alpha_mlp * (unit_output - middle)
-    grad_second = unit_back(second_sum, grad_out)
-    grad_alpha_mlp = jnp.sum(grad_second * (unit_output - middle), axis=0)
-    grad_output_own = low(unit_back(output, alpha_mlp * grad_second))
-    grad_output_oth = swap(grad_output_own)
-
-    def unlift(grad_rows, lifts):
-        lift_up, lift_gate, _ = lifts
-        lift_up = lift_up.astype(jnp.float32)
-        lift_gate = lift_gate.astype(jnp.float32)
-        grad_inner = contract_cols(grad_rows, w_down)
-        gating = lift_gate * scale_gate
-        sigmoid = jax.nn.sigmoid(gating)
-        grad_up = grad_inner * (gating * sigmoid)
-        grad_gate = grad_inner * (lift_up * scale_up) * sigmoid * (1.0 + gating * (1.0 - sigmoid))
-        sums = (jnp.sum(grad_up * lift_up, axis=0), jnp.sum(grad_gate * lift_gate, axis=0))
-        return low(grad_up * scale_up), low(grad_gate * scale_gate), sums
-
-    grad_lift_own = unlift(grad_output_own, lifted[0])
-    grad_lift_oth = unlift(grad_output_oth, lifted[1])
-    middle_got = swap(
-        low(contract_cols(grad_lift_oth[0], w_up) + contract_cols(grad_lift_oth[1], w_gate))
-    )
-    grad_middle = (
-        contract_cols(grad_lift_own[0], w_up)
-        + contract_cols(grad_lift_own[1], w_gate)
-        + middle_got.astype(jnp.float32)
-        + grad_second * (1.0 - alpha_mlp)
-    )
-    grad_first = unit_back(first_sum, grad_middle)
-    grad_alpha_attn = jnp.sum(grad_first * (unit_branch - hidden), axis=0)
-    grad_branch_own = low(unit_back(branch, alpha_attn * grad_first))
-    grad_branch_oth = swap(grad_branch_own)
-    grad_attended_own = low(contract_cols(grad_branch_own, w_out))
-    grad_attended_oth = low(contract_cols(grad_branch_oth, w_out))
-    grad_mixed_own, grad_mixed_oth, grad_scale_qk = attention_back(
-        *mixed, grad_attended_own, grad_attended_oth, scale_qk, places
-    )
-    hidden_got = swap(low(contract_cols(grad_mixed_oth, w_qkv)))
-    grad_hidden = (
-        contract_cols(grad_mixed_own, w_qkv)
-        + hidden_got.astype(jnp.float32)
-        + grad_first * (1.0 - alpha_attn)
-    )
-    operands = (
-        (hiddens, (grad_mixed_own, grad_mixed_oth)),
-        (attended, (grad_branch_own, grad_branch_oth)),
-        (middles, (grad_lift_own[0], grad_lift_oth[0])),
-        (middles, (grad_lift_own[1], grad_lift_oth[1])),
-        ((lifted[0][2], lifted[1][2]), (grad_output_own, grad_output_oth)),
-    )
-    small = (
-        jnp.concatenate([grad_alpha_attn, grad_alpha_mlp]),
-        grad_lift_own[2][0] + grad_lift_oth[2][0],
-        (grad_lift_own[2][1] + grad_lift_oth[2][1]) * math.sqrt(hidden.shape[1]),
-        grad_scale_qk[0],
-    )
-    return low(grad_hidden), operands, small
-
-
-def weight_grads(operands):
-    return tuple(
-        low(contract_rows(jnp.concatenate(left), jnp.concatenate(right)))
-        for left, right in operands
-    )
-
-
 MESH = pl.DeviceIdType.MESH
 
 
@@ -728,21 +444,45 @@
     return pl.multiple_of(offset, 128)
 
 
-def gather_kernel(
-    w_qkv, w_out, w_in, w_down, vectors, valid, tokens, cotangent,
-    o_qkv, o_out, o_up, o_gate, o_down, o_vectors, o_valid, row_own, row_oth,
+def every(count, work):
+    def step(n, carry):
+        work(n)
+        return carry
+
+    lax.fori_loop(0, count, step, 0)
+
+
+def silu(x):
+    return x * jax.nn.sigmoid(x)
+
+
+def forward_kernel(
+    w_qkv, w_out, w_in, w_down, vectors, valid, tokens, cotangent, place_col, start_col, place_row,
+    o_qkv, o_out, o_up, o_gate, o_down, o_vectors, o_valid, o_row,
+    o_hidden, o_mixed, o_attended, o_middle, o_lift_up, o_lift_gate, o_inner, o_branch, o_output,
+    o_result, o_log_sums,
+    wq, wo, wu, wg, wd, vec, flat, scale_up, scale_gate, alpha_attn, alpha_mlp,
+    hid, mixed, att, mid, lift_up, lift_gate, inner, branch, middle, output, result,
+    part_one, got_one, part_two, got_two, bias, raw, queries, keys, values, log_sums,
     first_send, first_recv, next_send, next_recv, row_send, row_recv, valid_send, valid_recv,
-    swap_send, swap_recv,
+    own_recv, oth_send, oth_recv, one_send, one_recv, mid_send, mid_recv, two_send, two_recv,
+    result_send, kept,
 ):
     c, s, f, fx, fy, layer = position()
+    sibling = (1 - c, s, f)
+    early = layer == 0
+    late = layer == 1
+    next_plane = (c, (s - 1) * 3, f)
+    half = 4 * BLOCK
+    width = w_out.shape[1]
     greet(
-        [(1 - c, s, f), (c, s, fx), (1 - c, s, fx), (c, s, fy), (1 - c, s, fy)]
+        [sibling, (c, s, fx), (1 - c, s, fx), (c, s, fy), (1 - c, s, fy)]
         + [(c, (s + step) % 4, f) for step in (1, 2, 3)]
     )
 
     for to, held in enumerate((cotangent.at[0], tokens.at[0], tokens.at[1], cotangent.at[1])):
         src = held.at[pl.ds(c * BLOCK, BLOCK)]
-        dst = row_own.at[pl.ds(s * BLOCK, BLOCK)]
+        dst = o_row.at[pl.ds(s * BLOCK, BLOCK)]
         flags, flags_to = valid.at[to // 2], o_valid.at[s]
 
         @pl.when(s == to)
@@ -757,19 +497,19 @@
 
     def pieces(item, h):
         if item == 0:
-            return [(vectors, o_vectors.at[f])]
+            return [(vectors, vec.at[f])]
         if item == 1:
             return [
                 (
                     w_qkv.at[:, pl.ds(lane(part * 256 + h * 128), 128)],
-                    o_qkv.at[pl.ds(f * 256, 256), pl.ds(part * 128, 128)],
+                    wq.at[pl.ds(f * 256, 256), pl.ds(part * 128, 128)],
                 )
                 for part in range(12)
             ]
         if item == 2:
-            return [(w_out.at[pl.ds(h * 128, 128)], o_out.at[pl.ds(f * 128, 128)])]
+            return [(w_out.at[pl.ds(h * 128, 128)], wo.at[pl.ds(f * 128, 128)])]
         if item in (3, 4):
-            to = (o_up, o_gate)[item - 3]
+            to = (wu, wg)[item - 3]
             return [
                 (
                     w_in.at[:, pl.ds(lane((item - 3) * 4096 + part * 1024 + h * 512), 512)],
@@ -777,69 +517,305 @@
                 )
                 for part in range(4)
             ]
-        return [(w_down.at[pl.ds(h * 512, 512)], o_down.at[pl.ds(f * 512, 512)])]
-
-    outputs = (o_vectors, o_qkv, o_out, o_up, o_gate, o_down)
+        return [(w_down.at[pl.ds(h * 512, 512)], wd.at[pl.ds(f * 512, 512)])]
+
+    weights = (vec, wq, wo, wu, wg, wd)
 
     def block(item, of):
         if item == 0:
-            return o_vectors.at[of]
-        rows = outputs[item].shape[0] // 4
-        return outputs[item].at[pl.ds(of * rows, rows)]
+            return vec.at[of]
+        rows = weights[item].shape[0] // 4
+        return weights[item].at[pl.ds(of * rows, rows)]
 
     def part_of(item, of, part):
         if item == 0:
-            return o_vectors.at[of, pl.ds(part * 16, 16)]
-        rows = outputs[item].shape[0] // 8
-        return outputs[item].at[pl.ds(of * 2 * rows + part * rows, rows)]
+            return vec.at[of, pl.ds(part * 16, 16)]
+        rows = weights[item].shape[0] // 8
+        return weights[item].at[pl.ds(of * 2 * rows + part * rows, rows)]
 
     targets = (
         ((c, s, fx), c, 1), ((c, s, fy), c, 2), ((1 - c, s, fx), 1 - c, 1),
-        ((1 - c, s, fy), 1 - c, 2), ((1 - c, s, f), 1 - c, 0),
-    )
-
-    @pl.when(c == layer)
-    def _():
-        for item in range(6):
-            for index, (device, h, came) in enumerate(targets):
-                for src, dst in pieces(item, h):
-                    remote(
-                        src, dst, first_send.at[item, index], first_recv.at[item, came], device
-                    ).start()
-            for src, dst in pieces(item, c):
-                pltpu.make_async_copy(src, dst, first_recv.at[item, 0]).start()
-
-    for came in range(4):
-        arrived(row_own.at[pl.ds(came * BLOCK, BLOCK)], row_recv.at[came])
-    swapped = remote(row_own, row_oth, swap_send, swap_recv, (1 - c, s, f))
-    swapped.start()
-
-    forwards = []
-    for item in range(6):
+        ((1 - c, s, fy), 1 - c, 2), (sibling, 1 - c, 0),
+    )
+
+    def spread(*items):
+        @pl.when(c == layer)
+        def _():
+            for item in items:
+                for index, (device, h, came) in enumerate(targets):
+                    for src, dst in pieces(item, h):
+                        remote(
+                            src, dst, first_send.at[item, index], first_recv.at[item, came], device
+                        ).start()
+                for src, dst in pieces(item, c):
+                    pltpu.make_async_copy(src, dst, first_recv.at[item, 0]).start()
+
+    spread(0, 1, 2, 3)
+
+    def relay(item):
         for part, (came, of, to) in enumerate(((1, fx, fy), (2, fy, fx))):
             arrived(block(item, of), first_recv.at[item, came])
-            forward = remote(
-                part_of(item, of, part), part_of(item, of, part),
-                next_send.at[item, part], next_recv.at[item, part], (c, s, to),
-            )
-            forward.start()
-            forwards.append(forward)
-
-    across = 3 - f
-    for item in range(6):
+            moved = part_of(item, of, part)
+            remote(
+                moved, moved, next_send.at[item, part], next_recv.at[item, part], (c, s, to)
+            ).start()
+
+    copies = []
+
+    def keep(src, dst):
+        copy = pltpu.make_async_copy(src, dst, kept.at[len(copies)])
+        copy.start()
+        copies.append(copy)
+
+    kept_weights = (None, o_qkv, o_out, o_up, o_gate, o_down)
+
+    def complete(item):
         arrived(block(item, f), first_recv.at[item, 0])
         for part in range(2):
-            arrived(part_of(item, across, part), next_recv.at[item, part])
-    for forward in forwards:
-        forward.wait_send()
-    swapped.wait()
-    for came in range(4):
-        arrived(o_valid.at[came], valid_recv.at[came])
-
-        @pl.when(s != came)
-        def _():
-            arrived(row_own.at[pl.ds(came * BLOCK, BLOCK)], row_send.at[came])
-            arrived(o_valid.at[came], valid_send.at[came])
+            arrived(part_of(item, 3 - f, part), next_recv.at[item, part])
+        if item:
+            keep(weights[item], kept_weights[item])
+
+    fits = (place_row[...] >= start_col[...]) & (place_row[...] <= place_col[...])
+    bias[...] = jnp.where(fits, 0.0, MASKED)
+    values[:, 2 * HEAD :] = jnp.ones_like(values[:, 2 * HEAD :])
+
+    relay(0)
+    relay(1)
+    spread(4)
+    relay(2)
+
+    def rows_of(b):
+        return pl.ds(b * BLOCK, BLOCK)
+
+    def to_sibling(b, src):
+        remote(src, hid.at[1, rows_of(b)], oth_send.at[b], oth_recv.at[b], sibling).start()
+
+    @pl.when(early)
+    def _():
+        for b in range(4):
+            held = o_row.at[rows_of(b)]
+            arrived(held, row_recv.at[b])
+            pltpu.make_async_copy(held, hid.at[0, rows_of(b)], own_recv.at[b]).start()
+            to_sibling(b, held)
+        for b in range(4):
+            arrived(hid.at[0, rows_of(b)], own_recv.at[b])
+
+    @pl.when(late)
+    def _():
+        relay(3)
+        spread(5)
+        relay(4)
+        relay(5)
+        for b in range(4):
+            arrived(o_row.at[rows_of(b)], row_recv.at[b])
+        for b in range(4):
+            arrived(hid.at[0, rows_of(b)], own_recv.at[b])
+            to_sibling(b, hid.at[0, rows_of(b)])
+
+    complete(0)
+    keep(vec, o_vectors)
+    flat[...] = vec[...].astype(jnp.float32)
+    for n in range(4):
+        for j in range(4):
+            at = slice(n * 512 + j * 128, n * 512 + (j + 1) * 128)
+            row = 2 + (n % 2) * 8 + j
+            scale_up[:, at] = flat[n // 2, pl.ds(row + c * 4, 1), :]
+            scale_gate[:, at] = flat[2 + n // 2, pl.ds(row + c * 4, 1), :] * math.sqrt(width)
+    for n in range(2):
+        for j in range(4):
+            at = slice(n * 512 + j * 128, n * 512 + (j + 1) * 128)
+            alpha_attn[:, at] = flat[n, 18 + j : 19 + j, :]
+            alpha_mlp[:, at] = flat[2 + n, 18 + j : 19 + j, :]
+
+    complete(1)
+    for side in range(2):
+        if side:
+            for b in range(4):
+                arrived(hid.at[1, rows_of(b)], oth_recv.at[b])
+            keep(hid, o_hidden)
+
+        def mix(n, side=side):
+            at = pl.ds(lane(n * 512), 512)
+            mixed[side, :, at] = low(dot(hid[side], wq[:, at]))
+
+        every(3, mix)
+    keep(mixed, o_mixed)
+
+    first = (lax.broadcasted_iota(jnp.int32, (8, 2 * HEAD), 1) == 0).astype(jnp.bfloat16)
+
+    def attend(pair):
+        def normal(to, part):
+            at = pl.ds(lane(part * (width // 2) + pair * 2 * HEAD), 2 * HEAD)
+            merge(raw, mixed[0, :, at], mixed[1, :, at])
+            normed, _ = normal_heads(raw[...].astype(jnp.float32))
+            to[...] = low(normed * flat[pair, pl.ds(c, 1), :])
+
+        normal(queries, 0)
+        normal(keys, 1)
+        at = pl.ds(lane(width + pair * 2 * HEAD), 2 * HEAD)
+        merge(values, mixed[0, :, at], mixed[1, :, at])
+        at = pl.ds(lane(pair * 2 * HEAD), 2 * HEAD)
+        for q in range(4):
+            upto = (q + 1) * 256
+            query = queries[q * 256 : upto] * SCORE_SCALE
+            query = jnp.concatenate([query * head_lanes(h, jnp.bfloat16) for h in range(2)])
+            summed = 0.0
+            for k in range(q + 1):
+                at_keys = slice(k * 256, (k + 1) * 256)
+                mask = jnp.concatenate([bias[q * 256 : upto, at_keys]] * 2)
+                weighted = jnp.exp(last_dims(query, keys[at_keys]) + mask)
+                summed = summed + dot(low(weighted), values[at_keys])
+            total = summed[:, 2 * HEAD :]
+            parts = summed[:, : 2 * HEAD] / total
+            parts = parts[:256], parts[256:]
+            log_sum = jnp.log(row_sums(total, first)[:1])
+            for h in range(2):
+                log_sums[pair, h : h + 1, q * 256 : upto] = log_sum[:, h * 256 : (h + 1) * 256]
+            joined = low(jnp.where(head_lanes(0, jnp.float32) > 0, parts[0], parts[1]))
+            att[0, q * BLOCK : (q + 1) * BLOCK, at] = joined[:BLOCK]
+            att[1, q * BLOCK : (q + 1) * BLOCK, at] = joined[BLOCK:]
+
+    every(4, attend)
+    keep(att, o_attended)
+    keep(log_sums, o_log_sums)
+
+    complete(2)
+
+    def branch_sent(n):
+        at = pl.ds(lane(n * 256), 256)
+        part_one[:, at] = low(dot(att[1], wo[:, at]))
+        remote(
+            part_one.at[:, at], got_one.at[:, at], one_send.at[n], one_recv.at[n], sibling
+        ).start()
+
+    def branch_own(n):
+        at = pl.ds(lane(n * 256), 256)
+        branch[:, at] = dot(att[0], wo[:, at])
+
+    every(4, branch_sent)
+    every(4, branch_own)
+    for n in range(4):
+        arrived(got_one.at[:, pl.ds(n * 256, 256)], one_recv.at[n])
+
+    def first_step(b):
+        rows = pl.ds(b * 64, 64)
+        total = branch[rows] + got_one[rows].astype(jnp.float32)
+        branch[rows] = total
+        hidden = hid[0, rows].astype(jnp.float32)
+        stepped = unit(hidden + alpha_attn[...] * (unit(total) - hidden))
+        middle[rows] = stepped
+        mid[0, rows] = low(stepped)
+
+        @pl.when(b % 2 == 1)
+        def _():
+            sent = rows_of(b // 2)
+            remote(
+                mid.at[0, sent], mid.at[1, sent], mid_send.at[b // 2], mid_recv.at[b // 2], sibling
+            ).start()
+
+    every(8, first_step)
+    keep(branch, o_branch)
+
+    @pl.when(early)
+    def _():
+        relay(3)
+        spread(5)
+
+    complete(3)
+    for side in range(2):
+        if side:
+            for b in range(4):
+                arrived(mid.at[1, rows_of(b)], mid_recv.at[b])
+            keep(mid, o_middle)
+
+        def lift(n, side=side):
+            at = pl.ds(lane(n * 512), 512)
+            lift_up[side, :, at] = low(dot(mid[side], wu[:, at]))
+
+        every(4, lift)
+    keep(lift_up, o_lift_up)
+
+    @pl.when(early)
+    def _():
+        relay(4)
+
+    complete(4)
+    for side in (1, 0):
+
+        def open_gate(n, side=side):
+            at = pl.ds(lane(n * 512), 512)
+            gate = dot(mid[side], wg[:, at])
+            lift_gate[side, :, at] = low(gate)
+            upward = lift_up[side, :, at].astype(jnp.float32) * scale_up[:, at]
+            inner[side, :, at] = low(upward * silu(gate * scale_gate[:, at]))
+
+        every(4, open_gate)
+    keep(lift_gate, o_lift_gate)
+    keep(inner, o_inner)
+
+    @pl.when(early)
+    def _():
+        relay(5)
+
+    complete(5)
+
+    def output_sent(n):
+        at = pl.ds(lane(n * 256), 256)
+        part_two[:, at] = low(dot(inner[1], wd[:, at]))
+        remote(
+            part_two.at[:, at], got_two.at[:, at], two_send.at[n], two_recv.at[n], sibling
+        ).start()
+
+    def output_own(n):
+        at = pl.ds(lane(n * 256), 256)
+        output[:, at] = dot(inner[0], wd[:, at])
+
+    every(4, output_sent)
+    every(4, output_own)
+    for n in range(4):
+        arrived(got_two.at[:, pl.ds(n * 256, 256)], two_recv.at[n])
+
+    def second_step(b):
+        rows = pl.ds(b * 64, 64)
+        total = output[rows] + got_two[rows].astype(jnp.float32)
+        output[rows] = total
+        start = middle[rows]
+        result[rows] = low(unit(start + alpha_mlp[...] * (unit(total) - start)))
+
+        @pl.when(early & (b % 2 == 1))
+        def _():
+            sent = rows_of(b // 2)
+            remote(
+                result.at[sent], hid.at[0, sent], result_send.at[b // 2], own_recv.at[b // 2],
+                next_plane,
+            ).start()
+
+    every(8, second_step)
+    keep(output, o_output)
+    keep(result, o_result)
+
+    for copy in copies:
+        copy.wait()
+    for item in range(6):
+        for part in range(2):
+            arrived(part_of(item, f, part), next_send.at[item, part])
+    for b in range(4):
+        rows = rows_of(b)
+        arrived(hid.at[1, rows], oth_send.at[b])
+        arrived(part_one.at[:, pl.ds(b * 256, 256)], one_send.at[b])
+        arrived(part_two.at[:, pl.ds(b * 256, 256)], two_send.at[b])
+        arrived(mid.at[0, rows], mid_send.at[b])
+        arrived(o_valid.at[b], valid_recv.at[b])
+
+        @pl.when(early)
+        def _():
+            arrived(result.at[rows], result_send.at[b])
+
+        @pl.when(s != b)
+        def _():
+            arrived(o_row.at[rows], row_send.at[b])
+            arrived(o_valid.at[b], valid_send.at[b])
 
     @pl.when(c == layer)
     def _():
@@ -848,37 +824,393 @@
                 arrived(block(item, f), first_send.at[item, index])
 
 
-def gather(w_qkv, w_out, w_in, w_down, vectors, valid, tokens, cotangent):
+def forward_all(w_qkv, w_out, w_in, w_down, vectors, valid, tokens, cotangent, places):
     width = w_out.shape[1]
     units = w_down.shape[0] * 4
-    low_shape = lambda *shape: jax.ShapeDtypeStruct(shape, jnp.bfloat16)
+    rows = 4 * BLOCK
+    place, start = places
     sems = pltpu.SemaphoreType.DMA
+
+    def low_shape(*shape):
+        return jax.ShapeDtypeStruct(shape, jnp.bfloat16)
+
+    def low_vmem(*shape):
+        return pltpu.VMEM(shape, jnp.bfloat16)
+
+    def full_vmem(*shape):
+        return pltpu.VMEM(shape, jnp.float32)
+
+    weights = [
+        (width, 3 * width // 2), (width // 2, width), (width, units // 2), (width, units // 2),
+        (units // 2, width),
+    ]
+    sides = [
+        (2, rows, width), (2, rows, 3 * width // 2), (2, rows, width // 2), (2, rows, width),
+        (2, rows, units // 2), (2, rows, units // 2), (2, rows, units // 2),
+    ]
+    anywhere = pl.BlockSpec(memory_space=pl.ANY)
+    near = pl.BlockSpec(memory_space=pltpu.VMEM)
     return pl.pallas_call(
-        gather_kernel,
+        forward_kernel,
+        out_shape=[low_shape(*shape) for shape in weights]
+        + [low_shape(4, *vectors.shape), low_shape(4, *valid.shape[1:]), low_shape(rows, width)]
+        + [low_shape(*shape) for shape in sides]
+        + [jax.ShapeDtypeStruct((rows, width), jnp.float32)] * 2
+        + [low_shape(rows, width)]
+        + [jax.ShapeDtypeStruct((4, 2, 2 * rows), jnp.float32)],
+        in_specs=[anywhere] * 8 + [near] * 3,
+        out_specs=[anywhere] * 19,
+        scratch_shapes=[low_vmem(*shape) for shape in weights]
+        + [
+            low_vmem(4, *vectors.shape), full_vmem(4, *vectors.shape),
+            full_vmem(1, units // 2), full_vmem(1, units // 2),
+            full_vmem(1, width), full_vmem(1, width),
+        ]
+        + [low_vmem(*shape) for shape in sides]
+        + [full_vmem(rows, width)] * 3
+        + [low_vmem(rows, width)] * 5
+        + [full_vmem(2 * rows, 2 * rows)]
+        + [low_vmem(2 * rows, 2 * HEAD)] * 3
+        + [low_vmem(2 * rows, 4 * HEAD)]
+        + [full_vmem(4, 2, 2 * rows)]
+        + [sems((6, 5)), sems((6, 3)), sems((6, 2)), sems((6, 2))]
+        + [sems((4,))] * 14
+        + [sems((20,))],
+        compiler_params=pltpu.CompilerParams(
+            collective_id=0, has_side_effects=True, vmem_limit_bytes=60 * 2**20
+        ),
+    )(
+        w_qkv, w_out, w_in, w_down, vectors, valid, tokens, cotangent,
+        place[:, None], start[:, None], place[None, :],
+    )
+
+
+def row_sums(x, lanes):
+    high = low(x)
+    rest = low(x - high.astype(jnp.float32))
+    return last_dims(lanes, high) + last_dims(lanes, rest)
+
+
+def backward_kernel(
+    w_qkv, w_out, w_up, w_gate, w_down, hidden, mixed_in, attended, up_in, gate_in, branch_in,
+    output_in, row, log_sums, scale_qk, scale_up, scale_gate, alpha_attn, alpha_mlp,
+    place_col, place_row, start_row,
+    o_output, o_up, o_gate, o_branch, o_mixed, o_grad, sum_alphas, sum_scales, sum_qk,
+    wq, wo, wu, wg, wd, hid, mixed, att, up, gate, branch, output, grad_in,
+    grad_output, grad_middle, part_one, got_one, grad_branch, grad_att, part_two, got_two, result,
+    bias, raw, queries, keys, values, grads, dq, dk, dv,
+    load, grad_recv, out_send, out_recv, one_send, one_recv, branch_send, branch_recv,
+    two_send, two_recv, result_send, kept,
+):
+    c, s, f, _, _, layer = position()
+    sibling = (1 - c, s, f)
+    early = layer == 0
+    late = layer == 1
+    partner = (c, (1 - layer) * (s - 1) * 3 + layer * (s // 3 + 1), f)
+    width = w_out.shape[1]
+    greet([sibling, partner])
+
+    loads = (
+        (output_in, output), (hidden.at[0], hid), (branch_in, branch), (w_down, wd), (gate_in, gate),
+        (up_in, up), (w_up, wu), (w_gate, wg), (w_out, wo), (mixed_in, mixed), (attended, att),
+        (w_qkv, wq),
+    )
+    for index, (src, dst) in enumerate(loads):
+        pltpu.make_async_copy(src, dst, load.at[index]).start()
+
+    def loaded(*names):
+        for index in names:
+            arrived(loads[index][1], load.at[index])
+
+    copies = []
+
+    def keep(src, dst):
+        copy = pltpu.make_async_copy(src, dst, kept.at[len(copies)])
+        copy.start()
+        copies.append(copy)
+
+    def rows_of(b):
+        return pl.ds(b * BLOCK, BLOCK)
+
+    @pl.when(late)
+    def _():
+        for b in range(4):
+            pltpu.make_async_copy(
+                row.at[rows_of(b)], grad_in.at[rows_of(b)], grad_recv.at[b]
+            ).start()
+
+    fits = (place_col[...] >= start_row[...]) & (place_col[...] <= place_row[...])
+    bias[...] = jnp.where(fits, 0.0, MASKED)
+    sum_alphas[...] = jnp.zeros_like(sum_alphas)
+    sum_scales[...] = jnp.zeros_like(sum_scales)
+    loaded(0, 1, 2)
+
+    def both(n):
+        return pl.ds(lane(n * 256), 256)
+
+    def second_step(b):
+        rows = pl.ds(b * 64, 64)
+
+        @pl.when(b % 2 == 0)
+        def _():
+            arrived(grad_in.at[rows_of(b // 2)], grad_recv.at[b // 2])
+
+        start = hid[rows].astype(jnp.float32)
+        middle = unit(start + alpha_attn[...] * (unit(branch[rows]) - start))
+        total = output[rows]
+        change = unit(total) - middle
+        grad = unit_back(middle + alpha_mlp[...] * change, grad_in[rows].astype(jnp.float32))
+        sum_alphas[1:2] += jnp.sum(grad * change, axis=0, keepdims=True)
+        grad_output[0, rows] = low(unit_back(total, alpha_mlp[...] * grad))
+        grad_middle[rows] = grad * (1.0 - alpha_mlp[...])
+
+        @pl.when(b % 2 == 1)
+        def _():
+            sent = rows_of(b // 2)
+            remote(
+                grad_output.at[0, sent], grad_output.at[1, sent], out_send.at[b // 2],
+                out_recv.at[b // 2], sibling,
+            ).start()
+
+    every(8, second_step)
+
+    loaded(3, 4, 5)
+    for side in range(2):
+        if side:
+            for b in range(4):
+                arrived(grad_output.at[1, rows_of(b)], out_recv.at[b])
+            keep(grad_output, o_output)
+
+        def close_gate(n, side=side):
+            at = pl.ds(lane(n * 512), 512)
+            grad = last_dims(grad_output[side], wd[pl.ds(n * 512, 512)])
+            lift_up = up[side, :, at].astype(jnp.float32)
+            lift_gate = gate[side, :, at].astype(jnp.float32)
+            gating = lift_gate * scale_gate[:, at]
+            sigmoid = jax.nn.sigmoid(gating)
+            grad_up = grad * (gating * sigmoid)
+            grad_gate = (
+                grad * (lift_up * scale_up[:, at]) * sigmoid * (1.0 + gating * (1.0 - sigmoid))
+            )
+            sum_scales[0:1, at] += jnp.sum(grad_up * lift_up, axis=0, keepdims=True)
+            sum_scales[1:2, at] += jnp.sum(grad_gate * lift_gate, axis=0, keepdims=True)
+            up[side, :, at] = low(grad_up * scale_up[:, at])
+            gate[side, :, at] = low(grad_gate * scale_gate[:, at])
+
+        every(4, close_gate)
+    keep(up, o_up)
+    keep(gate, o_gate)
+    loaded(6, 7)
+
+    def lifted(side, n):
+        rows = pl.ds(n * 256, 256)
+        return last_dims(up[side], wu[rows]) + last_dims(gate[side], wg[rows])
+
+    def middle_sent(n):
+        at = both(n)
+        part_one[:, at] = low(lifted(1, n))
+        remote(
+            part_one.at[:, at], got_one.at[:, at], one_send.at[n], one_recv.at[n], sibling
+        ).start()
+
+    def middle_own(n):
+        at = both(n)
+        grad_middle[:, at] = grad_middle[:, at] + lifted(0, n)
+
+    every(4, middle_sent)
+    every(4, middle_own)
+    for n in range(4):
+        arrived(got_one.at[:, pl.ds(n * 256, 256)], one_recv.at[n])
+
+    def first_step(b):
+        rows = pl.ds(b * 64, 64)
+        start = hid[rows].astype(jnp.float32)
+        total = branch[rows]
+        change = unit(total) - start
+        grad = grad_middle[rows] + got_one[rows].astype(jnp.float32)
+        grad = unit_back(start + alpha_attn[...] * change, grad)
+        sum_alphas[0:1] += jnp.sum(grad * change, axis=0, keepdims=True)
+        grad_branch[0, rows] = low(unit_back(total, alpha_attn[...] * grad))
+        grad_middle[rows] = grad * (1.0 - alpha_attn[...])
+
+        @pl.when(b % 2 == 1)
+        def _():
+            sent = rows_of(b // 2)
+            remote(
+                grad_branch.at[0, sent], grad_branch.at[1, sent], branch_send.at[b // 2],
+                branch_recv.at[b // 2], sibling,
+            ).start()
+
+    every(8, first_step)
+    loaded(8, 9, 10)
+    for side in range(2):
+        if side:
+            for b in range(4):
+                arrived(grad_branch.at[1, rows_of(b)], branch_recv.at[b])
+            keep(grad_branch, o_branch)
+
+        def attended_grad(n, side=side):
+            grad_att[side, :, both(n)] = low(
+                last_dims(grad_branch[side], wo[pl.ds(n * 256, 256)])
+            )
+
+        every(2, attended_grad)
+
+    def attend_back(pair):
+        def lanes(part):
+            return pl.ds(lane(part * (width // 2) + pair * 2 * HEAD), 2 * HEAD)
+
+        scale = scale_qk[pl.ds(pair, 1)]
+
+        def normal(part):
+            merge(raw, mixed[0, :, lanes(part)], mixed[1, :, lanes(part)])
+            return normal_heads(raw[...].astype(jnp.float32))
+
+        queries[...] = low(normal(0)[0] * scale) * SCORE_SCALE
+        keys[...] = low(normal(1)[0] * scale)
+        merge(values, mixed[0, :, lanes(2)], mixed[1, :, lanes(2)])
+        merge(grads, grad_att[0, :, lanes(0)], grad_att[1, :, lanes(0)])
+        merge(raw, att[0, :, lanes(0)], att[1, :, lanes(0)])
+        dk[...] = jnp.zeros_like(dk)
+        dv[...] = jnp.zeros_like(dv)
+        head = lax.broadcasted_iota(jnp.int32, (8, 2 * HEAD), 0)
+        marks = (lax.broadcasted_iota(jnp.int32, (8, 2 * HEAD), 1) // HEAD == head).astype(
+            jnp.bfloat16
+        )
+        for q in range(4):
+            at = slice(q * 256, (q + 1) * 256)
+            upto = slice(0, (q + 1) * 256)
+            deltas = row_sums(grads[at].astype(jnp.float32) * raw[at].astype(jnp.float32), marks)
+            delta = jnp.concatenate([deltas[h : h + 1] for h in range(2)], axis=1)
+            log_sum = jnp.concatenate([log_sums[pair, h : h + 1, at] for h in range(2)], axis=1)
+            query = jnp.concatenate([queries[at] * head_lanes(h, jnp.bfloat16) for h in range(2)])
+            grad = jnp.concatenate([grads[at] * head_lanes(h, jnp.bfloat16) for h in range(2)])
+            key = keys[upto]
+            mask = jnp.concatenate([bias[upto, at]] * 2, axis=1)
+            weights = jnp.exp(last_dims(key, query) + (mask - log_sum))
+            grad_scores = low(weights * (last_dims(values[upto], grad) - delta))
+            dv[upto] += dot(low(weights), grad)
+            dk[upto] += dot(grad_scores, query)
+            to_queries = contract_rows(grad_scores, key)
+            dq[at] = (
+                head_lanes(0, jnp.float32) * to_queries[:256]
+                + head_lanes(1, jnp.float32) * to_queries[256:]
+            )
+
+        scale_sum = 0.0
+        for part, grad in enumerate((dq, dk)):
+            normed, factor = normal(part)
+            found = grad[...] * SCORE_SCALE if part == 0 else grad[...]
+            scale_sum = scale_sum + jnp.sum(found * normed, axis=0, keepdims=True)
+            step = found * scale
+            grad[...] = factor * (step - normed * sums_of_halves(normed * step))
+        sum_qk[pl.ds(pair, 1)] = scale_sum
+        for part, grad in enumerate((dq, dk, dv)):
+            for q in range(4):
+                rows = slice(q * BLOCK, (q + 1) * BLOCK)
+                mixed[0, rows, lanes(part)] = low(grad[q * 256 : q * 256 + BLOCK])
+                mixed[1, rows, lanes(part)] = low(grad[q * 256 + BLOCK : (q + 1) * 256])
+
+    every(4, attend_back)
+    keep(mixed, o_mixed)
+    loaded(11)
+
+    def hidden_sent(n):
+        at = both(n)
+        part_two[:, at] = low(last_dims(mixed[1], wq[pl.ds(n * 256, 256)]))
+        remote(
+            part_two.at[:, at], got_two.at[:, at], two_send.at[n], two_recv.at[n], sibling
+        ).start()
+
+    def hidden_own(n):
+        at = both(n)
+        grad_middle[:, at] = grad_middle[:, at] + last_dims(mixed[0], wq[pl.ds(n * 256, 256)])
+
+    every(4, hidden_sent)
+    every(4, hidden_own)
+    for n in range(4):
+        arrived(got_two.at[:, pl.ds(n * 256, 256)], two_recv.at[n])
+
+    def finish(b):
+        rows = rows_of(b)
+        result[rows] = low(grad_middle[rows] + got_two[rows].astype(jnp.float32))
+
+        @pl.when(late)
+        def _():
+            remote(
+                result.at[rows], grad_in.at[rows], result_send.at[b], grad_recv.at[b], partner
+            ).start()
+
+    every(4, finish)
+    keep(result, o_grad)
+
+    for copy in copies:
+        copy.wait()
+    for b in range(4):
+        rows, at = rows_of(b), pl.ds(b * 256, 256)
+        arrived(grad_output.at[0, rows], out_send.at[b])
+        arrived(part_one.at[:, at], one_send.at[b])
+        arrived(grad_branch.at[0, rows], branch_send.at[b])
+        arrived(part_two.at[:, at], two_send.at[b])
+
+        @pl.when(late)
+        def _():
+            arrived(result.at[rows], result_send.at[b])
+
+
+def backward_all(weights, kept, row, log_sums, scales, places):
+    hidden, mixed, attended, _, (up, gate, _), branch, output = kept
+    rows, width = row.shape
+    units = up.shape[2]
+    place, start = places
+    sems = pltpu.SemaphoreType.DMA
+
+    def low_shape(*shape):
+        return jax.ShapeDtypeStruct(shape, jnp.bfloat16)
+
+    def full_shape(*shape):
+        return jax.ShapeDtypeStruct(shape, jnp.float32)
+
+    def low_vmem(*shape):
+        return pltpu.VMEM(shape, jnp.bfloat16)
+
+    def full_vmem(*shape):
+        return pltpu.VMEM(shape, jnp.float32)
+
+    anywhere = pl.BlockSpec(memory_space=pl.ANY)
+    near = pl.BlockSpec(memory_space=pltpu.VMEM)
+    one_side, two_sides = low_vmem(rows, width), low_vmem(2, rows, width)
+    return pl.pallas_call(
+        backward_kernel,
         out_shape=[
-            low_shape(width, 3 * width // 2),
-            low_shape(width // 2, width),
-            low_shape(width, units // 2),
-            low_shape(width, units // 2),
-            low_shape(units // 2, width),
-            low_shape(4, *vectors.shape),
-            low_shape(4, *valid.shape[1:]),
-            low_shape(4 * BLOCK, width),
-            low_shape(4 * BLOCK, width),
+            low_shape(2, rows, width), low_shape(2, rows, units), low_shape(2, rows, units),
+            low_shape(2, rows, width), low_shape(2, rows, 3 * width // 2), low_shape(rows, width),
+            full_shape(2, width), full_shape(2, units), full_shape(4, 2 * HEAD),
         ],
-        in_specs=[pl.BlockSpec(memory_space=pl.ANY)] * 8,
-        out_specs=[pl.BlockSpec(memory_space=pl.ANY)] * 9,
-        scratch_shapes=[
-            sems((6, 5)), sems((6, 3)), sems((6, 2)), sems((6, 2)), sems((4,)), sems((4,)),
-            sems((4,)), sems((4,)), sems, sems,
-        ],
-        compiler_params=pltpu.CompilerParams(collective_id=0, has_side_effects=True),
-    )(w_qkv, w_out, w_in, w_down, vectors, valid, tokens, cotangent)
+        in_specs=[anywhere] * 13 + [near] * 9,
+        out_specs=[anywhere] * 6 + [near] * 3,
+        scratch_shapes=[low_vmem(*weight.shape) for weight in weights]
+        + [one_side]
+        + [low_vmem(*part.shape) for part in (mixed, attended, up, gate)]
+        + [full_vmem(rows, width)] * 2
+        + [one_side, two_sides, full_vmem(rows, width), one_side, one_side, two_sides]
+        + [low_vmem(2, rows, width // 2), one_side, one_side, one_side]
+        + [full_vmem(2 * rows, 2 * rows)]
+        + [low_vmem(2 * rows, 2 * HEAD)] * 5
+        + [full_vmem(2 * rows, 2 * HEAD)] * 3
+        + [sems((12,))]
+        + [sems((4,))] * 10
+        + [sems((8,))],
+        compiler_params=pltpu.CompilerParams(
+            collective_id=2, has_side_effects=True, vmem_limit_bytes=60 * 2**20
+        ),
+    )(
+        *weights, hidden, mixed, attended, up, gate, branch, output, row, log_sums, *scales,
+        place[:, None], place[None, :], start[None, :],
+    )
 
 
 CHUNKS = 16
-
-
 BUFFERS, SEMAPHORES = 8, 18
 
 
@@ -1223,9 +1555,19 @@
     vectors = jnp.concatenate([qk_scale[0], mlp_scale[0], alphas[0]])
     vectors = jnp.pad(vectors, (0, 32 * 128 - vectors.shape[0])).reshape(32, 128)
     valid = low(jnp.pad(valid_mask[:, 0], ((0, 0), (0, 16 * 128 - group)))).reshape(2, 16, 128)
-    *weights, vectors, valid, row, row_oth = gather(
-        w_qkv[0], w_out[0], w_in[0], w_down[0], vectors, valid, tokens[:, 0], cotangent[:, 0]
-    )
+    index = jnp.arange(4 * group, dtype=jnp.int32)
+    place = (index // 256) * 256 + (((index // BLOCK) + c) % 2) * BLOCK + index % BLOCK
+    ends = jnp.cumsum(pick(lengths, micro, 0)[0])[:-1]
+    passed = place[:, None] >= ends[None, :]
+    start = jnp.max(jnp.where(passed, ends[None, :], 0), axis=1)
+    places = (place, start)
+    (
+        *weights, vectors, valid, row,
+        hidden, mixed, attended, middle, up, gate, inner, branch, output, result, log_sums,
+    ) = forward_all(
+        w_qkv[0], w_out[0], w_in[0], w_down[0], vectors, valid, tokens[:, 0], cotangent[:, 0], places
+    )
+    kept = (hidden, mixed, attended, middle, (up, gate, inner), branch, output)
     vectors = vectors.reshape(4, -1).astype(jnp.float32)
     cut_qk, cut_mlp = qk_scale.shape[1], qk_scale.shape[1] + mlp_scale.shape[1]
     all_qk = vectors[:, :cut_qk].reshape(4, 2, -1)
@@ -1233,34 +1575,32 @@
     all_alphas = vectors[:, cut_mlp : cut_mlp + alphas.shape[1]].reshape(2, 1, -1)
     mlp_half = pick(all_mlp, c, 2).reshape(2, 1, -1)
     scales = (
-        pick(all_qk, c, 1).reshape(1, -1),
+        pick(all_qk, c, 1),
         mlp_half[0],
         mlp_half[1] * math.sqrt(width),
         all_alphas[0],
         all_alphas[1],
     )
 
-    index = jnp.arange(4 * group, dtype=jnp.int32)
-    place = (index // 256) * 256 + (((index // BLOCK) + c) % 2) * BLOCK + index % BLOCK
-    ends = jnp.cumsum(pick(lengths, micro, 0)[0])[:-1]
-    passed = place[:, None] >= ends[None, :]
-    start = jnp.max(jnp.where(passed, ends[None, :], 0), axis=1)
-    places = (place, start)
     valid = pick(valid[:, :2], c, 1).reshape(-1).astype(jnp.float32)
 
-    result, _ = forward_row((row, row_oth), weights, scales, places)
-    arrived_row = along(result, [(1, 0), (2, 3)])
-    hidden_own = jnp.where(second, arrived_row, row)
-    result, kept = forward_row((hidden_own, swap(hidden_own)), weights, scales, places)
-    branch = kept[5]
     statistic = jnp.sum(valid * jnp.sum(branch * branch, axis=-1))
 
-    grad_row = row.astype(jnp.float32)
-    grad_hidden, _, _ = backward_row(grad_row, kept, weights, scales, places)
-    arrived_row = along(grad_hidden, [(0, 1), (3, 2)])
-    grad_row = jnp.where(second, grad_row, arrived_row.astype(jnp.float32))
-    grad_hidden, operands, small = backward_row(grad_row, kept, weights, scales, places)
-    g_qkv, g_out, g_up, g_gate, g_down = weight_grads(operands)
+    (
+        grad_output, grad_up, grad_gate, grad_branch, grad_mixed, grad_hidden,
+        sum_alphas, sum_scales, sum_qk,
+    ) = backward_all(weights, kept, row, log_sums, scales, places)
+    small = (sum_alphas.reshape(-1), sum_scales[0], sum_scales[1] * math.sqrt(width), sum_qk)
+
+    def weight_grad(left, right):
+        flat = [part.reshape(-1, part.shape[2]) for part in (left, right)]
+        return low(contract_rows(*flat))
+
+    g_down = weight_grad(inner, grad_output)
+    g_up = weight_grad(middle, grad_up)
+    g_gate = weight_grad(middle, grad_gate)
+    g_out = weight_grad(attended, grad_branch)
+    g_qkv = weight_grad(hidden, grad_mixed)
     g_out = g_out.reshape(4, BLOCK, 2, -1).transpose(0, 2, 1, 3).reshape(4 * 2 * BLOCK, -1)
 
     at_half = jnp.arange(2).reshape(1, 1, 2, 1) == c

time: 791 us -> 704 us (0.89)
  Pallas kernels: 459 us -> 631 us
  matrix products: 175 us -> 30.1 us
  waiting for transfers between devices: 60.7 us -> 0 us
  starting transfers between devices: 20.3 us -> 0 us
  other arithmetic: 41.2 us -> 23.5 us
  local copies, waits for them, and re-layouts: 24 us -> 12.7 us
    dot_general x38 -> x0, matrix products: 145 us -> none  [the longest x20 79.6 us: contract_cols(): lax.dot_general(left, right, (((1,), (1,)), ((), ())), preferred_element_...]
    pallas_call x5 -> x2, Pallas kernels: 211 us -> 327 us  [the longest x1 234 us: forward_all(): pl.pallas_call(forward_kernel, out_shape=[low_shape(*shape) for shape in...]
    ppermute x17 -> x0, waiting for transfers between devices: 60.7 us -> none  [the longest x2 49 us: along(): return lax.ppermute(x, 'seq', route)]
    pallas_call x1, Pallas kernels: 248 us -> 305 us  [reduce_all(): pl.pallas_call(reduce_kernel, out_shape=[low_shape(g_down.shape[0] // 2,...]
    ppermute x17 -> x0, starting transfers between devices: 20.3 us -> none  [the longest x15 17.6 us: swap(): return lax.ppermute(x, 'section', [(0, 1), (1, 0)])]
    reduce_sum x10 -> x0, other arithmetic: 12.6 us -> none  [the longest x3 6.1 us: unit(): jnp.sum(values * values, axis=-1, keepdims=True) + epsilon]
    unnamed x135 -> x40, local copies, waits for them, and re-layouts: 15.8 us -> 4.83 us
    convert_element_type x8 -> x0, other arithmetic: 8.71 us -> none  [low(): return x.astype(jnp.bfloat16)]
  transfers between devices with their start and end apart: 17 -> 0, of which waited for: 8 -> 0; matrix products, arithmetic and copies ran while one was open for 8% -> 0% of each run, Pallas kernels for 0% -> 0%
where the time goes in v3:
time: 704 us; the launch traced here: 701 us
  Pallas kernels  631 us (90%)
  matrix products  30.1 us (4%)
  other arithmetic  23.5 us (3%)
  local copies, waits for them, and re-layouts  12.7 us (2%)
    pallas_call x1, Pallas kernels, reduce_all(): pl.pallas_call(reduce_kernel, out_shape=[low_shape(g_down.shape[0] // 2,...  305 us
    pallas_call x1, Pallas kernels, forward_all(): pl.pallas_call(forward_kernel, out_shape=[low_shape(*shape) for shape in...  234 us
    pallas_call x1, Pallas kernels, backward_all(): pl.pallas_call(backward_kernel, out_shape=[low_shape(2, rows, width), low...  93 us
    dot_general x5, matrix products, contract_rows(): lax.dot_general(left, right, (((0,), (0,)), ((), ())), preferred_element_...  30.1 us

profile of v3, /device:TPU:0, one launch (start us, length us, event | category | flops | bytes accessed | tf_op | source)
XLA Modules:
  0.0 700.7 jit_solution(11137750267511604362)
XLA Ops:
  0.7 0.7 copy-done
  1.6 1.0 copy.42.start_col
  2.7 1.1 fusion.6.place_col
  3.8 0.6 fusion.24.place_row
  4.4 0.7 convert.11
  5.7 0.7 reduce.2
  6.5 0.7 reduce.3
  7.2 0.7 reduce.1
  7.9 0.6 fusion.18.vectors
  8.5 233.7 %shard_map.186 = (bf16[1024,1536]{1,0:T(8,128)(2,1)}, bf16[512,1024]{1,0:T(8,128)(2,1)}, bf16[1024,2048]{1,0:T(8,128)(2,1)}, bf16[1024,2048]{1,0:T(8,128)(2,1)},...) custom-call(bf16[256,3072]{1,0:T(8,128)(2,1)} %bitcast.113, ...), custom_call_target="tpu_custom_call" | custom-call | tf_op jit(solution)/shard_map/pallas_call | solution.py:853
  242.2 1.8 multiply_reduce_fusion
  244.0 0.7 slice.62
  245.3 0.6 pad.19.clone
  246.0 0.8 convert_bitcast_fusion
  246.8 0.6 constant_dynamic-slice_fusion.1
  249.9 93.0 %shard_map.187 = (bf16[2,512,1024]{2,1,0:T(8,128)(2,1)}, bf16[2,512,2048]{2,1,0:T(8,128)(2,1)}, bf16[2,512,2048]{2,1,0:T(8,128)(2,1)}, bf16[2,512,1024]{2,1,0:T(...) custom-call(bf16[1024,1536]{1,0:T(8,128)(2,1)} %get-tuple-element.46, ...), custom_call_target="tpu_custom_call" | custom-call | tf_op jit(solution)/shard_map/pallas_call | solution.py:1183
  342.9 0.8 slice_reduce_fusion
  343.9 0.7 broadcast_bitcast_fusion
  344.7 0.7 reshape_reshape.3
  345.5 6.9 bitcast_convert_fusion.3.g_qkv
  352.4 1.3 bitcast_convert_fusion.6
  353.6 1.0 reshape.371
  354.9 9.5 %bitcast_convert_fusion.g_gate = bf16[1024,2048]{1,0:T(8,128)(2,1)} fusion(bf16[2,512,1024]{2,1,0:T(8,128)(2,1)} %get-tuple-element.62, bf16[2,512,2048]{2,1,0:T(8,128)(2,1)} %get-tuple-element.64), kind=kOutput, calls=%fused_computation | convolution fusion | flops 4297064448 | bytes 10485760 | tf_op jit(solution)/shard_map/dot_general | solution.py:37
  364.4 6.2 bitcast_convert_fusion.1.g_up
  370.6 6.2 bitcast_convert_fusion.2.g_down
  376.8 304.6 %shard_map.188 = (bf16[1024,1024]{1,0:T(8,128)(2,1)}, bf16[256,8192]{1,0:T(8,128)(2,1)}, bf16[256,1024]{1,0:T(8,128)(2,1)S(1)}, bf16[256,3072]{1,0:T(8,128)(2,1)...) custom-call(bf16[2048,1024]{1,0:T(8,128)(2,1)} %bitcast_convert_fusion.2.g_down, ...), custom_call_target="tpu_custom_call" | custom-call | tf_op jit(solution)/shard_map/pallas_call | solution.py:1521
  681.4 6.7 bitcast_convert_fusion.4
  688.2 2.5 bitcast_convert_fusion.5
  690.6 2.0 bitcast_convert_fusion.7
  692.7 1.6 bitcast_convert_fusion.8
  694.2 1.1 bitcast_convert_fusion.9
  698.3 1.0 copy.82
  (63 shorter events, 6.8 us)
Async XLA Ops:
  0.6 0.7 copy-start
  1.6 240.6 %copy-start.9 = (s32[1024]{0:T(1024)}, s32[1024]{0:T(1024)S(1)}, u32[]{:S(2)}) copy-start(s32[1024]{0:T(1024)S(1)} %select_reduce_fusion) | copy-start | bytes 12292
  249.9 95.6 %copy-start.5 = (bf16[2,512,1024]{2,1,0:T(8,128)(2,1)S(1)}, bf16[2,512,1024]{2,1,0:T(8,128)(2,1)}, u32[]{:S(2)}) copy-start(bf16[2,512,1024]{2,1,0:T(8,128)(2,1)} %get-tuple-element.51.hidden) | copy-start | bytes 6291460
  345.5 6.9 copy-start.4
  345.5 6.9 copy-start.7
  354.8 9.5 %copy-start.11 = (bf16[2,512,2048]{2,1,0:T(8,128)(2,1)S(1)}, bf16[2,512,2048]{2,1,0:T(8,128)(2,1)}, u32[]{:S(2)}) copy-start(bf16[2,512,2048]{2,1,0:T(8,128)(2,1)} %get-tuple-element.63) | copy-start | bytes 12582916
  354.9 9.5 %copy-start.12 = (bf16[2,512,1024]{2,1,0:T(8,128)(2,1)S(1)}, bf16[2,512,1024]{2,1,0:T(8,128)(2,1)}, u32[]{:S(2)}) copy-start(bf16[2,512,1024]{2,1,0:T(8,128)(2,1)} %get-tuple-element.62) | copy-start | bytes 6291460
  364.4 6.2 copy-start.10
  364.4 6.2 copy-start.13
  370.6 6.2 copy-start.2
  370.6 6.2 copy-start.3
  681.4 6.7 copy-start.6
  688.2 2.5 copy-start.8
  692.7 6.6 copy-start.1

commit v4 on v0

--- a/solution.py
+++ b/solution.py
@@ -1,8 +1,12 @@
+import functools
 import math
+import types
 
 import jax
 import jax.numpy as jnp
 from jax import lax
+from jax.experimental import pallas as pl
+from jax.experimental.pallas import tpu as pltpu
 from jax.sharding import PartitionSpec as P
 
 HEAD = 64
@@ -254,7 +258,7 @@
     return (grad_hidden, grads)
 
 
-def per_device(
+def per_device_general(
     tokens, cotangent, lengths, valid_mask, w_qkv, w_out, w_in, w_down, qk_scale, mlp_scale, alphas
 ):
     shards = (w_qkv, w_out, w_in, w_down, qk_scale, mlp_scale, alphas)
@@ -362,6 +366,1347 @@
     )
 
 
+BLOCK = 128
+SCORE_SCALE = math.sqrt(HEAD)
+MASKED = -1e30
+
+
+def dot(left, right):
+    return jnp.dot(left, right, preferred_element_type=jnp.float32)
+
+
+def low(x):
+    return x.astype(jnp.bfloat16)
+
+
+def pick(x, index, axis):
+    return lax.dynamic_index_in_dim(x, index, axis, keepdims=False)
+
+
+def sums_of_halves(x):
+    row = lax.broadcasted_iota(jnp.int32, (2 * HEAD, 2 * HEAD), 0) // HEAD
+    col = lax.broadcasted_iota(jnp.int32, (2 * HEAD, 2 * HEAD), 1) // HEAD
+    same = (row == col).astype(jnp.bfloat16)
+    high = x.astype(jnp.bfloat16)
+    rest = (x - high.astype(jnp.float32)).astype(jnp.bfloat16)
+    return dot(high, same) + dot(rest, same)
+
+
+def normal_heads(raw):
+    factor = lax.rsqrt(sums_of_halves(raw * raw) + epsilon)
+    return raw * factor, factor
+
+
+def merge(to, own, oth):
+    for s in range(4):
+        to[s * 256 : s * 256 + BLOCK, : own.shape[1]] = own[s * BLOCK : (s + 1) * BLOCK]
+        to[s * 256 + BLOCK : (s + 1) * 256, : own.shape[1]] = oth[s * BLOCK : (s + 1) * BLOCK]
+
+
+def last_dims(left, right):
+    return lax.dot_general(left, right, (((1,), (1,)), ((), ())), preferred_element_type=jnp.float32)
+
+
+def head_lanes(h, dtype):
+    lane = lax.broadcasted_iota(jnp.int32, (1, 2 * HEAD), 1) // HEAD
+    return (lane == h).astype(dtype)
+
+
+MESH = pl.DeviceIdType.MESH
+
+
+def position():
+    c, s, f = (lax.axis_index(name) for name in ("section", "seq", "fsdp"))
+    x, y = f % 2, f // 2
+    layer = 1 - ((s + 1) // 2) % 2
+    return c, s, f, y * 2 + 1 - x, (1 - y) * 2 + x, layer
+
+
+def greet(devices):
+    barrier = pltpu.get_barrier_semaphore()
+    for device in devices:
+        pl.semaphore_signal(barrier, inc=1, device_id=device, device_id_type=MESH)
+    pl.semaphore_wait(barrier, len(devices))
+
+
+def remote(src, dst, send, recv, device):
+    return pltpu.make_async_remote_copy(
+        src_ref=src, dst_ref=dst, send_sem=send, recv_sem=recv, device_id=device, device_id_type=MESH
+    )
+
+
+def arrived(ref, sem):
+    pltpu.make_async_copy(ref, ref, sem).wait()
+
+
+def lane(offset):
+    return pl.multiple_of(offset, 128)
+
+
+def every(count, work):
+    def step(n, carry):
+        work(n)
+        return carry
+
+    lax.fori_loop(0, count, step, 0)
+
+
+def silu(x):
+    return x * jax.nn.sigmoid(x)
+
+
+def row_sums(x, lanes):
+    high = low(x)
+    rest = low(x - high.astype(jnp.float32))
+    return last_dims(lanes, high) + last_dims(lanes, rest)
+
+
+class Flow:
+    def __init__(self, buffers, semaphores):
+        (
+            self.near_own, self.near_far, self.far_in, self.own, self.passing,
+            self.from_left, self.from_right, self.pair_sum,
+        ) = buffers
+        (
+            self.load_own, self.load_pass, self.send_own, self.recv_own, self.send_far,
+            self.recv_far, self.send_next, self.recv_next, self.send_z, self.recv_left,
+            self.recv_right, self.recv_pair, self.send_on, self.send_back, self.send_out,
+            self.keep, self.give, self.given,
+        ) = [semaphores.at[n] for n in range(VECTOR_SEMAPHORES)]
+        self.place_of = position()
+
+    def begin(self, source):
+        c, s, f, fx, fy, _ = self.place_of
+        to = (c, s, fx)
+        remote(source(fx), self.near_own, self.send_own, self.recv_own, to).start()
+        remote(source(3 - f), self.near_far, self.send_far, self.recv_far, to).start()
+        pltpu.make_async_copy(source(fy), self.passing, self.load_pass).start()
+        pltpu.make_async_copy(source(f), self.own, self.load_own).start()
+
+    def pass_on(self):
+        c, s, _, _, fy, _ = self.place_of
+        arrived(self.passing, self.load_pass)
+        arrived(self.near_far, self.recv_far)
+        add(self.passing, self.passing, self.near_far)
+        remote(self.passing, self.far_in, self.send_next, self.recv_next, (c, s, fy)).start()
+
+    def finish_plane(self):
+        c, s, f, _, _, _ = self.place_of
+        own, send = self.own, self.send_z
+        arrived(own, self.load_own)
+        arrived(self.near_own, self.recv_own)
+        arrived(self.far_in, self.recv_next)
+        add(own, own, self.near_own, self.far_in)
+
+        @pl.when(s == 0)
+        def _():
+            remote(own, self.from_left, send, self.recv_left, (c, 1, f)).start()
+
+        @pl.when(s == 3)
+        def _():
+            remote(own, self.from_right, send, self.recv_right, (c, 2, f)).start()
+
+        @pl.when((s == 1) | (s == 2))
+        def _():
+            remote(own, self.pair_sum, send, self.recv_pair, (c, 3 - s, f)).start()
+
+    def middle_planes(self):
+        c, s, f, _, _, _ = self.place_of
+        left, right, pair = self.from_left, self.from_right, self.pair_sum
+
+        @pl.when(s == 1)
+        def _():
+            arrived(left, self.recv_left)
+            remote(left, left, self.send_on, self.recv_left, (c, 2, f)).start()
+
+        @pl.when(s == 2)
+        def _():
+            arrived(right, self.recv_right)
+            remote(right, right, self.send_on, self.recv_right, (c, 1, f)).start()
+
+        @pl.when((s == 1) | (s == 2))
+        def _():
+            arrived(pair, self.recv_pair)
+            arrived(pair, self.send_z)
+            add(pair, pair, self.own)
+            remote(pair, pair, self.send_out, self.recv_pair, (c, (s - 1) * 3, f)).start()
+
+    def all_planes(self, dst):
+        c, s, f, _, _, _ = self.place_of
+        left, right, pair = self.from_left, self.from_right, self.pair_sum
+        own, total = self.own, self.near_own
+
+        @pl.when(s == 1)
+        def _():
+            arrived(right, self.recv_right)
+            remote(right, right, self.send_back, self.recv_right, (c, 0, f)).start()
+
+        @pl.when(s == 2)
+        def _():
+            arrived(left, self.recv_left)
+            remote(left, left, self.send_back, self.recv_left, (c, 3, f)).start()
+
+        @pl.when((s == 1) | (s == 2))
+        def _():
+            add(total, left, right)
+
+        @pl.when(s == 0)
+        def _():
+            arrived(pair, self.recv_pair)
+            arrived(right, self.recv_right)
+            add(total, own, right)
+
+        @pl.when(s == 3)
+        def _():
+            arrived(pair, self.recv_pair)
+            arrived(left, self.recv_left)
+            add(total, own, left)
+
+        for owner, chunk in ((0, pair), (1, total)):
+
+            @pl.when(c == owner)
+            def _():
+                pltpu.make_async_copy(chunk, dst, self.keep).start()
+
+            @pl.when(c != owner)
+            def _():
+                remote(chunk, dst, self.give, self.given, (1 - c, s, f)).start()
+
+    def settle(self):
+        _, s, _, _, _, _ = self.place_of
+        for sem in (
+            self.send_own, self.send_far, self.send_next, self.keep, self.give, self.given
+        ):
+            arrived(self.own, sem)
+
+        @pl.when((s == 1) | (s == 2))
+        def _():
+            for sem in (self.send_on, self.send_back, self.send_out):
+                arrived(self.own, sem)
+
+        @pl.when((s == 0) | (s == 3))
+        def _():
+            arrived(self.own, self.send_z)
+
+
+def add(to, *refs):
+    total = refs[0][...].astype(jnp.float32)
+    for ref in refs[1:]:
+        total = total + ref[...].astype(jnp.float32)
+    to[...] = total.astype(to.dtype)
+
+
+VECTOR_SEMAPHORES = 18
+CHUNKS = 16
+READY = 4
+AHEAD = 3
+INPUTS = 11
+OUTPUTS = 19
+
+
+def scratch_of(width, units, vector_rows, flag_rows):
+    rows = 4 * BLOCK
+    half = units // 2
+
+    def low_vmem(*shape):
+        return pltpu.VMEM(shape, jnp.bfloat16)
+
+    def full_vmem(*shape):
+        return pltpu.VMEM(shape, jnp.float32)
+
+    def sems(*shape):
+        return pltpu.SemaphoreType.DMA(shape)
+
+    low_row, full_row, low_rows = low_vmem(rows, width), full_vmem(rows, width), low_vmem(2, rows, width)
+    pair, pair_full = low_vmem(2 * rows, 2 * HEAD), full_vmem(2 * rows, 2 * HEAD)
+    return dict(
+        wq=low_vmem(width, 3 * width // 2), wo=low_vmem(width // 2, width),
+        wu=low_vmem(width, half), wg=low_vmem(width, half), wd=low_vmem(half, width),
+        vec=low_vmem(4, vector_rows, 128), flat=full_vmem(4, vector_rows, 128),
+        flags=low_vmem(4, flag_rows, 128), flags_full=full_vmem(4, flag_rows, 128),
+        scale_up=full_vmem(1, half), scale_gate=full_vmem(1, half),
+        alpha_attn=full_vmem(1, width), alpha_mlp=full_vmem(1, width),
+        hid=low_rows, mixed=low_vmem(2, rows, 3 * width // 2), att=low_vmem(2, rows, width // 2),
+        mid=low_rows, up=low_vmem(2, rows, half), gate=low_vmem(2, rows, half),
+        inner=low_vmem(2, rows, half), branch=full_row, middle=full_row, output=full_row,
+        result=low_row, part=low_row, got=low_row,
+        bias=full_vmem(2 * rows, 2 * rows), raw=pair, queries=pair, keys=pair,
+        values=low_vmem(2 * rows, 4 * HEAD), grads=pair, dq=pair_full, dk=pair_full, dv=pair_full,
+        log_sums=full_vmem(4, 2, 2 * rows),
+        grad_in=low_row, grad_rows=low_rows,
+        sum_alphas=full_vmem(2, width), sum_scales=full_vmem(2, half), sum_qk=full_vmem(4, 2 * HEAD),
+        sum_valid=full_vmem(1, 128), terms=full_vmem(4, 24, 128),
+        v0=full_vmem(24, 128), v1=full_vmem(24, 128), v2=full_vmem(24, 128), v3=full_vmem(24, 128),
+        v4=full_vmem(24, 128), v5=full_vmem(24, 128), v6=full_vmem(24, 128), v7=full_vmem(24, 128),
+        first_send=sems(6, 5), first_recv=sems(6, 3), next_send=sems(6, 2), next_recv=sems(6, 2),
+        row_send=sems(4), row_recv=sems(4), flag_send=sems(4), flag_recv=sems(4),
+        own_recv=sems(4), oth_send=sems(4), oth_recv=sems(4),
+        part_send=sems(4, 4), part_recv=sems(4, 4),
+        mid_send=sems(3, 4), mid_recv=sems(3, 4), result_send=sems(4), grad_recv=sems(4),
+        owner_send=sems(2, 4), owner_recv=sems(2, 2, 2),
+        vector=sems(VECTOR_SEMAPHORES), staged=sems(2), load=sems(9, 4),
+        send_own=sems(CHUNKS), recv_own=sems(CHUNKS), send_far=sems(CHUNKS), recv_far=sems(CHUNKS),
+        send_next=sems(CHUNKS), recv_next=sems(CHUNKS), send_z=sems(CHUNKS), stored=sems(CHUNKS),
+        recv_left=sems(CHUNKS), recv_right=sems(CHUNKS), recv_pair=sems(CHUNKS),
+        send_on=sems(CHUNKS), send_back=sems(CHUNKS), send_out=sems(CHUNKS),
+        keep=sems(CHUNKS), give=sems(CHUNKS), given=sems(CHUNKS),
+    )
+
+
+def relay_kernel(names, *refs):
+    (
+        w_qkv, w_out, w_in, w_down, vectors, valid, tokens, cotangent,
+        start_col, place_row, start_row,
+    ) = refs[:INPUTS]
+    (
+        o_down, o_in, o_out, o_qkv, o_vectors, o_hidden, o_grad, o_row,
+        g_down, g_up, g_gate, g_out, g_qkv,
+        near_own, near_far, far_in, from_left, from_right, pair_sum,
+    ) = refs[INPUTS : INPUTS + OUTPUTS]
+    plane_sum, *refs = refs[INPUTS + OUTPUTS :]
+    r = types.SimpleNamespace(**dict(zip(names, refs)))
+    c, s, f, fx, fy, layer = position()
+    sibling = (1 - c, s, f)
+    early, late = layer == 0, layer == 1
+    late_plane = (c, (s - 1) * 3, f)
+    early_plane = (c, s // 3 + 1, f)
+    width = w_out.shape[1]
+    full = jnp.float32
+    greet(
+        [sibling, (c, s, fx), (1 - c, s, fx), (c, s, fy), (1 - c, s, fy)]
+        + [(core, (s + step) % 4, f) for core in (0, 1) for step in (1, 2, 3)]
+    )
+
+    def rows_of(b):
+        return pl.ds(b * BLOCK, BLOCK)
+
+    def columns(n):
+        return pl.ds(lane(n * 256), 256)
+
+    for to, held in enumerate((cotangent.at[0], tokens.at[0], tokens.at[1], cotangent.at[1])):
+        src = held.at[pl.ds(c * BLOCK, BLOCK)]
+        dst = o_row.at[rows_of(s)]
+        flags, flags_to = valid.at[to // 2], r.flags.at[s]
+
+        @pl.when(s == to)
+        def _():
+            pltpu.make_async_copy(src, dst, r.row_recv.at[s]).start()
+            pltpu.make_async_copy(flags, flags_to, r.flag_recv.at[s]).start()
+
+        @pl.when(s != to)
+        def _():
+            remote(src, dst, r.row_send.at[to], r.row_recv.at[s], (c, to, f)).start()
+            remote(flags, flags_to, r.flag_send.at[to], r.flag_recv.at[s], (c, to, f)).start()
+
+    def pieces(item, h):
+        if item == 0:
+            return [(vectors, r.vec.at[f])]
+        if item == 1:
+            return [
+                (
+                    w_qkv.at[:, pl.ds(lane(part * 256 + h * 128), 128)],
+                    r.wq.at[pl.ds(f * 256, 256), pl.ds(part * 128, 128)],
+                )
+                for part in range(12)
+            ]
+        if item == 2:
+            return [(w_out.at[pl.ds(h * 128, 128)], r.wo.at[pl.ds(f * 128, 128)])]
+        if item in (3, 4):
+            to = (r.wu, r.wg)[item - 3]
+            return [
+                (
+                    w_in.at[:, pl.ds(lane((item - 3) * 4096 + part * 1024 + h * 512), 512)],
+                    to.at[pl.ds(f * 256, 256), pl.ds(part * 512, 512)],
+                )
+                for part in range(4)
+            ]
+        return [(w_down.at[pl.ds(h * 512, 512)], r.wd.at[pl.ds(f * 512, 512)])]
+
+    weights = (r.vec, r.wq, r.wo, r.wu, r.wg, r.wd)
+
+    def block(item, of):
+        if item == 0:
+            return r.vec.at[of]
+        rows = weights[item].shape[0] // 4
+        return weights[item].at[pl.ds(of * rows, rows)]
+
+    def part_of(item, of, part):
+        if item == 0:
+            return r.vec.at[of, pl.ds(part * 16, 16)]
+        rows = weights[item].shape[0] // 8
+        return weights[item].at[pl.ds(of * 2 * rows + part * rows, rows)]
+
+    targets = (
+        ((c, s, fx), c, 1), ((c, s, fy), c, 2), ((1 - c, s, fx), 1 - c, 1),
+        ((1 - c, s, fy), 1 - c, 2), (sibling, 1 - c, 0),
+    )
+
+    def spread(*items):
+        @pl.when(c == layer)
+        def _():
+            for item in items:
+                for index, (device, h, came) in enumerate(targets):
+                    for src, dst in pieces(item, h):
+                        remote(
+                            src, dst, r.first_send.at[item, index], r.first_recv.at[item, came],
+                            device,
+                        ).start()
+                for src, dst in pieces(item, c):
+                    pltpu.make_async_copy(src, dst, r.first_recv.at[item, 0]).start()
+
+    def relay(item):
+        for part, (came, of, to) in enumerate(((1, fx, fy), (2, fy, fx))):
+            arrived(block(item, of), r.first_recv.at[item, came])
+            moved = part_of(item, of, part)
+            remote(
+                moved, moved, r.next_send.at[item, part], r.next_recv.at[item, part], (c, s, to)
+            ).start()
+
+    def complete(item):
+        arrived(block(item, f), r.first_recv.at[item, 0])
+        for part in range(2):
+            arrived(part_of(item, 3 - f, part), r.next_recv.at[item, part])
+
+    spread(0, 1, 2, 3)
+    index = lax.broadcasted_iota(jnp.int32, (8 * BLOCK, 1), 0)
+    place_col = (index // 256) * 256 + (index // BLOCK + c) % 2 * BLOCK + index % BLOCK
+    fits = (place_row[...] >= start_col[...]) & (place_row[...] <= place_col)
+    r.bias[...] = jnp.where(fits, 0.0, MASKED)
+    r.values[:, 2 * HEAD :] = jnp.ones_like(r.values[:, 2 * HEAD :])
+    for sums in (r.sum_alphas, r.sum_scales, r.sum_valid, r.terms):
+        sums[...] = jnp.zeros_like(sums)
+    relay(0)
+    relay(1)
+    spread(4)
+    relay(2)
+
+    def to_sibling(b, src):
+        remote(src, r.hid.at[1, rows_of(b)], r.oth_send.at[b], r.oth_recv.at[b], sibling).start()
+
+    @pl.when(early)
+    def _():
+        for b in range(4):
+            held = o_row.at[rows_of(b)]
+            arrived(held, r.row_recv.at[b])
+            pltpu.make_async_copy(held, r.hid.at[0, rows_of(b)], r.own_recv.at[b]).start()
+            to_sibling(b, held)
+        for b in range(4):
+            arrived(r.hid.at[0, rows_of(b)], r.own_recv.at[b])
+
+    @pl.when(late)
+    def _():
+        relay(3)
+        spread(5)
+        relay(4)
+        relay(5)
+        for b in range(4):
+            held = o_row.at[rows_of(b)]
+            arrived(held, r.row_recv.at[b])
+            pltpu.make_async_copy(held, r.grad_in.at[rows_of(b)], r.grad_recv.at[b]).start()
+        for b in range(4):
+            arrived(r.hid.at[0, rows_of(b)], r.own_recv.at[b])
+            to_sibling(b, r.hid.at[0, rows_of(b)])
+
+    complete(0)
+    r.flat[...] = r.vec[...].astype(full)
+    for n in range(4):
+        for j in range(4):
+            at = slice(n * 512 + j * 128, n * 512 + (j + 1) * 128)
+            row = pl.ds(2 + (n % 2) * 8 + j + c * 4, 1)
+            r.scale_up[:, at] = r.flat[n // 2, row, :]
+            r.scale_gate[:, at] = r.flat[2 + n // 2, row, :] * math.sqrt(width)
+    for n in range(2):
+        for j in range(4):
+            at = slice(n * 512 + j * 128, n * 512 + (j + 1) * 128)
+            r.alpha_attn[:, at] = r.flat[n, 18 + j : 19 + j, :]
+            r.alpha_mlp[:, at] = r.flat[2 + n, 18 + j : 19 + j, :]
+
+    complete(1)
+    for side in range(2):
+        if side:
+            for b in range(4):
+                arrived(r.hid.at[1, rows_of(b)], r.oth_recv.at[b])
+
+        def mix(n, side=side):
+            at = pl.ds(lane(n * 512), 512)
+            r.mixed[side, :, at] = low(dot(r.hid[side], r.wq[:, at]))
+
+        every(3, mix)
+
+    first = (lax.broadcasted_iota(jnp.int32, (8, 2 * HEAD), 1) == 0).astype(jnp.bfloat16)
+
+    def lanes_of(pair, part):
+        return pl.ds(lane(part * (width // 2) + pair * 2 * HEAD), 2 * HEAD)
+
+    def normal(pair, part):
+        at = lanes_of(pair, part)
+        merge(r.raw, r.mixed[0, :, at], r.mixed[1, :, at])
+        return normal_heads(r.raw[...].astype(full))
+
+    def prepare(pair):
+        scale = r.flat[pair, pl.ds(c, 1), :]
+        r.queries[...] = low(normal(pair, 0)[0] * scale) * SCORE_SCALE
+        r.keys[...] = low(normal(pair, 1)[0] * scale)
+        at = lanes_of(pair, 2)
+        merge(r.values, r.mixed[0, :, at], r.mixed[1, :, at])
+
+    def of_heads(block):
+        return jnp.concatenate([block * head_lanes(h, jnp.bfloat16) for h in range(2)])
+
+    def attend(pair):
+        @pl.when(early & (pair == 2))
+        def _():
+            relay(3)
+            spread(5)
+
+        prepare(pair)
+        at = lanes_of(pair, 0)
+        for q in range(4):
+            upto = (q + 1) * 256
+            query = of_heads(r.queries[q * 256 : upto])
+            summed = 0.0
+            for k in range(q + 1):
+                at_keys = slice(k * 256, (k + 1) * 256)
+                mask = jnp.concatenate([r.bias[q * 256 : upto, at_keys]] * 2)
+                weighted = jnp.exp(last_dims(query, r.keys[at_keys]) + mask)
+                summed = summed + dot(low(weighted), r.values[at_keys])
+            total = summed[:, 2 * HEAD :]
+            parts = summed[:, : 2 * HEAD] / total
+            log_sum = jnp.log(row_sums(total, first)[:1])
+            for h in range(2):
+                r.log_sums[pair, h : h + 1, q * 256 : upto] = log_sum[:, h * 256 : (h + 1) * 256]
+            joined = low(jnp.where(head_lanes(0, full) > 0, parts[:256], parts[256:]))
+            r.att[0, q * BLOCK : (q + 1) * BLOCK, at] = joined[:BLOCK]
+            r.att[1, q * BLOCK : (q + 1) * BLOCK, at] = joined[BLOCK:]
+
+    every(4, attend)
+
+    def exchange(index, product, to):
+        send, recv = r.part_send.at[index], r.part_recv.at[index]
+
+        def sent(n):
+            at = columns(n)
+            r.part[:, at] = low(product(1, n))
+            remote(r.part.at[:, at], r.got.at[:, at], send.at[n], recv.at[n], sibling).start()
+
+        def own(n):
+            at = columns(n)
+            to[:, at] = product(0, n) if to is not r.middle else to[:, at] + product(0, n)
+
+        every(4, sent)
+        every(4, own)
+        for n in range(4):
+            arrived(r.got.at[:, columns(n)], recv.at[n])
+
+    def settle_sent(index):
+        for n in range(4):
+            arrived(r.part.at[:, columns(n)], r.part_send.at[index, n])
+
+    def share_rows(array, index, b):
+        @pl.when(b % 2 == 1)
+        def _():
+            rows = rows_of(b // 2)
+            remote(
+                array.at[0, rows], array.at[1, rows], r.mid_send.at[index, b // 2],
+                r.mid_recv.at[index, b // 2], sibling,
+            ).start()
+
+    def shared(array, index):
+        for b in range(4):
+            arrived(array.at[1, rows_of(b)], r.mid_recv.at[index, b])
+
+    def settle_shared(array, index):
+        for b in range(4):
+            arrived(array.at[0, rows_of(b)], r.mid_send.at[index, b])
+
+    complete(2)
+    exchange(
+        0, lambda side, n: dot(r.att[side], r.wo[:, columns(n)]), r.branch,
+    )
+
+    def first_step(b):
+        rows = pl.ds(b * 64, 64)
+        total = r.branch[rows] + r.got[rows].astype(full)
+        r.branch[rows] = total
+        hidden = r.hid[0, rows].astype(full)
+        stepped = unit(hidden + r.alpha_attn[...] * (unit(total) - hidden))
+        r.middle[rows] = stepped
+        r.mid[0, rows] = low(stepped)
+        share_rows(r.mid, 0, b)
+
+    every(8, first_step)
+
+    @pl.when(early)
+    def _():
+        relay(4)
+
+    complete(3)
+    for side in range(2):
+        if side:
+            shared(r.mid, 0)
+
+        def lift(n, side=side):
+            at = pl.ds(lane(n * 512), 512)
+            r.up[side, :, at] = low(dot(r.mid[side], r.wu[:, at]))
+
+        every(4, lift)
+
+    @pl.when(early)
+    def _():
+        relay(5)
+
+    complete(4)
+    for side in (1, 0):
+
+        def open_gate(n, side=side):
+            at = pl.ds(lane(n * 512), 512)
+            gate = dot(r.mid[side], r.wg[:, at])
+            r.gate[side, :, at] = low(gate)
+            upward = r.up[side, :, at].astype(full) * r.scale_up[:, at]
+            r.inner[side, :, at] = low(upward * silu(gate * r.scale_gate[:, at]))
+
+        every(4, open_gate)
+
+    complete(5)
+    settle_sent(0)
+    exchange(
+        1, lambda side, n: dot(r.inner[side], r.wd[:, columns(n)]), r.output,
+    )
+
+    def second_step(b):
+        rows = pl.ds(b * 64, 64)
+        total = r.output[rows] + r.got[rows].astype(full)
+        r.output[rows] = total
+        start = r.middle[rows]
+        r.result[rows] = low(unit(start + r.alpha_mlp[...] * (unit(total) - start)))
+
+        @pl.when(early & (b % 2 == 1))
+        def _():
+            sent = rows_of(b // 2)
+            remote(
+                r.result.at[sent], r.hid.at[0, sent], r.result_send.at[b // 2],
+                r.own_recv.at[b // 2], late_plane,
+            ).start()
+
+    every(8, second_step)
+
+    def to_owners(array, held, to_ref):
+        for to in range(4):
+            src = held.at[rows_of(to)]
+            dst = to_ref.at[s // 2, pl.ds(c * BLOCK, BLOCK)]
+            recv = r.owner_recv.at[array, s // 2, c]
+            here = (s == to) & (c == layer)
+
+            @pl.when(here)
+            def _():
+                pltpu.make_async_copy(src, dst, r.owner_send.at[array, to]).start()
+
+            @pl.when(jnp.logical_not(here))
+            def _():
+                remote(src, dst, r.owner_send.at[array, to], recv, (layer, to, f)).start()
+
+    to_owners(0, r.result, o_hidden)
+
+    for b in range(4):
+        arrived(r.flags.at[b], r.flag_recv.at[b])
+    r.flags_full[...] = r.flags[...].astype(full)
+    ones = jnp.ones((8, width), jnp.bfloat16)
+    for b in range(4):
+        squares = row_sums(r.branch[rows_of(b)] * r.branch[rows_of(b)], ones)[:1]
+        r.sum_valid[...] += squares * r.flags_full[b, pl.ds(c, 1), :]
+
+    def near_of(k):
+        return fx + (fy - fx) * (k % 2)
+
+    def far_of(k):
+        return fy + (fx - fy) * (k % 2)
+
+    def with_source(k, work):
+        @pl.when(k < 4)
+        def _():
+            at = pl.ds(lane((k % 2) * 512), 512)
+            work(lambda to: g_down.at[pl.ds(to * 512 + (k // 2) * 256, 256), at])
+
+        for begins, ref in ((4, g_up), (8, g_gate), (12, g_out), (13, g_qkv)):
+
+            @pl.when((k >= begins) & (k < begins + ref.shape[1] // 512))
+            def _():
+                at = pl.ds(lane((k - begins) * 512), 512)
+                work(lambda to: ref.at[pl.ds(to * 256, 256), at])
+
+    def begin(k):
+        def start(source):
+            to = (c, s, near_of(k))
+            remote(
+                source(near_of(k)), near_own.at[k], r.send_own.at[k], r.recv_own.at[k], to
+            ).start()
+            remote(source(3 - f), near_far.at[k], r.send_far.at[k], r.recv_far.at[k], to).start()
+
+        with_source(k, start)
+
+    places = {
+        "pass": (r.wu, 0, 4), "own": (r.wu, 4, 4), "pair": (r.wu, 8, 4), "far": (r.wu, 12, 2),
+        "other": (r.wu, 14, 2), "late": (r.wg, 0, 4), "near": (r.wg, 4, 2), "last": (r.wg, 6, 2),
+        "side": (r.wg, 8, 2),
+    }
+    order = list(places)
+
+    def slot(name, k):
+        ref, base, count = places[name]
+        n = base + k % count
+        return ref.at[pl.ds(n // 4 * 256, 256), pl.ds(lane(n % 4 * 512), 512)]
+
+    def load_sem(name, k):
+        return r.load.at[order.index(name), k % places[name][2]]
+
+    def fetch(src, name, k):
+        pltpu.make_async_copy(src, slot(name, k), load_sem(name, k)).start()
+
+    def fetched(name, k):
+        arrived(slot(name, k), load_sem(name, k))
+
+    def again(k, work):
+        pl.when(k >= 4)(work)
+
+    def pass_load(k):
+        arrived(near_far.at[k], r.recv_far.at[k])
+
+        again(k, lambda: arrived(slot("pass", k), r.send_next.at[k - 4]))
+        with_source(k, lambda source: fetch(source(far_of(k)), "pass", k))
+        fetch(near_far.at[k], "far", k)
+
+    def pass_send(k):
+        fetched("pass", k)
+        fetched("far", k)
+        total = slot("pass", k)
+        add(total, total, slot("far", k))
+        remote(
+            total, far_in.at[k], r.send_next.at[k], r.recv_next.at[k], (c, s, far_of(k))
+        ).start()
+
+    def plane_load(k):
+        arrived(near_own.at[k], r.recv_own.at[k])
+        arrived(far_in.at[k], r.recv_next.at[k])
+
+        again(k, lambda: arrived(slot("own", k), r.send_z.at[k - 4]))
+        with_source(k, lambda source: fetch(source(f), "own", k))
+        fetch(near_own.at[k], "near", k)
+        fetch(far_in.at[k], "last", k)
+
+    def plane_send(k):
+        for name in ("own", "near", "last"):
+            fetched(name, k)
+        own, send = slot("own", k), r.send_z.at[k]
+        add(own, own, slot("near", k), slot("last", k))
+        pltpu.make_async_copy(own, plane_sum.at[k], r.stored.at[k]).start()
+
+        @pl.when(s == 0)
+        def _():
+            remote(own, from_left.at[k], send, r.recv_left.at[k], (c, 1, f)).start()
+
+        @pl.when(s == 3)
+        def _():
+            remote(own, from_right.at[k], send, r.recv_right.at[k], (c, 2, f)).start()
+
+        @pl.when(early)
+        def _():
+            remote(own, pair_sum.at[k], send, r.recv_pair.at[k], (c, 3 - s, f)).start()
+
+    def plane_done(k):
+        arrived(plane_sum.at[k], r.stored.at[k])
+
+    def in_plane(t, least, most, slack):
+        for lag, work in (
+            (0, pass_load), (1, pass_send), (5 + slack, plane_done), (3 + slack, plane_load),
+            (4 + slack, plane_send),
+        ):
+            @pl.when((t >= lag + least) & (t < lag + most))
+            def _():
+                work(t - lag)
+
+    def relay_on(k):
+        @pl.when(s == 1)
+        def _():
+            arrived(from_left.at[k], r.recv_left.at[k])
+            remote(
+                from_left.at[k], from_left.at[k], r.send_on.at[k], r.recv_left.at[k], (c, 2, f)
+            ).start()
+
+        @pl.when(s == 2)
+        def _():
+            arrived(from_right.at[k], r.recv_right.at[k])
+            remote(
+                from_right.at[k], from_right.at[k], r.send_on.at[k], r.recv_right.at[k], (c, 1, f)
+            ).start()
+
+    def relay_out(k):
+        @pl.when(s == 1)
+        def _():
+            arrived(from_right.at[k], r.recv_right.at[k])
+            remote(
+                from_right.at[k], from_right.at[k], r.send_back.at[k], r.recv_right.at[k], (c, 0, f)
+            ).start()
+
+        @pl.when(s == 2)
+        def _():
+            arrived(from_left.at[k], r.recv_left.at[k])
+            remote(
+                from_left.at[k], from_left.at[k], r.send_back.at[k], r.recv_left.at[k], (c, 3, f)
+            ).start()
+
+    def everything(chunk):
+        return chunk
+
+    def place(k, owner, chunk):
+        def put(pieces):
+            for src, dst in pieces:
+
+                @pl.when(c == owner)
+                def _():
+                    pltpu.make_async_copy(src(chunk), dst, r.keep.at[k]).start()
+
+                @pl.when(c != owner)
+                def _():
+                    remote(src(chunk), dst, r.give.at[k], r.given.at[k], sibling).start()
+
+        @pl.when(k < 4)
+        def _():
+            rows = pl.ds(c * 512 + (k // 2) * 256, 256)
+            put([(everything, o_down.at[rows, pl.ds(lane((k % 2) * 512), 512)])])
+
+        @pl.when((k >= 4) & (k < 12))
+        def _():
+            put([(everything, o_in.at[:, pl.ds(lane((k - 4) * 1024 + c * 512), 512)])])
+
+        @pl.when(k == 12)
+        def _():
+            put([
+                (
+                    lambda chunk, part=part: chunk.at[pl.ds(part * 128, 128)],
+                    o_out.at[pl.ds(c * 128, 128), pl.ds(part * 512, 512)],
+                )
+                for part in range(2)
+            ])
+
+        @pl.when(k > 12)
+        def _():
+            put([
+                (
+                    lambda chunk, part=part: chunk.at[:, pl.ds(part * 128, 128)],
+                    o_qkv.at[:, pl.ds(lane((k - 13) * 1024 + part * 256 + c * 128), 128)],
+                )
+                for part in range(4)
+            ])
+
+    def placed(k, owner):
+        @pl.when(c == owner)
+        def _():
+            arrived(plane_sum.at[k], r.keep.at[k])
+
+        @pl.when(c != owner)
+        def _():
+            arrived(plane_sum.at[k], r.give.at[k])
+
+    def pair_load(k):
+        @pl.when(early)
+        def _():
+            arrived(pair_sum.at[k], r.recv_pair.at[k])
+
+            @pl.when(k >= 4)
+            def _():
+                arrived(slot("pair", k), r.send_out.at[k - 4])
+                placed(k - 4, 0)
+
+            fetch(plane_sum.at[k], "pair", k)
+            fetch(pair_sum.at[k], "other", k)
+
+    def pair_send(k):
+        @pl.when(early)
+        def _():
+            fetched("pair", k)
+            fetched("other", k)
+            total = slot("pair", k)
+            add(total, total, slot("other", k))
+            remote(total, pair_sum.at[k], r.send_out.at[k], r.recv_pair.at[k], late_plane).start()
+            place(k, 0, total)
+
+    def pair_take(k):
+        @pl.when(late)
+        def _():
+            arrived(pair_sum.at[k], r.recv_pair.at[k])
+            place(k, 0, pair_sum.at[k])
+
+    def late_load(k):
+        again(k, lambda: placed(k - 4, 1))
+
+        @pl.when(early)
+        def _():
+            fetch(from_left.at[k], "late", k)
+            fetch(from_right.at[k], "side", k)
+
+        @pl.when(s == 0)
+        def _():
+            arrived(from_right.at[k], r.recv_right.at[k])
+            fetch(from_right.at[k], "side", k)
+
+        @pl.when(s == 3)
+        def _():
+            arrived(from_left.at[k], r.recv_left.at[k])
+            fetch(from_left.at[k], "side", k)
+
+        @pl.when(late)
+        def _():
+            fetch(plane_sum.at[k], "late", k)
+
+    def late_place(k):
+        fetched("late", k)
+        fetched("side", k)
+        total = slot("late", k)
+        add(total, total, slot("side", k))
+        place(k, 1, total)
+
+    def between_planes(t):
+        @pl.when(early)
+        def _():
+            for lag, work in ((1, relay_on), (3, relay_out)):
+                @pl.when((t >= lag + READY) & (t < lag + CHUNKS))
+                def _():
+                    work(t - lag)
+
+        for lag, work, least, most in (
+            (4, pair_load, 0, READY), (5, pair_send, 0, READY), (8, pair_load, READY, CHUNKS),
+            (9, pair_send, READY, CHUNKS), (18, pair_take, 0, CHUNKS),
+            (6 + 8 * layer, late_load, 0, CHUNKS), (7 + 8 * layer, late_place, 0, CHUNKS),
+        ):
+            @pl.when((t >= lag + least) & (t < lag + most))
+            def _():
+                work(t - lag)
+
+    def weight_grad(count, tile, width_of, pieces):
+        def stage(n):
+            return r.wd.at[pl.ds((n % 2) * 256, 256), pl.ds(0, width_of)]
+
+        def work(n):
+            @pl.when(n >= 2)
+            def _():
+                arrived(stage(n), r.staged.at[n % 2])
+
+            left, right = tile(n)
+            total = contract_rows(left(0), right(0)) + contract_rows(left(1), right(1))
+            stage(n)[...] = low(total)
+            for src, dst in pieces(n, stage(n)):
+                pltpu.make_async_copy(src, dst, r.staged.at[n % 2]).start()
+
+        every(count, work)
+        for n in range(count - 2, count):
+            arrived(stage(n), r.staged.at[n % 2])
+
+    def grad_of_down():
+        weight_grad(
+            8,
+            lambda n: (lambda side: r.inner[side, :, columns(n)], lambda side: r.grad_rows[side]),
+            width,
+            lambda n, src: [(src, g_down.at[pl.ds(n * 256, 256)])],
+        )
+
+    def grad_of_lift(ref, to):
+        weight_grad(
+            8,
+            lambda n: (
+                lambda side: r.mid[side, :, columns(n // 2)],
+                lambda side: ref[side, :, pl.ds(lane((n % 2) * 1024), 1024)],
+            ),
+            1024,
+            lambda n, src: [
+                (src, to.at[pl.ds((n // 2) * 256, 256), pl.ds(lane((n % 2) * 1024), 1024)])
+            ],
+        )
+
+    def grad_of_out():
+        weight_grad(
+            2,
+            lambda n: (lambda side: r.att[side, :, columns(n)], lambda side: r.grad_rows[side]),
+            width,
+            lambda n, src: [
+                (
+                    src.at[pl.ds(owner * 128, 128), pl.ds(part * 512, 512)],
+                    g_out.at[pl.ds(n * 512 + owner * 256 + part * 128, 128)],
+                )
+                for owner in range(2)
+                for part in range(2)
+            ],
+        )
+
+    def grad_of_qkv():
+        weight_grad(
+            12,
+            lambda n: (
+                lambda side: r.hid[side, :, columns(n // 3)],
+                lambda side: r.mixed[side, :, pl.ds(lane((n % 3) * 512), 512)],
+            ),
+            512,
+            lambda n, src: [
+                (src, g_qkv.at[pl.ds((n // 3) * 256, 256), pl.ds(lane((n % 3) * 512), 512)])
+            ],
+        )
+
+    fits = (place_col >= start_row[...]) & (place_col <= place_row[...])
+    r.bias[...] = jnp.where(fits, 0.0, MASKED)
+    for item in range(6):
+        for part in range(2):
+            arrived(part_of(item, f, part), r.next_send.at[item, part])
+
+    @pl.when(early)
+    def _():
+        for k in range(2):
+            relay_on(k)
+
+    def second_back(b):
+        rows = pl.ds(b * 64, 64)
+
+        @pl.when(b % 2 == 0)
+        def _():
+            arrived(r.grad_in.at[rows_of(b // 2)], r.grad_recv.at[b // 2])
+
+        start = r.hid[0, rows].astype(full)
+        middle = unit(start + r.alpha_attn[...] * (unit(r.branch[rows]) - start))
+        total = r.output[rows]
+        change = unit(total) - middle
+        grad = unit_back(middle + r.alpha_mlp[...] * change, r.grad_in[rows].astype(full))
+        r.sum_alphas[1:2] += jnp.sum(grad * change, axis=0, keepdims=True)
+        r.grad_rows[0, rows] = low(unit_back(total, r.alpha_mlp[...] * grad))
+        r.middle[rows] = grad * (1.0 - r.alpha_mlp[...])
+        share_rows(r.grad_rows, 1, b)
+
+    every(8, second_back)
+
+    for side in range(2):
+        if side:
+            shared(r.grad_rows, 1)
+
+        def close_gate(n, side=side):
+            at = pl.ds(lane(n * 512), 512)
+            grad = last_dims(r.grad_rows[side], r.wd[pl.ds(n * 512, 512)])
+            lift_up = r.up[side, :, at].astype(full)
+            lift_gate = r.gate[side, :, at].astype(full)
+            gating = lift_gate * r.scale_gate[:, at]
+            sigmoid = jax.nn.sigmoid(gating)
+            grad_up = grad * (gating * sigmoid)
+            grad_gate = (
+                grad * (lift_up * r.scale_up[:, at]) * sigmoid * (1.0 + gating * (1.0 - sigmoid))
+            )
+            r.sum_scales[0:1, at] += jnp.sum(grad_up * lift_up, axis=0, keepdims=True)
+            r.sum_scales[1:2, at] += jnp.sum(grad_gate * lift_gate, axis=0, keepdims=True)
+            r.up[side, :, at] = low(grad_up * r.scale_up[:, at])
+            r.gate[side, :, at] = low(grad_gate * r.scale_gate[:, at])
+
+        every(4, close_gate)
+    grad_of_down()
+    for k in range(READY):
+        begin(k)
+
+    def lifted(side, n):
+        rows = pl.ds(n * 256, 256)
+        return last_dims(r.up[side], r.wu[rows]) + last_dims(r.gate[side], r.wg[rows])
+
+    settle_sent(1)
+    exchange(2, lifted, r.middle)
+    in_plane(0, 0, READY, 0)
+    settle_shared(r.grad_rows, 1)
+
+    def first_back(b):
+        rows = pl.ds(b * 64, 64)
+        start = r.hid[0, rows].astype(full)
+        total = r.branch[rows]
+        change = unit(total) - start
+        grad = r.middle[rows] + r.got[rows].astype(full)
+        grad = unit_back(start + r.alpha_attn[...] * change, grad)
+        r.sum_alphas[0:1] += jnp.sum(grad * change, axis=0, keepdims=True)
+        r.grad_rows[0, rows] = low(unit_back(total, r.alpha_attn[...] * grad))
+        r.middle[rows] = grad * (1.0 - r.alpha_attn[...])
+        share_rows(r.grad_rows, 2, b)
+
+    every(8, first_back)
+
+    @pl.when(early)
+    def _():
+        for k in range(2, READY):
+            relay_on(k)
+
+    shared(r.grad_rows, 2)
+    in_plane(1, 0, READY, 0)
+
+    marks = (
+        lax.broadcasted_iota(jnp.int32, (8, 2 * HEAD), 1) // HEAD
+        == lax.broadcasted_iota(jnp.int32, (8, 2 * HEAD), 0)
+    ).astype(jnp.bfloat16)
+
+    def attend_back(pair):
+        in_plane(2 + pair, 0, READY, 0)
+
+        @pl.when(early)
+        def _():
+            relay_out(pair)
+
+        prepare(pair)
+        at = lanes_of(pair, 0)
+        heads = r.wo[pl.ds(pair * 128, 128)]
+        merge(r.grads, *(low(last_dims(r.grad_rows[side], heads)) for side in range(2)))
+        merge(r.raw, r.att[0, :, at], r.att[1, :, at])
+        r.dk[...] = jnp.zeros_like(r.dk)
+        r.dv[...] = jnp.zeros_like(r.dv)
+        for q in range(4):
+            at = slice(q * 256, (q + 1) * 256)
+            upto = slice(0, (q + 1) * 256)
+            deltas = row_sums(r.grads[at].astype(full) * r.raw[at].astype(full), marks)
+            delta = jnp.concatenate([deltas[h : h + 1] for h in range(2)], axis=1)
+            log_sum = jnp.concatenate([r.log_sums[pair, h : h + 1, at] for h in range(2)], axis=1)
+            query, grad, key = of_heads(r.queries[at]), of_heads(r.grads[at]), r.keys[upto]
+            mask = jnp.concatenate([r.bias[upto, at]] * 2, axis=1)
+            weighted = jnp.exp(last_dims(key, query) + (mask - log_sum))
+            grad_scores = low(
+                weighted * (last_dims(r.values[upto, : 2 * HEAD], grad) - delta)
+            )
+            r.dv[upto] += dot(low(weighted), grad)
+            r.dk[upto] += dot(grad_scores, query)
+            to_queries = contract_rows(grad_scores, key)
+            r.dq[at] = (
+                head_lanes(0, full) * to_queries[:256] + head_lanes(1, full) * to_queries[256:]
+            )
+
+        scale = r.flat[pair, pl.ds(c, 1), :]
+        scale_sum = 0.0
+        for part, grad in enumerate((r.dq, r.dk)):
+            normed, factor = normal(pair, part)
+            found = grad[...] * SCORE_SCALE if part == 0 else grad[...]
+            scale_sum = scale_sum + jnp.sum(found * normed, axis=0, keepdims=True)
+            step = found * scale
+            grad[...] = factor * (step - normed * sums_of_halves(normed * step))
+        r.sum_qk[pl.ds(pair, 1)] = scale_sum
+        for part, grad in enumerate((r.dq, r.dk, r.dv)):
+            at = lanes_of(pair, part)
+            for q in range(4):
+                rows = slice(q * BLOCK, (q + 1) * BLOCK)
+                r.mixed[0, rows, at] = low(grad[q * 256 : q * 256 + BLOCK])
+                r.mixed[1, rows, at] = low(grad[q * 256 + BLOCK : (q + 1) * 256])
+
+    every(4, attend_back)
+
+    settle_sent(2)
+    exchange(
+        3, lambda side, n: last_dims(r.mixed[side], r.wq[pl.ds(n * 256, 256)]), r.middle,
+    )
+
+    for b in range(4):
+        rows = rows_of(b)
+
+        @pl.when(early)
+        def _():
+            arrived(r.result.at[rows], r.result_send.at[b])
+
+        arrived(r.result.at[rows], r.owner_send.at[0, b])
+
+    def finish(b):
+        rows = rows_of(b)
+        r.result[rows] = low(r.middle[rows] + r.got[rows].astype(full))
+
+        @pl.when(late)
+        def _():
+            remote(
+                r.result.at[rows], r.grad_in.at[rows], r.result_send.at[b], r.grad_recv.at[b],
+                early_plane,
+            ).start()
+
+    every(4, finish)
+    to_owners(1, r.result, o_grad)
+
+    for owner in range(4):
+        r.terms[owner, pl.ds(c, 1), :] = r.sum_qk[owner : owner + 1]
+        for n in range(2):
+            for j in range(4):
+                at = slice((owner % 2 * 2 + n) * 512 + j * 128, (owner % 2 * 2 + n) * 512 + (j + 1) * 128)
+                scale = math.sqrt(width) if owner // 2 else 1.0
+                r.terms[owner, pl.ds(2 + n * 8 + j + c * 4, 1), :] = (
+                    r.sum_scales[owner // 2 : owner // 2 + 1, at] * scale
+                )
+        for j in range(4):
+            at = slice(owner % 2 * 512 + j * 128, owner % 2 * 512 + (j + 1) * 128)
+            r.terms[owner, 18 + j : 19 + j, :] = r.sum_alphas[owner // 2 : owner // 2 + 1, at]
+        r.terms[owner, 22:23, :] = r.sum_valid[...]
+    flow = Flow((r.v0, r.v1, r.v2, r.v3, r.v4, r.v5, r.v6, r.v7), r.vector)
+    flow.begin(lambda to: r.terms.at[to])
+
+    every(3, lambda n: in_plane(6 + n, 0, READY, 0))
+    grad_of_lift(r.up, g_up)
+    for k in range(READY, READY + AHEAD):
+        begin(k)
+
+    def step(t):
+        @pl.when(t == READY + 1)
+        def _():
+            grad_of_lift(r.gate, g_gate)
+
+        @pl.when(t == READY + 5)
+        def _():
+            grad_of_out()
+            grad_of_qkv()
+
+        @pl.when(t + AHEAD < CHUNKS)
+        def _():
+            begin(t + AHEAD)
+
+        in_plane(t, READY, CHUNKS, 2)
+        between_planes(t)
+        for at, work in (
+            (READY + 2, flow.pass_on), (READY + 4, flow.finish_plane), (READY + 10, flow.middle_planes),
+        ):
+            pl.when(t == at)(work)
+
+        @pl.when(t == READY + 14 + 14 * layer)
+        def _():
+            flow.all_planes(o_vectors.at[c])
+
+    every(CHUNKS + 18 - READY, lambda n: step(n + READY))
+
+    def settle(k):
+        chunk = plane_sum.at[k]
+        for sem in (r.send_own, r.send_far, r.given):
+            arrived(chunk, sem.at[k])
+
+        @pl.when(early)
+        def _():
+            arrived(chunk, r.send_on.at[k])
+            arrived(chunk, r.send_back.at[k])
+
+        @pl.when(k >= CHUNKS - 4)
+        def _():
+            arrived(chunk, r.send_next.at[k])
+            arrived(chunk, r.send_z.at[k])
+            placed(k, 1)
+
+        @pl.when(early & (k >= CHUNKS - 4))
+        def _():
+            arrived(chunk, r.send_out.at[k])
+            placed(k, 0)
+
+        @pl.when(late)
+        def _():
+            placed(k, 0)
+
+    every(CHUNKS, settle)
+    flow.settle()
+    settle_shared(r.mid, 0)
+    settle_shared(r.grad_rows, 2)
+    settle_sent(3)
+    for b in range(4):
+        rows = rows_of(b)
+        arrived(r.hid.at[1, rows], r.oth_send.at[b])
+
+        @pl.when(late)
+        def _():
+            arrived(r.result.at[rows], r.result_send.at[b])
+
+        @pl.when(s != b)
+        def _():
+            arrived(o_row.at[rows], r.row_send.at[b])
+            arrived(r.flags.at[b], r.flag_send.at[b])
+
+        arrived(r.result.at[rows], r.owner_send.at[1, b])
+
+    for array, to_ref in enumerate((o_hidden, o_grad)):
+        for micro in range(2):
+            for core in range(2):
+
+                @pl.when(jnp.logical_not((c == layer) & (c == core) & (s // 2 == micro)))
+                def _():
+                    arrived(
+                        to_ref.at[micro, pl.ds(core * BLOCK, BLOCK)],
+                        r.owner_recv.at[array, micro, core],
+                    )
+
+    @pl.when(c == layer)
+    def _():
+        for item in range(6):
+            for index in range(len(targets)):
+                arrived(block(item, f), r.first_send.at[item, index])
+
+
+def relay_all(w_qkv, w_out, w_in, w_down, vectors, valid, tokens, cotangent, places):
+    width = w_out.shape[1]
+    units = w_down.shape[0] * 4
+    half = units // 2
+    place, start = places
+
+    def low_shape(*shape):
+        return jax.ShapeDtypeStruct(shape, jnp.bfloat16)
+
+    chunks = low_shape(CHUNKS, 256, 512)
+    rows = low_shape(2, 2 * BLOCK, width)
+    anywhere = pl.BlockSpec(memory_space=pl.ANY)
+    near = pl.BlockSpec(memory_space=pltpu.VMEM)
+    scratch = scratch_of(width, units, vectors.shape[0], valid.shape[1])
+    out_shape = [
+        low_shape(half // 2, width), low_shape(width // 4, 2 * units), low_shape(width // 4, width),
+        low_shape(width // 4, 3 * width), jax.ShapeDtypeStruct((2, 24, 128), jnp.float32),
+        rows, rows, low_shape(4 * BLOCK, width),
+        low_shape(half, width), low_shape(width, half), low_shape(width, half),
+        low_shape(width, width // 2), low_shape(width, 3 * width // 2),
+    ] + [chunks] * 7
+    return pl.pallas_call(
+        functools.partial(relay_kernel, tuple(scratch)),
+        out_shape=out_shape,
+        in_specs=[anywhere] * 8 + [near] * 3,
+        out_specs=[anywhere] * len(out_shape),
+        scratch_shapes=list(scratch.values()),
+        compiler_params=pltpu.CompilerParams(
+            collective_id=0, has_side_effects=True, vmem_limit_bytes=62 * 2**20
+        ),
+    )(
+        w_qkv, w_out, w_in, w_down, vectors, valid, tokens, cotangent,
+        start[:, None], place[None, :], start[None, :],
+    )[:7]
+
+
+def per_device(
+    tokens, cotangent, lengths, valid_mask, w_qkv, w_out, w_in, w_down, qk_scale, mlp_scale, alphas
+):
+    c, s, f, _, _, layer = position()
+    second = layer == 1
+    micro = s // 2
+    width = tokens.shape[3]
+    group = tokens.shape[2]
+    units = w_down.shape[1] * 4
+
+    vectors = jnp.concatenate([qk_scale[0], mlp_scale[0], alphas[0]])
+    vectors = jnp.pad(vectors, (0, 32 * 128 - vectors.shape[0])).reshape(32, 128)
+    valid = low(jnp.pad(valid_mask[:, 0], ((0, 0), (0, 16 * 128 - group)))).reshape(2, 16, 128)
+    index = jnp.arange(4 * group, dtype=jnp.int32)
+    place = (index // 256) * 256 + (((index // BLOCK) + c) % 2) * BLOCK + index % BLOCK
+    ends = jnp.cumsum(pick(lengths, micro, 0)[0])[:-1]
+    passed = place[:, None] >= ends[None, :]
+    start = jnp.max(jnp.where(passed, ends[None, :], 0), axis=1)
+    places = (place, start)
+    grad_down, grad_in_proj, grad_out, grad_qkv, vectors, hidden_out, grad_in = relay_all(
+        w_qkv[0], w_out[0], w_in[0], w_down[0], vectors, valid, tokens[:, 0], cotangent[:, 0], places
+    )
+    cut_qk, cut_mlp = qk_scale.shape[1], qk_scale.shape[1] + mlp_scale.shape[1]
+    full = jnp.sum(vectors, axis=0).reshape(-1)
+    cuts = (cut_qk, cut_mlp, cut_mlp + alphas.shape[1])
+    grad_qk_scale = full[: cuts[0]][None]
+    grad_mlp_scale = full[cuts[0] : cuts[1]][None]
+    grad_alphas = full[cuts[1] : cuts[2]][None]
+    token_count = tokens.shape[0] * lax.axis_size("fsdp") * 4 * group
+    total = jnp.sum(full[cuts[2] : cuts[2] + 128], keepdims=True)
+    rms_stats = jnp.sqrt(total / token_count + epsilon)
+    as_float = [
+        part.astype(jnp.float32)[None] for part in (grad_qkv, grad_out, grad_in_proj, grad_down)
+    ]
+    return (
+        hidden_out[None, :, None], grad_in.astype(jnp.float32)[None, :, None], *as_float,
+        grad_qk_scale, grad_mlp_scale, grad_alphas, rms_stats,
+    )
+
+
 def solution(mesh):
     placed = (
         P(None, "fsdp", "seq", None),
@@ -376,8 +1721,9 @@
         P("section", "fsdp"),
         P("section", "fsdp"),
     )
+    planes = mesh.shape["section"] == 2 and mesh.shape["seq"] == 4 and mesh.shape["fsdp"] == 4
     return jax.shard_map(
-        per_device,
+        per_device if planes else per_device_general,
         mesh=mesh,
         in_specs=placed,
         out_specs=(

time: 2550 us -> 653 us (0.26)
  waiting for transfers between devices: 1490 us -> 0 us
  Pallas kernels: 0 us -> 624 us
  matrix products: 465 us -> 0 us
  other arithmetic: 222 us -> 19.9 us
  local copies, waits for them, and re-layouts: 167 us -> 6.14 us
  blocking collectives: 123 us -> 0 us
  loops' own time: 33.6 us -> 0 us
    all_gather x14 -> x0, waiting for transfers between devices: 872 us -> none  [the longest x1 159 us: per_device(): lax.all_gather(shards[2], 'fsdp', axis=1, tiled=True)]
    pallas_call x0 -> x1, Pallas kernels: none -> 624 us  [relay_all(): pl.pallas_call(functools.partial(relay_kernel, tuple(scratch)), out_shape...]
    dot_general x57 -> x0, matrix products: 465 us -> none  [the longest x12 149 us: contract_rows(): lax.dot_general(left, right, (((0,), (0,)), ((), ())), preferred_element_...]
    reduce_scatter x10 -> x0, waiting for transfers between devices: 397 us -> none  [the longest x4 321 us: per_device(): lax.psum_scatter(for_sending(sums), 'fsdp', scatter_dimension=0, tiled=True)]
    psum x1 -> x0, waiting for transfers between devices: 213 us -> none  [per_device(): lax.psum(for_sending(shard_sums), 'seq')]
    convert_element_type x34 -> x0, other arithmetic: 86 us -> none  [the longest x7 38.9 us: for_sending(): a.astype(jnp.bfloat16)]
    reduce_sum x45 -> x2, other arithmetic: 64.1 us -> 1.46 us  [the longest x1 0.86 us: per_device(): full = jnp.sum(vectors, axis=0).reshape(-1)]
    psum x2 -> x0, blocking collectives: 60.3 us -> none  [the longest x1 43.5 us: per_device(): total_stat = lax.psum(stat_sum, ('seq', 'fsdp'))]
  transfers between devices with their start and end apart: 31 -> 0, of which waited for: 22 -> 0; matrix products, arithmetic and copies ran while one was open for 13% -> 0% of each run, Pallas kernels for 0% -> 0%
where the time goes in v4:
time: 653 us
  Pallas kernels  624 us (96%)
  other arithmetic  19.9 us (3%)
    pallas_call x1, Pallas kernels, relay_all(): pl.pallas_call(functools.partial(relay_kernel, tuple(scratch)), out_shape...  624 us

profile of v4, /device:TPU:0, one launch (start us, length us, event | category | flops | bytes accessed | tf_op | source)
XLA Modules:
  0.0 652.7 jit_solution(11558699130950878866)
XLA Ops:
  0.6 0.0 copy-start
  0.7 0.7 copy-done
  1.3 0.2 reduce-window.4
  1.5 0.7 reduce.1
  2.2 0.7 reduce.3
  2.9 0.7 convert.10
  3.6 0.7 reduce.2
  4.3 0.6 fusion.5.refs_4_
  4.9 0.6 fusion.10.refs_9_
  5.6 0.1 select_reduce_fusion
  5.7 0.0 copy-start.6
  5.7 0.6 copy.33
  6.3 1.0 copy.26.refs_8_
  7.3 0.0 copy-done.6
  7.3 624.2 %shard_map.186 = (bf16[1024,1024]{1,0:T(8,128)(2,1)}, bf16[256,8192]{1,0:T(8,128)(2,1)}, bf16[256,1024]{1,0:T(8,128)(2,1)}, bf16[256,3072]{1,0:T(8,128)(2,1)}, f...) custom-call(bf16[256,3072]{1,0:T(8,128)(2,1)} %bitcast.49, ...), custom_call_target="tpu_custom_call" | custom-call | tf_op jit(solution)/shard_map/pallas_call | solution.py:1655
  631.5 0.0 copy-start.4
  631.5 0.9 reduce_sum.18
  632.4 0.6 slice_reduce_fusion
  633.7 0.6 slice.25
  634.2 0.6 slice.27
  634.8 0.6 slice.26
  635.4 2.1 bitcast_convert_fusion.4
  637.5 2.9 bitcast_convert_fusion.3
  640.5 0.0 copy-done.4
  640.5 2.0 bitcast_convert_fusion.2
  642.5 0.0 copy-done.3
  642.5 2.6 bitcast_convert_fusion.1
  645.1 1.1 copy-done.2
  646.2 4.4 bitcast_convert_fusion
  650.6 0.0 copy-done.5
  650.6 1.0 copy.36
  651.6 0.0 copy-done.1
  (9 shorter events, 0.0 us)
Async XLA Ops:
  0.6 0.7 copy-start
  5.7 1.7 copy-start.6
  631.5 9.0 %copy-start.4 = (bf16[256,3072]{1,0:T(8,128)(2,1)S(1)}, bf16[256,3072]{1,0:T(8,128)(2,1)}, u32[]{:S(2)}) copy-start(bf16[256,3072]{1,0:T(8,128)(2,1)} %get-tuple-element.19) | copy-start | bytes 4718596
  637.5 5.0 copy-start.3
  642.5 3.7 copy-start.2
  646.2 4.4 copy-start.5
  646.2 5.4 copy-start.1

commit v5 on v4

--- a/solution.py
+++ b/solution.py
@@ -598,6 +598,7 @@
 
 VECTOR_SEMAPHORES = 18
 CHUNKS = 16
+SHARED = (1, 2, 3, 4)
 READY = 4
 AHEAD = 3
 INPUTS = 11
@@ -638,7 +639,8 @@
         sum_valid=full_vmem(1, 128), terms=full_vmem(4, 24, 128),
         v0=full_vmem(24, 128), v1=full_vmem(24, 128), v2=full_vmem(24, 128), v3=full_vmem(24, 128),
         v4=full_vmem(24, 128), v5=full_vmem(24, 128), v6=full_vmem(24, 128), v7=full_vmem(24, 128),
-        first_send=sems(6, 5), first_recv=sems(6, 3), next_send=sems(6, 2), next_recv=sems(6, 2),
+        first_send=sems(6, 3), first_recv=sems(6, 3), next_send=sems(6, 2), next_recv=sems(6, 2),
+        plane_send=sems(6, 3), plane_recv=sems(6, 3),
         row_send=sems(4), row_recv=sems(4), flag_send=sems(4), flag_recv=sems(4),
         own_recv=sems(4), oth_send=sems(4), oth_recv=sems(4),
         part_send=sems(4, 4), part_recv=sems(4, 4),
@@ -673,7 +675,7 @@
     width = w_out.shape[1]
     full = jnp.float32
     greet(
-        [sibling, (c, s, fx), (1 - c, s, fx), (c, s, fy), (1 - c, s, fy)]
+        [sibling, (c, s, fx), (c, s, fy)]
         + [(core, (s + step) % 4, f) for core in (0, 1) for step in (1, 2, 3)]
     )
 
@@ -683,9 +685,8 @@
     def columns(n):
         return pl.ds(lane(n * 256), 256)
 
-    for to, held in enumerate((cotangent.at[0], tokens.at[0], tokens.at[1], cotangent.at[1])):
-        src = held.at[pl.ds(c * BLOCK, BLOCK)]
-        dst = o_row.at[rows_of(s)]
+    def send_row(to, held):
+        src, dst = held.at[pl.ds(c * BLOCK, BLOCK)], o_row.at[rows_of(s)]
         flags, flags_to = valid.at[to // 2], r.flags.at[s]
 
         @pl.when(s == to)
@@ -697,6 +698,9 @@
         def _():
             remote(src, dst, r.row_send.at[to], r.row_recv.at[s], (c, to, f)).start()
             remote(flags, flags_to, r.flag_send.at[to], r.flag_recv.at[s], (c, to, f)).start()
+
+    send_row(1, tokens.at[0])
+    send_row(2, tokens.at[1])
 
     def pieces(item, h):
         if item == 0:
@@ -723,6 +727,10 @@
         return [(w_down.at[pl.ds(h * 512, 512)], r.wd.at[pl.ds(f * 512, 512)])]
 
     weights = (r.vec, r.wq, r.wo, r.wu, r.wg, r.wd)
+    other_plane = (c, 3 - s, f)
+
+    def quarter(item):
+        return 0 if item == 0 else weights[item].shape[0] // 16
 
     def block(item, of):
         if item == 0:
@@ -736,38 +744,133 @@
         rows = weights[item].shape[0] // 8
         return weights[item].at[pl.ds(of * 2 * rows + part * rows, rows)]
 
-    targets = (
-        ((c, s, fx), c, 1), ((c, s, fy), c, 2), ((1 - c, s, fx), 1 - c, 1),
-        ((1 - c, s, fy), 1 - c, 2), (sibling, 1 - c, 0),
-    )
+    def quarters(item, of, least, count):
+        size = quarter(item)
+        return weights[item].at[pl.ds(of * 4 * size + least * size, count * size)]
+
+    @pl.when(c == layer)
+    def _():
+        for item in range(6):
+            for src, dst in pieces(item, 1 - c):
+                remote(
+                    src, dst, r.first_send.at[item, 2], r.first_recv.at[item, 0], sibling
+                ).start()
+            for src, dst in pieces(item, c):
+                pltpu.make_async_copy(src, dst, r.first_recv.at[item, 0]).start()
+
+    ways = ((1, fx, fy), (2, fy, fx))
 
     def spread(*items):
+        for item in items:
+            arrived(block(item, f), r.first_recv.at[item, 0])
+
+            def send(moved, item=item):
+                for part, (came, to, _) in enumerate(ways):
+                    remote(
+                        moved, moved, r.first_send.at[item, part], r.first_recv.at[item, came],
+                        (c, s, to),
+                    ).start()
+
+            if item in SHARED:
+
+                @pl.when(early)
+                def _():
+                    send(quarters(item, f, s - 1, 3))
+
+                @pl.when(late)
+                def _():
+                    send(block(item, f))
+            else:
+                send(block(item, f))
+
+    def forward(moved, item, part, to):
+        remote(moved, moved, r.next_send.at[item, part], r.next_recv.at[item, part], to).start()
+
+    def share(moved, item, part):
+        remote(
+            moved, moved, r.plane_send.at[item, part], r.plane_recv.at[item, part], other_plane
+        ).start()
+
+    def relay(item):
+        def halves():
+            for part, (came, of, to) in enumerate(ways):
+                arrived(block(item, of), r.first_recv.at[item, came])
+                forward(part_of(item, of, part), item, part, (c, s, to))
+
+        if item not in SHARED:
+            halves()
+        else:
+            pl.when(late)(halves)
+
+            @pl.when(early)
+            def _():
+                for part, (came, of, to) in enumerate(ways):
+                    arrived(quarters(item, of, 0, 3), r.first_recv.at[item, came])
+                    forward(quarters(item, of, (s - 1) * 2 + part, 1), item, part, (c, s, to))
+                for part, (came, of, to) in enumerate(ways):
+                    share(quarters(item, of, (s - 1) * 3, 1), item, part)
+
+    def relay_across(item):
+        @pl.when(early)
+        def _():
+            for part in range(2):
+                arrived(quarters(item, 3 - f, (s - 1) * 2 + part, 1), r.next_recv.at[item, part])
+            share(quarters(item, 3 - f, (s - 1) * 2, 2), item, 2)
+
+    def complete(item):
+        def halves():
+            for part in range(2):
+                arrived(part_of(item, 3 - f, part), r.next_recv.at[item, part])
+
+        if item not in SHARED:
+            halves()
+        else:
+            pl.when(late)(halves)
+
+            @pl.when(early)
+            def _():
+                for part, of in ((0, fx), (1, fy)):
+                    arrived(quarters(item, of, (2 - s) * 3, 1), r.plane_recv.at[item, part])
+                arrived(quarters(item, 3 - f, (2 - s) * 2, 2), r.plane_recv.at[item, 2])
+
+    def settle_relays():
+        for item in range(6):
+
+            def halves():
+                for part in range(2):
+                    arrived(part_of(item, f, part), r.next_send.at[item, part])
+
+            if item not in SHARED:
+                halves()
+            else:
+                pl.when(late)(halves)
+
+                @pl.when(early)
+                def _():
+                    for part in range(2):
+                        arrived(quarters(item, f, 0, 1), r.next_send.at[item, part])
+                        arrived(quarters(item, f, 0, 1), r.plane_send.at[item, part])
+                    arrived(quarters(item, f, 0, 2), r.plane_send.at[item, 2])
+
+    def settle_spread():
+        for item in range(6):
+
+            def sent(moved, item=item):
+                for part in range(2):
+                    arrived(moved, r.first_send.at[item, part])
+
+            if item in SHARED:
+                pl.when(early)(lambda: sent(quarters(item, f, 0, 3)))
+                pl.when(late)(lambda: sent(block(item, f)))
+            else:
+                sent(block(item, f))
+
         @pl.when(c == layer)
         def _():
-            for item in items:
-                for index, (device, h, came) in enumerate(targets):
-                    for src, dst in pieces(item, h):
-                        remote(
-                            src, dst, r.first_send.at[item, index], r.first_recv.at[item, came],
-                            device,
-                        ).start()
-                for src, dst in pieces(item, c):
-                    pltpu.make_async_copy(src, dst, r.first_recv.at[item, 0]).start()
-
-    def relay(item):
-        for part, (came, of, to) in enumerate(((1, fx, fy), (2, fy, fx))):
-            arrived(block(item, of), r.first_recv.at[item, came])
-            moved = part_of(item, of, part)
-            remote(
-                moved, moved, r.next_send.at[item, part], r.next_recv.at[item, part], (c, s, to)
-            ).start()
-
-    def complete(item):
-        arrived(block(item, f), r.first_recv.at[item, 0])
-        for part in range(2):
-            arrived(part_of(item, 3 - f, part), r.next_recv.at[item, part])
-
-    spread(0, 1, 2, 3)
+            for item in range(6):
+                arrived(block(item, f), r.first_send.at[item, 2])
+
+    spread(0, 1, 2)
     index = lax.broadcasted_iota(jnp.int32, (8 * BLOCK, 1), 0)
     place_col = (index // 256) * 256 + (index // BLOCK + c) % 2 * BLOCK + index % BLOCK
     fits = (place_row[...] >= start_col[...]) & (place_row[...] <= place_col)
@@ -777,8 +880,9 @@
         sums[...] = jnp.zeros_like(sums)
     relay(0)
     relay(1)
-    spread(4)
+    spread(3)
     relay(2)
+    relay_across(1)
 
     def to_sibling(b, src):
         remote(src, r.hid.at[1, rows_of(b)], r.oth_send.at[b], r.oth_recv.at[b], sibling).start()
@@ -795,14 +899,11 @@
 
     @pl.when(late)
     def _():
+        spread(4)
         relay(3)
         spread(5)
         relay(4)
         relay(5)
-        for b in range(4):
-            held = o_row.at[rows_of(b)]
-            arrived(held, r.row_recv.at[b])
-            pltpu.make_async_copy(held, r.grad_in.at[rows_of(b)], r.grad_recv.at[b]).start()
         for b in range(4):
             arrived(r.hid.at[0, rows_of(b)], r.own_recv.at[b])
             to_sibling(b, r.hid.at[0, rows_of(b)])
@@ -854,9 +955,17 @@
         return jnp.concatenate([block * head_lanes(h, jnp.bfloat16) for h in range(2)])
 
     def attend(pair):
+        @pl.when(early & (pair == 0))
+        def _():
+            relay_across(2)
+            spread(4)
+
         @pl.when(early & (pair == 2))
         def _():
             relay(3)
+
+        @pl.when(early & (pair == 3))
+        def _():
             spread(5)
 
         prepare(pair)
@@ -934,6 +1043,9 @@
         r.mid[0, rows] = low(stepped)
         share_rows(r.mid, 0, b)
 
+    relay_across(3)
+    send_row(0, cotangent.at[0])
+    send_row(3, cotangent.at[1])
     every(8, first_step)
 
     @pl.when(early)
@@ -950,6 +1062,8 @@
             r.up[side, :, at] = low(dot(r.mid[side], r.wu[:, at]))
 
         every(4, lift)
+
+    relay_across(4)
 
     @pl.when(early)
     def _():
@@ -1006,6 +1120,13 @@
                 remote(src, dst, r.owner_send.at[array, to], recv, (layer, to, f)).start()
 
     to_owners(0, r.result, o_hidden)
+
+    @pl.when(late)
+    def _():
+        for b in range(4):
+            held = o_row.at[rows_of(b)]
+            arrived(held, r.row_recv.at[b])
+            pltpu.make_async_copy(held, r.grad_in.at[rows_of(b)], r.grad_recv.at[b]).start()
 
     for b in range(4):
         arrived(r.flags.at[b], r.flag_recv.at[b])
@@ -1037,10 +1158,10 @@
     def begin(k):
         def start(source):
             to = (c, s, near_of(k))
+            remote(source(3 - f), near_far.at[k], r.send_far.at[k], r.recv_far.at[k], to).start()
             remote(
                 source(near_of(k)), near_own.at[k], r.send_own.at[k], r.recv_own.at[k], to
             ).start()
-            remote(source(3 - f), near_far.at[k], r.send_far.at[k], r.recv_far.at[k], to).start()
 
         with_source(k, start)
 
@@ -1117,8 +1238,8 @@
 
     def in_plane(t, least, most, slack):
         for lag, work in (
-            (0, pass_load), (1, pass_send), (5 + slack, plane_done), (3 + slack, plane_load),
-            (4 + slack, plane_send),
+            (5 + slack, plane_done), (4 + slack, plane_send), (3 + slack, plane_load),
+            (1, pass_send), (0, pass_load),
         ):
             @pl.when((t >= lag + least) & (t < lag + most))
             def _():
@@ -1268,14 +1389,13 @@
     def between_planes(t):
         @pl.when(early)
         def _():
-            for lag, work in ((1, relay_on), (3, relay_out)):
-                @pl.when((t >= lag + READY) & (t < lag + CHUNKS))
+            for lag, work, least in ((-2, relay_on, READY + 2), (0, relay_out, READY)):
+                @pl.when((t >= lag + least) & (t < lag + CHUNKS))
                 def _():
                     work(t - lag)
 
         for lag, work, least, most in (
-            (4, pair_load, 0, READY), (5, pair_send, 0, READY), (8, pair_load, READY, CHUNKS),
-            (9, pair_send, READY, CHUNKS), (18, pair_take, 0, CHUNKS),
+            (7, pair_load, READY, CHUNKS), (8, pair_send, READY, CHUNKS), (18, pair_take, 0, CHUNKS),
             (6 + 8 * layer, late_load, 0, CHUNKS), (7 + 8 * layer, late_place, 0, CHUNKS),
         ):
             @pl.when((t >= lag + least) & (t < lag + most))
@@ -1352,9 +1472,8 @@
 
     fits = (place_col >= start_row[...]) & (place_col <= place_row[...])
     r.bias[...] = jnp.where(fits, 0.0, MASKED)
-    for item in range(6):
-        for part in range(2):
-            arrived(part_of(item, f, part), r.next_send.at[item, part])
+    settle_relays()
+    settle_spread()
 
     @pl.when(early)
     def _():
@@ -1405,6 +1524,13 @@
     for k in range(READY):
         begin(k)
 
+    @pl.when(early)
+    def _():
+        for k in range(2, READY):
+            relay_on(k)
+        for k in range(2):
+            relay_out(k)
+
     def lifted(side, n):
         rows = pl.ds(n * 256, 256)
         return last_dims(r.up[side], r.wu[rows]) + last_dims(r.gate[side], r.wg[rows])
@@ -1431,7 +1557,7 @@
     @pl.when(early)
     def _():
         for k in range(2, READY):
-            relay_on(k)
+            relay_out(k)
 
     shared(r.grad_rows, 2)
     in_plane(1, 0, READY, 0)
@@ -1444,9 +1570,9 @@
     def attend_back(pair):
         in_plane(2 + pair, 0, READY, 0)
 
-        @pl.when(early)
-        def _():
-            relay_out(pair)
+        @pl.when(early & (pair % 2 == 1))
+        def _():
+            relay_on(READY + pair // 2)
 
         prepare(pair)
         at = lanes_of(pair, 0)
@@ -1540,6 +1666,11 @@
     grad_of_lift(r.up, g_up)
     for k in range(READY, READY + AHEAD):
         begin(k)
+    for k in range(READY + 1):
+        if k < READY:
+            pair_load(k)
+        if k:
+            pair_send(k - 1)
 
     def step(t):
         @pl.when(t == READY + 1)
@@ -1555,8 +1686,8 @@
         def _():
             begin(t + AHEAD)
 
-        in_plane(t, READY, CHUNKS, 2)
         between_planes(t)
+        in_plane(t, READY, CHUNKS, 1)
         for at, work in (
             (READY + 2, flow.pass_on), (READY + 4, flow.finish_plane), (READY + 10, flow.middle_planes),
         ):
@@ -1623,12 +1754,6 @@
                         to_ref.at[micro, pl.ds(core * BLOCK, BLOCK)],
                         r.owner_recv.at[array, micro, core],
                     )
-
-    @pl.when(c == layer)
-    def _():
-        for item in range(6):
-            for index in range(len(targets)):
-                arrived(block(item, f), r.first_send.at[item, index])
 
 
 def relay_all(w_qkv, w_out, w_in, w_down, vectors, valid, tokens, cotangent, places):

time: 653 us -> 616 us (0.943)
  Pallas kernels: 624 us -> 587 us
    pallas_call x1, Pallas kernels: 624 us -> 587 us  [relay_all(): pl.pallas_call(functools.partial(relay_kernel, tuple(scratch)), out_shape...]
where the time goes in v5:
time: 616 us
  Pallas kernels  587 us (95%)
  other arithmetic  19.9 us (3%)
    pallas_call x1, Pallas kernels, relay_all(): pl.pallas_call(functools.partial(relay_kernel, tuple(scratch)), out_shape...  587 us

profile of v5, /device:TPU:0, one launch (start us, length us, event | category | flops | bytes accessed | tf_op | source)
XLA Modules:
  0.0 615.6 jit_solution(1357392320927582617)
XLA Ops:
  0.6 0.0 copy-start
  0.7 0.7 copy-done
  1.3 0.2 reduce-window.4
  1.5 0.7 reduce.1
  2.2 0.7 reduce.3
  2.9 0.7 convert.10
  3.6 0.7 reduce.2
  4.3 0.6 fusion.5.refs_4_
  4.9 0.6 fusion.10.refs_9_
  5.6 0.1 select_reduce_fusion
  5.7 0.0 copy-start.6
  5.7 0.6 copy.33
  6.3 1.0 copy.26.refs_8_
  7.3 0.0 copy-done.6
  7.3 587.1 %shard_map.186 = (bf16[1024,1024]{1,0:T(8,128)(2,1)}, bf16[256,8192]{1,0:T(8,128)(2,1)}, bf16[256,1024]{1,0:T(8,128)(2,1)}, bf16[256,3072]{1,0:T(8,128)(2,1)}, f...) custom-call(bf16[256,3072]{1,0:T(8,128)(2,1)} %bitcast.49, ...), custom_call_target="tpu_custom_call" | custom-call | tf_op jit(solution)/shard_map/pallas_call | solution.py:1780
  594.4 0.0 copy-start.4
  594.4 0.9 reduce_sum.18
  595.3 0.6 slice_reduce_fusion
  596.6 0.6 slice.25
  597.2 0.6 slice.27
  597.7 0.6 slice.26
  598.3 2.1 bitcast_convert_fusion.4
  600.5 2.9 bitcast_convert_fusion.3
  603.4 0.0 copy-done.4
  603.4 2.0 bitcast_convert_fusion.2
  605.4 0.0 copy-done.3
  605.4 2.6 bitcast_convert_fusion.1
  608.0 1.1 copy-done.2
  609.2 4.4 bitcast_convert_fusion
  613.5 0.0 copy-done.5
  613.5 1.0 copy.36
  614.5 0.0 copy-done.1
  (9 shorter events, 0.0 us)
Async XLA Ops:
  0.6 0.7 copy-start
  5.7 1.7 copy-start.6
  594.4 9.0 %copy-start.4 = (bf16[256,3072]{1,0:T(8,128)(2,1)S(1)}, bf16[256,3072]{1,0:T(8,128)(2,1)}, u32[]{:S(2)}) copy-start(bf16[256,3072]{1,0:T(8,128)(2,1)} %get-tuple-element.19) | copy-start | bytes 4718596
  600.5 5.0 copy-start.3
  605.4 3.7 copy-start.2
  609.1 4.4 copy-start.5
  609.2 5.4 copy-start.1

commit v6 on v5

--- a/solution.py
+++ b/solution.py
@@ -599,7 +599,6 @@
 VECTOR_SEMAPHORES = 18
 CHUNKS = 16
 SHARED = (1, 2, 3, 4)
-READY = 4
 AHEAD = 3
 INPUTS = 11
 OUTPUTS = 19
@@ -1128,14 +1127,6 @@
             arrived(held, r.row_recv.at[b])
             pltpu.make_async_copy(held, r.grad_in.at[rows_of(b)], r.grad_recv.at[b]).start()
 
-    for b in range(4):
-        arrived(r.flags.at[b], r.flag_recv.at[b])
-    r.flags_full[...] = r.flags[...].astype(full)
-    ones = jnp.ones((8, width), jnp.bfloat16)
-    for b in range(4):
-        squares = row_sums(r.branch[rows_of(b)] * r.branch[rows_of(b)], ones)[:1]
-        r.sum_valid[...] += squares * r.flags_full[b, pl.ds(c, 1), :]
-
     def near_of(k):
         return fx + (fy - fx) * (k % 2)
 
@@ -1189,14 +1180,12 @@
     def again(k, work):
         pl.when(k >= 4)(work)
 
-    def pass_load(k):
+    def pass_on(k):
         arrived(near_far.at[k], r.recv_far.at[k])
 
         again(k, lambda: arrived(slot("pass", k), r.send_next.at[k - 4]))
         with_source(k, lambda source: fetch(source(far_of(k)), "pass", k))
         fetch(near_far.at[k], "far", k)
-
-    def pass_send(k):
         fetched("pass", k)
         fetched("far", k)
         total = slot("pass", k)
@@ -1205,7 +1194,7 @@
             total, far_in.at[k], r.send_next.at[k], r.recv_next.at[k], (c, s, far_of(k))
         ).start()
 
-    def plane_load(k):
+    def plane_total(k):
         arrived(near_own.at[k], r.recv_own.at[k])
         arrived(far_in.at[k], r.recv_next.at[k])
 
@@ -1213,8 +1202,6 @@
         with_source(k, lambda source: fetch(source(f), "own", k))
         fetch(near_own.at[k], "near", k)
         fetch(far_in.at[k], "last", k)
-
-    def plane_send(k):
         for name in ("own", "near", "last"):
             fetched(name, k)
         own, send = slot("own", k), r.send_z.at[k]
@@ -1236,12 +1223,18 @@
     def plane_done(k):
         arrived(plane_sum.at[k], r.stored.at[k])
 
-    def in_plane(t, least, most, slack):
-        for lag, work in (
-            (5 + slack, plane_done), (4 + slack, plane_send), (3 + slack, plane_load),
-            (1, pass_send), (0, pass_load),
-        ):
-            @pl.when((t >= lag + least) & (t < lag + most))
+    def in_plane(t):
+        @pl.when((t + AHEAD < CHUNKS) & (early | (t == 0) | (t > 3)))
+        def _():
+            begin(t + AHEAD)
+
+        @pl.when(late & (t == 3))
+        def _():
+            for k in range(4, 7):
+                begin(k)
+
+        for lag, work in ((3, plane_done), (2, plane_total), (0, pass_on)):
+            @pl.when((t >= lag) & (t < lag + CHUNKS))
             def _():
                 work(t - lag)
 
@@ -1355,7 +1348,10 @@
         @pl.when(late)
         def _():
             arrived(pair_sum.at[k], r.recv_pair.at[k])
-            place(k, 0, pair_sum.at[k])
+            again(k, lambda: placed(k - 4, 0))
+            fetch(pair_sum.at[k], "pair", k)
+            fetched("pair", k)
+            place(k, 0, slot("pair", k))
 
     def late_load(k):
         again(k, lambda: placed(k - 4, 1))
@@ -1389,16 +1385,16 @@
     def between_planes(t):
         @pl.when(early)
         def _():
-            for lag, work, least in ((-2, relay_on, READY + 2), (0, relay_out, READY)):
-                @pl.when((t >= lag + least) & (t < lag + CHUNKS))
+            for lag, work in ((-4, relay_on), (-2, relay_out)):
+                @pl.when(t < lag + CHUNKS)
                 def _():
                     work(t - lag)
 
-        for lag, work, least, most in (
-            (7, pair_load, READY, CHUNKS), (8, pair_send, READY, CHUNKS), (18, pair_take, 0, CHUNKS),
-            (6 + 8 * layer, late_load, 0, CHUNKS), (7 + 8 * layer, late_place, 0, CHUNKS),
+        for lag, work in (
+            (4, pair_load), (4, pair_send), (19, pair_take), (6 + 10 * layer, late_load),
+            (6 + 10 * layer, late_place),
         ):
-            @pl.when((t >= lag + least) & (t < lag + most))
+            @pl.when((t >= lag) & (t < lag + CHUNKS))
             def _():
                 work(t - lag)
 
@@ -1477,8 +1473,7 @@
 
     @pl.when(early)
     def _():
-        for k in range(2):
-            relay_on(k)
+        relay_on(0)
 
     def second_back(b):
         rows = pl.ds(b * 64, 64)
@@ -1521,15 +1516,24 @@
 
         every(4, close_gate)
     grad_of_down()
-    for k in range(READY):
+    for k in range(AHEAD):
         begin(k)
+
+    def relays(on, out):
+        @pl.when(early)
+        def _():
+            for k in on:
+                relay_on(k)
+            for k in out:
+                relay_out(k)
+
+    relays((1, 2), (0,))
 
     @pl.when(early)
     def _():
-        for k in range(2, READY):
-            relay_on(k)
-        for k in range(2):
-            relay_out(k)
+        grad_of_lift(r.up, g_up)
+
+    relays((3,), (1,))
 
     def lifted(side, n):
         rows = pl.ds(n * 256, 256)
@@ -1537,7 +1541,8 @@
 
     settle_sent(1)
     exchange(2, lifted, r.middle)
-    in_plane(0, 0, READY, 0)
+    in_plane(0)
+    relays((4,), (2,))
     settle_shared(r.grad_rows, 1)
 
     def first_back(b):
@@ -1554,13 +1559,7 @@
 
     every(8, first_back)
 
-    @pl.when(early)
-    def _():
-        for k in range(2, READY):
-            relay_out(k)
-
     shared(r.grad_rows, 2)
-    in_plane(1, 0, READY, 0)
 
     marks = (
         lax.broadcasted_iota(jnp.int32, (8, 2 * HEAD), 1) // HEAD
@@ -1568,11 +1567,14 @@
     ).astype(jnp.bfloat16)
 
     def attend_back(pair):
-        in_plane(2 + pair, 0, READY, 0)
-
-        @pl.when(early & (pair % 2 == 1))
-        def _():
-            relay_on(READY + pair // 2)
+        @pl.when(pair % 2 == 0)
+        def _():
+            in_plane(1 + pair // 2)
+
+        @pl.when(early & (pair % 2 == 0))
+        def _():
+            relay_on(5 + pair // 2)
+            relay_out(3 + pair // 2)
 
         prepare(pair)
         at = lanes_of(pair, 0)
@@ -1618,6 +1620,7 @@
 
     every(4, attend_back)
 
+    relays((7,), (5,))
     settle_sent(2)
     exchange(
         3, lambda side, n: last_dims(r.mixed[side], r.wq[pl.ds(n * 256, 256)]), r.middle,
@@ -1645,6 +1648,14 @@
 
     every(4, finish)
     to_owners(1, r.result, o_grad)
+
+    for b in range(4):
+        arrived(r.flags.at[b], r.flag_recv.at[b])
+    r.flags_full[...] = r.flags[...].astype(full)
+    ones = jnp.ones((8, width), jnp.bfloat16)
+    for b in range(4):
+        squares = row_sums(r.branch[rows_of(b)] * r.branch[rows_of(b)], ones)[:1]
+        r.sum_valid[...] += squares * r.flags_full[b, pl.ds(c, 1), :]
 
     for owner in range(4):
         r.terms[owner, pl.ds(c, 1), :] = r.sum_qk[owner : owner + 1]
@@ -1662,42 +1673,32 @@
     flow = Flow((r.v0, r.v1, r.v2, r.v3, r.v4, r.v5, r.v6, r.v7), r.vector)
     flow.begin(lambda to: r.terms.at[to])
 
-    every(3, lambda n: in_plane(6 + n, 0, READY, 0))
-    grad_of_lift(r.up, g_up)
-    for k in range(READY, READY + AHEAD):
-        begin(k)
-    for k in range(READY + 1):
-        if k < READY:
-            pair_load(k)
-        if k:
-            pair_send(k - 1)
+    @pl.when(late)
+    def _():
+        grad_of_lift(r.up, g_up)
+
+    in_plane(3)
 
     def step(t):
-        @pl.when(t == READY + 1)
+        @pl.when(t == 4)
         def _():
             grad_of_lift(r.gate, g_gate)
 
-        @pl.when(t == READY + 5)
+        @pl.when(t == 8)
         def _():
             grad_of_out()
             grad_of_qkv()
 
-        @pl.when(t + AHEAD < CHUNKS)
-        def _():
-            begin(t + AHEAD)
-
         between_planes(t)
-        in_plane(t, READY, CHUNKS, 1)
-        for at, work in (
-            (READY + 2, flow.pass_on), (READY + 4, flow.finish_plane), (READY + 10, flow.middle_planes),
-        ):
+        in_plane(t)
+        for at, work in ((6, flow.pass_on), (8, flow.finish_plane), (12, flow.middle_planes)):
             pl.when(t == at)(work)
 
-        @pl.when(t == READY + 14 + 14 * layer)
+        @pl.when(t == 16 + 18 * layer)
         def _():
             flow.all_planes(o_vectors.at[c])
 
-    every(CHUNKS + 18 - READY, lambda n: step(n + READY))
+    every(CHUNKS + 19 - 4, lambda n: step(n + 4))
 
     def settle(k):
         chunk = plane_sum.at[k]
@@ -1715,14 +1716,13 @@
             arrived(chunk, r.send_z.at[k])
             placed(k, 1)
 
+        @pl.when(k >= CHUNKS - 4)
+        def _():
+            placed(k, 0)
+
         @pl.when(early & (k >= CHUNKS - 4))
         def _():
             arrived(chunk, r.send_out.at[k])
-            placed(k, 0)
-
-        @pl.when(late)
-        def _():
-            placed(k, 0)
 
     every(CHUNKS, settle)
     flow.settle()

time: 616 us -> 582 us (0.945)
  Pallas kernels: 587 us -> 551 us
    pallas_call x1, Pallas kernels: 587 us -> 551 us  [relay_all(): pl.pallas_call(functools.partial(relay_kernel, tuple(scratch)), out_shape...]
where the time goes in v6:
time: 582 us; the launch traced here: 580 us
  Pallas kernels  551 us (95%)
  other arithmetic  19.9 us (3%)
  local copies, waits for them, and re-layouts  6.14 us (1%)
    pallas_call x1, Pallas kernels, relay_all(): pl.pallas_call(functools.partial(relay_kernel, tuple(scratch)), out_shape...  551 us

profile of v6, /device:TPU:0, one launch (start us, length us, event | category | flops | bytes accessed | tf_op | source)
XLA Modules:
  0.0 580.0 jit_solution(16499268767385375618)
XLA Ops:
  0.6 0.0 copy-start
  0.7 0.7 copy-done
  1.3 0.2 reduce-window.4
  1.5 0.7 reduce.1
  2.2 0.7 reduce.3
  2.9 0.7 convert.10
  3.6 0.7 reduce.2
  4.3 0.6 fusion.5.refs_4_
  4.9 0.6 fusion.10.refs_9_
  5.6 0.1 select_reduce_fusion
  5.7 0.0 copy-start.6
  5.7 0.6 copy.33
  6.3 1.0 copy.26.refs_8_
  7.3 0.0 copy-done.6
  7.3 551.5 %shard_map.186 = (bf16[1024,1024]{1,0:T(8,128)(2,1)}, bf16[256,8192]{1,0:T(8,128)(2,1)}, bf16[256,1024]{1,0:T(8,128)(2,1)}, bf16[256,3072]{1,0:T(8,128)(2,1)}, f...) custom-call(bf16[256,3072]{1,0:T(8,128)(2,1)} %bitcast.49, ...), custom_call_target="tpu_custom_call" | custom-call | tf_op jit(solution)/shard_map/pallas_call | solution.py:1780
  558.8 0.0 copy-start.4
  558.8 0.9 reduce_sum.18
  559.7 0.6 slice_reduce_fusion
  561.0 0.6 slice.25
  561.5 0.6 slice.27
  562.1 0.6 slice.26
  562.7 2.1 bitcast_convert_fusion.4
  564.9 2.9 bitcast_convert_fusion.3
  567.8 0.0 copy-done.4
  567.8 2.0 bitcast_convert_fusion.2
  569.8 0.0 copy-done.3
  569.8 2.6 bitcast_convert_fusion.1
  572.4 1.1 copy-done.2
  573.5 4.4 bitcast_convert_fusion
  577.9 0.0 copy-done.5
  577.9 1.0 copy.36
  578.9 0.0 copy-done.1
  (9 shorter events, 0.0 us)
Async XLA Ops:
  0.6 0.7 copy-start
  5.7 1.7 copy-start.6
  558.8 9.0 %copy-start.4 = (bf16[256,3072]{1,0:T(8,128)(2,1)S(1)}, bf16[256,3072]{1,0:T(8,128)(2,1)}, u32[]{:S(2)}) copy-start(bf16[256,3072]{1,0:T(8,128)(2,1)} %get-tuple-element.19) | copy-start | bytes 4718596
  564.9 5.0 copy-start.3
  569.8 3.7 copy-start.2
  573.5 4.4 copy-start.5
  573.5 5.4 copy-start.1

commit v7 on v6

--- a/solution.py
+++ b/solution.py
@@ -600,7 +600,7 @@
 CHUNKS = 16
 SHARED = (1, 2, 3, 4)
 AHEAD = 3
-INPUTS = 11
+INPUTS = 9
 OUTPUTS = 19
 
 
@@ -657,7 +657,7 @@
 def relay_kernel(names, *refs):
     (
         w_qkv, w_out, w_in, w_down, vectors, valid, tokens, cotangent,
-        start_col, place_row, start_row,
+        ends,
     ) = refs[:INPUTS]
     (
         o_down, o_in, o_out, o_qkv, o_vectors, o_hidden, o_grad, o_row,
@@ -870,9 +870,18 @@
                 arrived(block(item, f), r.first_send.at[item, 2])
 
     spread(0, 1, 2)
-    index = lax.broadcasted_iota(jnp.int32, (8 * BLOCK, 1), 0)
-    place_col = (index // 256) * 256 + (index // BLOCK + c) % 2 * BLOCK + index % BLOCK
-    fits = (place_row[...] >= start_col[...]) & (place_row[...] <= place_col)
+
+    def placed_at(axis):
+        index = lax.broadcasted_iota(jnp.int32, (1, 8 * BLOCK) if axis else (8 * BLOCK, 1), axis)
+        place = (index // 256) * 256 + (index // BLOCK + c) % 2 * BLOCK + index % BLOCK
+        start = jnp.zeros_like(place)
+        for n in range(ends.shape[0]):
+            start = jnp.maximum(start, jnp.where(place >= ends[n], ends[n], 0))
+        return place, start
+
+    place_col, start_col = placed_at(0)
+    place_row, start_row = placed_at(1)
+    fits = (place_row >= start_col) & (place_row <= place_col)
     r.bias[...] = jnp.where(fits, 0.0, MASKED)
     r.values[:, 2 * HEAD :] = jnp.ones_like(r.values[:, 2 * HEAD :])
     for sums in (r.sum_alphas, r.sum_scales, r.sum_valid, r.terms):
@@ -1466,7 +1475,7 @@
             ],
         )
 
-    fits = (place_col >= start_row[...]) & (place_col <= place_row[...])
+    fits = (place_col >= start_row) & (place_col <= place_row)
     r.bias[...] = jnp.where(fits, 0.0, MASKED)
     settle_relays()
     settle_spread()
@@ -1756,11 +1765,10 @@
                     )
 
 
-def relay_all(w_qkv, w_out, w_in, w_down, vectors, valid, tokens, cotangent, places):
+def relay_all(w_qkv, w_out, w_in, w_down, vectors, valid, tokens, cotangent, ends):
     width = w_out.shape[1]
     units = w_down.shape[0] * 4
     half = units // 2
-    place, start = places
 
     def low_shape(*shape):
         return jax.ShapeDtypeStruct(shape, jnp.bfloat16)
@@ -1768,7 +1776,7 @@
     chunks = low_shape(CHUNKS, 256, 512)
     rows = low_shape(2, 2 * BLOCK, width)
     anywhere = pl.BlockSpec(memory_space=pl.ANY)
-    near = pl.BlockSpec(memory_space=pltpu.VMEM)
+    scalars = pl.BlockSpec(memory_space=pltpu.SMEM)
     scratch = scratch_of(width, units, vectors.shape[0], valid.shape[1])
     out_shape = [
         low_shape(half // 2, width), low_shape(width // 4, 2 * units), low_shape(width // 4, width),
@@ -1780,15 +1788,14 @@
     return pl.pallas_call(
         functools.partial(relay_kernel, tuple(scratch)),
         out_shape=out_shape,
-        in_specs=[anywhere] * 8 + [near] * 3,
+        in_specs=[anywhere] * 8 + [scalars],
         out_specs=[anywhere] * len(out_shape),
         scratch_shapes=list(scratch.values()),
         compiler_params=pltpu.CompilerParams(
             collective_id=0, has_side_effects=True, vmem_limit_bytes=62 * 2**20
         ),
     )(
-        w_qkv, w_out, w_in, w_down, vectors, valid, tokens, cotangent,
-        start[:, None], place[None, :], start[None, :],
+        w_qkv, w_out, w_in, w_down, vectors, valid, tokens, cotangent, ends,
     )[:7]
 
 
@@ -1805,14 +1812,9 @@
     vectors = jnp.concatenate([qk_scale[0], mlp_scale[0], alphas[0]])
     vectors = jnp.pad(vectors, (0, 32 * 128 - vectors.shape[0])).reshape(32, 128)
     valid = low(jnp.pad(valid_mask[:, 0], ((0, 0), (0, 16 * 128 - group)))).reshape(2, 16, 128)
-    index = jnp.arange(4 * group, dtype=jnp.int32)
-    place = (index // 256) * 256 + (((index // BLOCK) + c) % 2) * BLOCK + index % BLOCK
     ends = jnp.cumsum(pick(lengths, micro, 0)[0])[:-1]
-    passed = place[:, None] >= ends[None, :]
-    start = jnp.max(jnp.where(passed, ends[None, :], 0), axis=1)
-    places = (place, start)
     grad_down, grad_in_proj, grad_out, grad_qkv, vectors, hidden_out, grad_in = relay_all(
-        w_qkv[0], w_out[0], w_in[0], w_down[0], vectors, valid, tokens[:, 0], cotangent[:, 0], places
+        w_qkv[0], w_out[0], w_in[0], w_down[0], vectors, valid, tokens[:, 0], cotangent[:, 0], ends
     )
     cut_qk, cut_mlp = qk_scale.shape[1], qk_scale.shape[1] + mlp_scale.shape[1]
     full = jnp.sum(vectors, axis=0).reshape(-1)

time: 582 us -> 580 us (level)
  no operation moved by 1% of the time
where the time goes in v7:
time: 580 us; the launch traced here: 578 us
  Pallas kernels  551 us (95%)
  other arithmetic  19.1 us (3%)
    pallas_call x1, Pallas kernels, relay_all(): pl.pallas_call(functools.partial(relay_kernel, tuple(scratch)), out_shape...  551 us

profile of v7, /device:TPU:0, one launch (start us, length us, event | category | flops | bytes accessed | tf_op | source)
XLA Modules:
  0.0 578.3 jit_solution(1744398221782780607)
XLA Ops:
  0.6 0.0 copy-start
  0.7 0.7 copy-done
  1.3 0.2 reduce-window.4
  1.5 0.5 slice_bitcast_fusion.refs_8_
  2.0 0.7 reduce.1
  2.7 0.7 reduce.3
  3.4 0.7 convert.10
  4.1 0.7 reduce.2
  4.8 0.6 fusion.5.refs_4_
  5.5 0.6 copy.27
  6.1 551.0 %shard_map.186 = (bf16[1024,1024]{1,0:T(8,128)(2,1)}, bf16[256,8192]{1,0:T(8,128)(2,1)}, bf16[256,1024]{1,0:T(8,128)(2,1)}, bf16[256,3072]{1,0:T(8,128)(2,1)}, f...) custom-call(bf16[256,3072]{1,0:T(8,128)(2,1)} %bitcast.47, ...), custom_call_target="tpu_custom_call" | custom-call | tf_op jit(solution)/shard_map/pallas_call | solution.py:1788
  557.1 0.0 copy-start.4
  557.1 0.9 reduce_sum.18
  558.0 0.6 slice_reduce_fusion
  559.3 0.6 slice.28
  559.8 0.6 slice.30
  560.4 0.6 slice.29
  561.0 2.1 bitcast_convert_fusion.4
  563.1 0.0 copy-start.3
  563.1 2.9 bitcast_convert_fusion.3
  566.1 0.0 copy-done.4
  566.1 2.0 bitcast_convert_fusion.2
  568.1 0.0 copy-done.3
  568.1 0.0 copy-start.2
  568.1 2.6 bitcast_convert_fusion.1
  570.7 1.1 copy-done.2
  571.8 0.0 copy-start.5
  571.8 0.0 copy-start.1
  571.8 4.4 bitcast_convert_fusion
  576.2 0.0 copy-done.5
  576.2 1.0 copy.30
  577.2 0.0 copy-done.1
  (3 shorter events, 0.0 us)
Async XLA Ops:
  0.6 0.7 copy-start
  557.1 9.0 %copy-start.4 = (bf16[256,3072]{1,0:T(8,128)(2,1)S(1)}, bf16[256,3072]{1,0:T(8,128)(2,1)}, u32[]{:S(2)}) copy-start(bf16[256,3072]{1,0:T(8,128)(2,1)} %get-tuple-element.19) | copy-start | bytes 4718596
  563.1 5.0 copy-start.3
  568.1 3.7 copy-start.2
  571.8 4.4 copy-start.5
  571.8 5.4 copy-start.1
